TPU v7x, 32 devices: a whole 2x2x4 slice. The times are simulated.
32 devices in a mesh: members: 2 (over y), belt: 4 (over z), across: 2 (over x), lev: 2 (over core).
Axes of the slice: x: 2, y: 2, z: 4, core: 2. Of those that a mesh axis runs over, the one named last changes fastest.
Arguments:
- wind: bfloat16 [2, 24, 64, 4096], P(None, ('members', 'lev'), 'across', 'belt'), parts along dimension 1, may hold values from -6 to 6
- metric: float32 [64, 4096], P('across', 'belt'), may hold values from 0.5 to 2
- kappa: float32 [2, 64, 4096], P(None, 'across', 'belt'), may hold values from 0.03 to 0.24
- edge_peer: int32 [2, 4], replicated, may hold values from 0 to 3, each once within a row
- edge_flip: int32 [2, 4], replicated, may hold values from 0 to 1
- edge_turn: int32 [2, 4], replicated, may hold values from 0 to 3
Outputs:
- controls: float32 [2, 24, 64, 4096], P(None, ('members', 'lev'), 'across', 'belt'), parts along dimension 1
There are 2 independent parts, one for each index of `members`. A program takes and returns all parts, laid end to end along the dimension named above; an argument that names none is the same for every part. Nothing has to cross between parts.
Inputs may be any that keep to these rules, and one draw needn't show every extreme that they name: `edge_peer`: each row names every column block once.
All inputs are finite; a program needn't handle non-finite values.
Results may differ from a plain program's by a relative error of at most 0.0003.
Values may be sent and summed in bfloat16 or wider, within the bound.
No kernel may reach another device: no remote copies, remote signals or barrier semaphores. Data moves between devices by JAX's collectives and lax.ppermute only.
A program may use at most 64 MiB of HBM per device.

v0:
```python
import jax
import jax.numpy as jnp
from jax import lax
from jax.sharding import PartitionSpec as P

STEPS = 6


def padded_2(array, sides, width):
    for axis, dim in sides:
        size, length = (lax.axis_size(axis), array.shape[dim])
        up = [(i, (i + 1) % size) for i in range(size)]
        down = [(j, i) for i, j in up]
        last = lax.slice_in_dim(array, length - width, length, axis=dim)
        leading = lax.slice_in_dim(array, 0, width, axis=dim)
        before = lax.ppermute(last, axis, up)
        after = lax.ppermute(leading, axis, down)
        array = jnp.concatenate([before, array, after], axis=dim)
    return array


def turn_factors(turns):
    cosine = jnp.where(turns == 0, 1.0, jnp.where(turns == 2, -1.0, 0.0)).astype(jnp.float32)
    sine_neg = jnp.where(turns == 1, -1.0, jnp.where(turns == 3, 1.0, 0.0)).astype(jnp.float32)
    return (cosine, sine_neg)


def coefficients(depth, padded_kappa, rows, across_at, across_count):
    global_row = across_at * rows + jnp.arange(rows + 2 * depth - 1, dtype=jnp.int32) - depth
    valid = ((global_row >= 0) & (global_row < across_count * rows - 1)).astype(jnp.float32)
    belt_coef = 0.5 * (padded_kappa[:, :, :-1] + padded_kappa[:, :, 1:])
    across_coef = 0.5 * (padded_kappa[:, :-1] + padded_kappa[:, 1:]) * valid[None, :, None]
    return (belt_coef, across_coef)


def advance(field_pad, belt_coef, across_coef, offset):
    height = field_pad.shape[2]
    width = field_pad.shape[3]
    belt_part = belt_coef[:, offset : offset + height, offset : offset + width - 1]
    across_part = across_coef[:, offset : offset + height - 1, offset : offset + width]
    belt_flux = belt_part[:, None] * (field_pad[:, :, :, 1:] - field_pad[:, :, :, :-1])
    across_flux = across_part[:, None] * (field_pad[:, :, 1:, :] - field_pad[:, :, :-1, :])
    return (
        field_pad[:, :, 1:-1, 1:-1]
        + belt_flux[:, :, 1:-1, 1:]
        - belt_flux[:, :, 1:-1, :-1]
        + across_flux[:, :, 1:, 1:-1]
        - across_flux[:, :, :-1, 1:-1]
    )


def per_device(wind, metric, kappa, edge_peer, edge_flip, edge_turn):
    rows = wind.shape[2]
    cols = wind.shape[3]
    across_count = lax.axis_size("across")
    across_at = lax.axis_index("across")
    belt_at = lax.axis_index("belt")
    padded = padded_2(wind, (("belt", 3), ("across", 2)), 1).astype(jnp.float32)
    rims = jnp.stack([wind[:, :, 0, :], wind[:, :, rows - 1, :]])
    gathered = lax.all_gather(rims, "belt", axis=3, tiled=True)
    ghosts = []
    for which_edge in range(2):
        facing = edge_peer[which_edge, belt_at]
        piece = lax.dynamic_slice_in_dim(gathered[which_edge], facing * cols, cols, 2).astype(
            jnp.float32
        )
        piece = jnp.where(edge_flip[which_edge, belt_at] == 1, piece[:, :, ::-1], piece)
        cosine, sine_neg = turn_factors(edge_turn[which_edge, belt_at])
        ghosts.append(
            jnp.stack(
                [cosine * piece[0] + sine_neg * piece[1], cosine * piece[1] - sine_neg * piece[0]]
            )
        )
    top_row = jnp.where(across_at == 0, ghosts[0], padded[:, :, 0, 1:-1])
    bottom_row = jnp.where(across_at == across_count - 1, ghosts[1], padded[:, :, -1, 1:-1])
    padded = padded.at[:, :, 0, 1:-1].set(top_row).at[:, :, -1, 1:-1].set(bottom_row)
    across_diff = 0.5 * (padded[:, :, 2:, 1:-1] - padded[:, :, :-2, 1:-1])
    belt_diff = 0.5 * (padded[:, :, 1:-1, 2:] - padded[:, :, 1:-1, :-2])
    curl_part = metric * (across_diff[0] - belt_diff[1])
    divergent = metric * (-belt_diff[0] - across_diff[1])
    fields = jnp.stack([curl_part, divergent])
    kappa_pad = padded_2(kappa, (("belt", 2), ("across", 1)), 3)
    belt_coef, across_coef = coefficients(3, kappa_pad, rows, across_at, across_count)
    for repeat in range(STEPS // 3):
        field_pad = padded_2(fields, (("belt", 3), ("across", 2)), 3)
        for inner in range(3):
            field_pad = advance(field_pad, belt_coef, across_coef, inner)
        fields = field_pad
    return fields


def solution(mesh):
    return jax.shard_map(
        per_device,
        mesh=mesh,
        in_specs=(
            P(None, ("members", "lev"), "across", "belt"),
            P("across", "belt"),
            P(None, "across", "belt"),
            P(),
            P(),
            P(),
        ),
        out_specs=P(None, ("members", "lev"), "across", "belt"),
        check_vma=False,
    )
```

profile of v0, /device:TPU:0, one launch (start us, length us, event | category | flops | bytes accessed | tf_op | source)
XLA Modules:
  0.0 122.3 jit_solution(2449018391207157927)
XLA Ops:
  0.0 1.6 %copy.11 = bf16[2,6,32,1024]{3,1,2,0:T(8,128)(2,1)S(1)} copy(bf16[2,6,32,1024]{3,2,1,0:T(8,128)(2,1)} %param.10) | data formatting | bytes 1572864 | tf_op args[0]
  1.7 3.1 %collective-permute-start = (bf16[2,6,32,1]{3,1,2,0:T(8,128)(2,1)S(1)}, bf16[2,6,32,1]{3,1,2,0:T(8,128)(2,1)S(1)}, u32[]{:S(2)}, u32[]{:S(2)}) collective-permute-start(bf16[2,6,32,1]{3,1,2,0:T(8,128)(2,1)S(1)} %get-tuple-element.46), channel_id=1, source_target_pairs={{0,4},{4,8},{8,12},{12,0},{1,5},{5,9},{9,13},{13,1},{2,6},{6,10},{... | collective-permute-start | bytes 2312 | tf_op jit(solution)/shard_map/ppermute | solution.py:16
  4.8 2.1 %collective-permute-start.1 = (bf16[2,6,32,1]{3,1,2,0:T(8,128)(2,1)S(1)}, bf16[2,6,32,1]{3,1,2,0:T(8,128)(2,1)S(1)}, u32[]{:S(2)}, u32[]{:S(2)}) collective-permute-start(bf16[2,6,32,1]{3,1,2,0:T(8,128)(2,1)S(1)} %get-tuple-element.45), channel_id=1, source_target_pairs={{4,0},{8,4},{12,8},{0,12},{5,1},{9,5},{13,9},{1,13},{6,2},{10,6},{... | collective-permute-start | bytes 2312 | tf_op jit(solution)/shard_map/ppermute | solution.py:17
  6.9 0.8 fusion.27
  7.8 3.8 %collective-permute-start.9 = (f32[2,32,3]{2,1,0:T(8,128)S(1)}, f32[2,32,3]{2,1,0:T(8,128)S(1)}, u32[]{:S(2)}, u32[]{:S(2)}) collective-permute-start(f32[2,32,3]{2,1,0:T(8,128)S(1)} %get-tuple-element.51), channel_id=1, source_target_pairs={{4,0},{8,4},{12,8},{0,12},{5,1},{9,5},{13,9},{1,13},{6,2},{10,6},{... | collective-permute-start | bytes 2312 | tf_op jit(solution)/shard_map/ppermute | solution.py:17
  11.6 1.1 fusion.25
  12.7 0.6 constant_dynamic-slice_fusion.3
  14.6 0.6 constant_dynamic-slice_fusion.5
  20.4 13.9 %all_gather.3 = bf16[2,2,6,4096]{3,2,1,0:T(8,128)(2,1)S(1)} all-gather(bf16[2,2,6,1024]{3,2,1,0:T(8,128)(2,1)S(1)} %pad_maximum_fusion.4), channel_id=1, replica_groups=mesh['members'=2,'belt'=4,'across'=2,'lev'=2] {'belt'}, dimensions={3}, use_global_device_ids=true | all-gather | bytes 245760 | tf_op jit(solution)/shard_map/all_gather | solution.py:60
  34.3 0.6 rev.7
  37.5 1.9 %concatenate.32 = bf16[2,6,32,1026]{3,1,2,0:T(8,128)(2,1)S(1)} concatenate(bf16[2,6,32,1]{3,1,2,0:T(8,128)(2,1)S(1)} %collective-permute-done, bf16[2,6,32,1024]{3,1,2,0:T(8,128)(2,1)S(1)} %copy.11, bf16[2,6,32,1]{3,1,2,0:T(8,128)(2,1)S(1)} %collective-permute-done.1), dimensions={3} | concatenate | bytes 1575936 | tf_op jit(solution)/shard_map/concatenate | solution.py:18
  39.4 1.6 %collective-permute-start.2 = (bf16[2,6,1,1026]{3,1,2,0:T(8,128)(2,1)S(1)}, bf16[2,6,1,1026]{3,1,2,0:T(8,128)(2,1)S(1)}, u32[]{:S(2)}, u32[]{:S(2)}) collective-permute-start(bf16[2,6,1,1026]{3,1,2,0:T(8,128)(2,1)S(1)} %get-tuple-element.43), channel_id=1, source_target_pairs={{0,2},{2,0},{1,3},{3,1},{4,6},{6,4},{5,7},{7,5},{8,10},{10,8},{9,1... | collective-permute-start | bytes 73880 | tf_op jit(solution)/shard_map/ppermute | solution.py:16
  41.8 1.6 %collective-permute-start.10 = (f32[2,3,1030]{2,1,0:T(4,128)S(1)}, f32[2,3,1030]{2,1,0:T(4,128)S(1)}, u32[]{:S(2)}, u32[]{:S(2)}) collective-permute-start(f32[2,3,1030]{2,1,0:T(4,128)S(1)} %get-tuple-element.49), channel_id=1, source_target_pairs={{0,2},{2,0},{1,3},{3,1},{4,6},{6,4},{5,7},{7,5},{8,10},{10,8},{9,1... | collective-permute-start | bytes 74168 | tf_op jit(solution)/shard_map/ppermute | solution.py:16
  43.9 1.2 collective-permute-done.3
  45.0 1.6 %maximum_convert_fusion = f32[2,6,34,1026]{3,1,2,0:T(8,128)S(1)} fusion(bf16[2,6,1,1026]{3,1,2,0:T(8,128)(2,1)S(1)} %collective-permute-done.3, bf16[2,6,32,1026]{3,1,2,0:T(8,128)(2,1)} %copy-done.1, bf16[2,6,1,1026]{3,1,2,0:T(8,128)(2,1)S(1)} %collective-permute-done.2), kind=kLoop, calls=%fused_computation.59 | loop fusion | flops 1255824 | bytes 2511648 | tf_op jit(solution)/shard_map/convert_element_type | solution.py:58
  46.8 1.9 %scatter.6 = f32[2,6,34,1026]{3,1,2,0:T(8,128)S(1)} dynamic-update-slice(f32[2,6,34,1026]{3,1,2,0:T(8,128)S(1)} %maximum_convert_fusion, f32[2,6,1,1024]{3,1,2,0:T(8,128)S(1)} %get-tuple-element.34, s32[]{:T(128)} %constant.110.clone.1, s32[]{:T(128)} %constant.110.clone.1, s32[]{:T(128)} %bitcast.9, s32[]{:T(128)} %bitcast.10) | dynamic-update-slice | bytes 98308 | tf_op jit(solution)/shard_map/scatter | solution.py:76
  48.7 0.7 scatter.9
  49.4 1.7 %fusion.13 = (f32[2,6,32,1024]{3,1,2,0:T(8,128)S(1)}, f32[2,6,32,1024]{3,1,2,0:T(8,128)S(1)}) fusion(f32[2,6,34,1026]{3,1,2,0:T(8,128)S(1)} %scatter.9), kind=kLoop, calls=%fused_computation.58 | loop fusion | flops 1572864 | bytes 9437184 | tf_op jit(solution)/shard_map/mul | solution.py:77
  51.6 1.6 %pad_maximum_fusion = f32[2,6,32,1024]{3,1,2,0:T(8,128)} fusion(f32[1,6,32,1024]{3,1,2,0:T(8,128)S(1)} %get-tuple-element.29, f32[1,6,32,1024]{3,1,2,0:T(8,128)S(1)} %get-tuple-element.30), kind=kLoop, calls=%fused_computation.2 | loop fusion | flops 393216 | bytes 3145728 | tf_op jit(solution)/shard_map/stack | solution.py:81
  53.3 3.8 %collective-permute-start.5 = (f32[2,6,32,3]{3,1,2,0:T(8,128)S(1)}, f32[2,6,32,3]{3,1,2,0:T(8,128)}, u32[]{:S(2)}, u32[]{:S(2)}) collective-permute-start(f32[2,6,32,3]{3,1,2,0:T(8,128)S(1)} %get-tuple-element.41), channel_id=1, source_target_pairs={{4,0},{8,4},{12,8},{0,12},{5,1},{9,5},{13,9},{1,13},{6,2},{10,6},{... | collective-permute-start | bytes 13832 | tf_op jit(solution)/shard_map/ppermute | solution.py:17
  57.3 4.3 %collective-permute-done.4 = f32[2,6,32,3]{3,1,2,0:T(8,128)S(1)} collective-permute-done((f32[2,6,32,3]{3,1,2,0:T(8,128)S(1)}, f32[2,6,32,3]{3,1,2,0:T(8,128)S(1)}, u32[]{:S(2)}, u32[]{:S(2)}) %collective-permute-start.4) | collective-permute-done | bytes 4640 | tf_op jit(solution)/shard_map/ppermute | solution.py:16
  61.7 1.0 collective-permute-done.5
  62.7 3.3 %concatenate.34 = f32[2,6,32,1030]{3,1,2,0:T(8,128)S(1)} concatenate(f32[2,6,32,3]{3,1,2,0:T(8,128)S(1)} %collective-permute-done.4, f32[2,6,32,1024]{3,1,2,0:T(8,128)} %pad_maximum_fusion, f32[2,6,32,3]{3,1,2,0:T(8,128)} %collective-permute-done.5), dimensions={3} | concatenate | bytes 3164160 | tf_op jit(solution)/shard_map/concatenate | solution.py:18
  66.5 1.6 %collective-permute-start.7 = (f32[2,6,3,1030]{3,1,2,0:T(8,128)S(1)}, f32[2,6,3,1030]{3,1,2,0:T(8,128)S(1)}, u32[]{:S(2)}, u32[]{:S(2)}) collective-permute-start(f32[2,6,3,1030]{3,1,2,0:T(8,128)S(1)} %get-tuple-element.38), channel_id=1, source_target_pairs={{2,0},{0,2},{3,1},{1,3},{6,4},{4,6},{7,5},{5,7},{10,8},{8,10},{11,... | collective-permute-start | bytes 444968 | tf_op jit(solution)/shard_map/ppermute | solution.py:17
  68.9 3.1 %collective-permute-done.6 = f32[2,6,3,1030]{3,1,2,0:T(8,128)S(1)} collective-permute-done((f32[2,6,3,1030]{3,1,2,0:T(8,128)S(1)}, f32[2,6,3,1030]{3,1,2,0:T(8,128)S(1)}, u32[]{:S(2)}, u32[]{:S(2)}) %collective-permute-start.6) | collective-permute-done | bytes 148352 | tf_op jit(solution)/shard_map/ppermute | solution.py:16
  72.0 2.4 %collective-permute-done.7 = f32[2,6,3,1030]{3,1,2,0:T(8,128)S(1)} collective-permute-done((f32[2,6,3,1030]{3,1,2,0:T(8,128)S(1)}, f32[2,6,3,1030]{3,1,2,0:T(8,128)S(1)}, u32[]{:S(2)}, u32[]{:S(2)}) %collective-permute-start.7) | collective-permute-done | bytes 148352 | tf_op jit(solution)/shard_map/ppermute | solution.py:17
  74.6 0.9 fusion.1
  75.9 2.8 %slice_subtract_fusion.8 = f32[2,6,36,1028]{3,1,2,0:T(8,128)S(1)} fusion(f32[2,6,37,1030]{3,1,2,0:T(8,128)S(1)} %fusion.3, f32[2,6,38,1029]{3,1,2,0:T(8,128)S(1)} %fusion.1, f32[2,6,38,1030]{3,1,2,0:T(8,128)S(1)} %pad_maximum_fusion.1), kind=kLoop, calls=%fused_computation.23 | loop fusion | flops 1776384 | bytes 10658304 | tf_op jit(solution)/shard_map/sub | solution.py:44
  78.7 0.9 fusion.5
  80.0 2.6 %slice_subtract_fusion.16 = f32[2,6,34,1026]{3,1,2,0:T(8,128)S(1)} fusion(f32[2,6,35,1028]{3,1,2,0:T(8,128)S(1)} %fusion.7, f32[2,6,36,1027]{3,1,2,0:T(8,128)S(1)} %fusion.5, f32[2,6,36,1028]{3,1,2,0:T(8,128)S(1)} %slice_subtract_fusion.8), kind=kLoop, calls=%fused_computation.39 | loop fusion | flops 1674432 | bytes 10046592 | tf_op jit(solution)/shard_map/sub | solution.py:44
  82.7 0.8 fusion.9
  83.8 2.2 %slice_subtract_fusion.22 = f32[2,6,32,1024]{3,1,2,0:T(8,128)S(1)} fusion(f32[2,6,33,1026]{3,1,2,0:T(8,128)S(1)} %fusion.11, f32[2,6,34,1025]{3,1,2,0:T(8,128)S(1)} %fusion.9, f32[2,6,34,1026]{3,1,2,0:T(8,128)S(1)} %slice_subtract_fusion.16), kind=kLoop, calls=%fused_computation.51 | loop fusion | flops 1572864 | bytes 9437184 | tf_op jit(solution)/shard_map/sub | solution.py:44
  86.2 1.2 collective-permute-start.12
  87.4 2.7 %collective-permute-start.13 = (f32[2,6,32,3]{3,1,2,0:T(8,128)S(1)}, f32[2,6,32,3]{3,1,2,0:T(8,128)}, u32[]{:S(2)}, u32[]{:S(2)}) collective-permute-start(f32[2,6,32,3]{3,1,2,0:T(8,128)S(1)} %get-tuple-element.39), channel_id=1, source_target_pairs={{4,0},{8,4},{12,8},{0,12},{5,1},{9,5},{13,9},{1,13},{6,2},{10,6},{... | collective-permute-start | bytes 13832 | tf_op jit(solution)/shard_map/ppermute | solution.py:17
  90.1 4.5 %collective-permute-done.12 = f32[2,6,32,3]{3,1,2,0:T(8,128)S(1)} collective-permute-done((f32[2,6,32,3]{3,1,2,0:T(8,128)S(1)}, f32[2,6,32,3]{3,1,2,0:T(8,128)S(1)}, u32[]{:S(2)}, u32[]{:S(2)}) %collective-permute-start.12) | collective-permute-done | bytes 4640 | tf_op jit(solution)/shard_map/ppermute | solution.py:16
  94.6 0.7 copy-done.9
  95.3 1.4 %collective-permute-done.13 = f32[2,6,32,3]{3,1,2,0:T(8,128)} collective-permute-done((f32[2,6,32,3]{3,1,2,0:T(8,128)S(1)}, f32[2,6,32,3]{3,1,2,0:T(8,128)}, u32[]{:S(2)}, u32[]{:S(2)}) %collective-permute-start.13) | collective-permute-done | bytes 4640 | tf_op jit(solution)/shard_map/ppermute | solution.py:17
  96.7 3.3 %concatenate.38 = f32[2,6,32,1030]{3,1,2,0:T(8,128)S(1)} concatenate(f32[2,6,32,3]{3,1,2,0:T(8,128)} %copy-done.9, f32[2,6,32,1024]{3,1,2,0:T(8,128)} %copy-done, f32[2,6,32,3]{3,1,2,0:T(8,128)} %collective-permute-done.13), dimensions={3} | concatenate | bytes 3164160 | tf_op jit(solution)/shard_map/concatenate | solution.py:18
  100.5 1.6 %collective-permute-start.15 = (f32[2,6,3,1030]{3,1,2,0:T(8,128)S(1)}, f32[2,6,3,1030]{3,1,2,0:T(8,128)S(1)}, u32[]{:S(2)}, u32[]{:S(2)}) collective-permute-start(f32[2,6,3,1030]{3,1,2,0:T(8,128)S(1)} %get-tuple-element.36), channel_id=1, source_target_pairs={{2,0},{0,2},{3,1},{1,3},{6,4},{4,6},{7,5},{5,7},{10,8},{8,10},{11,... | collective-permute-start | bytes 444968 | tf_op jit(solution)/shard_map/ppermute | solution.py:17
  102.1 3.9 %collective-permute-done.14 = f32[2,6,3,1030]{3,1,2,0:T(8,128)S(1)} collective-permute-done((f32[2,6,3,1030]{3,1,2,0:T(8,128)S(1)}, f32[2,6,3,1030]{3,1,2,0:T(8,128)S(1)}, u32[]{:S(2)}, u32[]{:S(2)}) %collective-permute-start.14) | collective-permute-done | bytes 148352 | tf_op jit(solution)/shard_map/ppermute | solution.py:16
  106.0 2.4 %collective-permute-done.15 = f32[2,6,3,1030]{3,1,2,0:T(8,128)S(1)} collective-permute-done((f32[2,6,3,1030]{3,1,2,0:T(8,128)S(1)}, f32[2,6,3,1030]{3,1,2,0:T(8,128)S(1)}, u32[]{:S(2)}, u32[]{:S(2)}) %collective-permute-start.15) | collective-permute-done | bytes 148352 | tf_op jit(solution)/shard_map/ppermute | solution.py:17
  108.6 0.9 fusion
  109.9 2.8 %slice_subtract_fusion.5 = f32[2,6,36,1028]{3,1,2,0:T(8,128)S(1)} fusion(f32[2,6,37,1030]{3,1,2,0:T(8,128)S(1)} %fusion.2, f32[2,6,38,1029]{3,1,2,0:T(8,128)S(1)} %fusion, f32[2,6,38,1030]{3,1,2,0:T(8,128)S(1)} %pad_maximum_fusion.2), kind=kLoop, calls=%fused_computation.17 | loop fusion | flops 1776384 | bytes 10658304 | tf_op jit(solution)/shard_map/sub | solution.py:44
  112.8 0.9 fusion.4
  114.1 2.7 %slice_subtract_fusion.13 = f32[2,6,34,1026]{3,1,2,0:T(8,128)S(1)} fusion(f32[2,6,35,1028]{3,1,2,0:T(8,128)S(1)} %fusion.6, f32[2,6,36,1027]{3,1,2,0:T(8,128)S(1)} %fusion.4, f32[2,6,36,1028]{3,1,2,0:T(8,128)S(1)} %slice_subtract_fusion.5), kind=kLoop, calls=%fused_computation.33 | loop fusion | flops 1674432 | bytes 10046592 | tf_op jit(solution)/shard_map/sub | solution.py:44
  116.8 0.7 fusion.8
  118.0 2.2 %slice_subtract_fusion.20 = f32[2,6,32,1024]{3,1,2,0:T(8,128)S(1)} fusion(f32[2,6,33,1026]{3,1,2,0:T(8,128)S(1)} %fusion.10, f32[2,6,34,1025]{3,1,2,0:T(8,128)S(1)} %fusion.8, f32[2,6,34,1026]{3,1,2,0:T(8,128)S(1)} %slice_subtract_fusion.13), kind=kLoop, calls=%fused_computation.47 | loop fusion | flops 1572864 | bytes 9437184 | tf_op jit(solution)/shard_map/sub | solution.py:44
  120.3 2.1 %copy.16 = f32[2,6,32,1024]{3,2,1,0:T(8,128)} copy(f32[2,6,32,1024]{3,1,2,0:T(8,128)S(1)} %slice_subtract_fusion.20) | data formatting | bytes 3145728 | tf_op jit(solution)/shard_map/sub | solution.py:44
  (78 shorter events, 8.5 us)
Async XLA Ops:
  0.0 12.7 %copy-start.12 = (s32[2,4]{1,0:T(2,128)S(1)}, s32[2,4]{1,0:T(2,128)}, u32[]{:S(2)}) copy-start(s32[2,4]{1,0:T(2,128)} %param.13) | copy-start | bytes 100
  0.0 12.7 %copy-start.13 = (s32[2,4]{1,0:T(2,128)S(1)}, s32[2,4]{1,0:T(2,128)}, u32[]{:S(2)}) copy-start(s32[2,4]{1,0:T(2,128)} %param.14) | copy-start | bytes 100
  0.0 14.6 %copy-start.11 = (s32[2,4]{1,0:T(2,128)S(1)}, s32[2,4]{1,0:T(2,128)}, u32[]{:S(2)}) copy-start(s32[2,4]{1,0:T(2,128)} %param.15) | copy-start | bytes 100
  1.7 35.7 %collective-permute-start = (bf16[2,6,32,1]{3,1,2,0:T(8,128)(2,1)S(1)}, bf16[2,6,32,1]{3,1,2,0:T(8,128)(2,1)S(1)}, u32[]{:S(2)}, u32[]{:S(2)}) collective-permute-start(bf16[2,6,32,1]{3,1,2,0:T(8,128)(2,1)S(1)} %get-tuple-element.46), channel_id=1, source_target_pairs={{0,4},{4,8},{8,12},{12,0},{1,5},{5,9},{9,13},{13,1},{2,6},{6,10},{... | collective-permute-start | bytes 2312 | tf_op jit(solution)/shard_map/ppermute | solution.py:16
  4.8 32.7 %collective-permute-start.1 = (bf16[2,6,32,1]{3,1,2,0:T(8,128)(2,1)S(1)}, bf16[2,6,32,1]{3,1,2,0:T(8,128)(2,1)S(1)}, u32[]{:S(2)}, u32[]{:S(2)}) collective-permute-start(bf16[2,6,32,1]{3,1,2,0:T(8,128)(2,1)S(1)} %get-tuple-element.45), channel_id=1, source_target_pairs={{4,0},{8,4},{12,8},{0,12},{5,1},{9,5},{13,9},{1,13},{6,2},{10,6},{... | collective-permute-start | bytes 2312 | tf_op jit(solution)/shard_map/ppermute | solution.py:17
  7.8 33.8 %collective-permute-start.8 = (f32[2,32,3]{2,1,0:T(8,128)S(1)}, f32[2,32,3]{2,1,0:T(8,128)S(1)}, u32[]{:S(2)}, u32[]{:S(2)}) collective-permute-start(f32[2,32,3]{2,1,0:T(8,128)S(1)} %get-tuple-element.52), channel_id=1, source_target_pairs={{0,4},{4,8},{8,12},{12,0},{1,5},{5,9},{9,13},{13,1},{2,6},{6,10},{... | collective-permute-start | bytes 2312 | tf_op jit(solution)/shard_map/ppermute | solution.py:16
  7.8 33.8 %collective-permute-start.9 = (f32[2,32,3]{2,1,0:T(8,128)S(1)}, f32[2,32,3]{2,1,0:T(8,128)S(1)}, u32[]{:S(2)}, u32[]{:S(2)}) collective-permute-start(f32[2,32,3]{2,1,0:T(8,128)S(1)} %get-tuple-element.51), channel_id=1, source_target_pairs={{4,0},{8,4},{12,8},{0,12},{5,1},{9,5},{13,9},{1,13},{6,2},{10,6},{... | collective-permute-start | bytes 2312 | tf_op jit(solution)/shard_map/ppermute | solution.py:17
  12.7 28.9 %copy-start.8 = (f32[2,32,1024]{2,1,0:T(8,128)S(1)}, f32[2,32,1024]{2,1,0:T(8,128)}, u32[]{:S(2)}) copy-start(f32[2,32,1024]{2,1,0:T(8,128)} %param.12) | copy-start | bytes 786436
  39.4 4.4 %copy-start.1 = (bf16[2,6,32,1026]{3,1,2,0:T(8,128)(2,1)}, bf16[2,6,32,1026]{3,1,2,0:T(8,128)(2,1)S(1)}, u32[]{:S(2)}) copy-start(bf16[2,6,32,1026]{3,1,2,0:T(8,128)(2,1)S(1)} %concatenate.32) | copy-start | bytes 2363908
  39.4 4.4 %collective-permute-start.2 = (bf16[2,6,1,1026]{3,1,2,0:T(8,128)(2,1)S(1)}, bf16[2,6,1,1026]{3,1,2,0:T(8,128)(2,1)S(1)}, u32[]{:S(2)}, u32[]{:S(2)}) collective-permute-start(bf16[2,6,1,1026]{3,1,2,0:T(8,128)(2,1)S(1)} %get-tuple-element.43), channel_id=1, source_target_pairs={{0,2},{2,0},{1,3},{3,1},{4,6},{6,4},{5,7},{7,5},{8,10},{10,8},{9,1... | collective-permute-start | bytes 73880 | tf_op jit(solution)/shard_map/ppermute | solution.py:16
  41.1 4.0 %collective-permute-start.3 = (bf16[2,6,1,1026]{3,1,2,0:T(8,128)(2,1)S(1)}, bf16[2,6,1,1026]{3,1,2,0:T(8,128)(2,1)S(1)}, u32[]{:S(2)}, u32[]{:S(2)}) collective-permute-start(bf16[2,6,1,1026]{3,1,2,0:T(8,128)(2,1)S(1)} %get-tuple-element.44), channel_id=1, source_target_pairs={{2,0},{0,2},{3,1},{1,3},{6,4},{4,6},{7,5},{5,7},{10,8},{8,10},{11,... | collective-permute-start | bytes 73880 | tf_op jit(solution)/shard_map/ppermute | solution.py:17
  41.8 15.4 %collective-permute-start.10 = (f32[2,3,1030]{2,1,0:T(4,128)S(1)}, f32[2,3,1030]{2,1,0:T(4,128)S(1)}, u32[]{:S(2)}, u32[]{:S(2)}) collective-permute-start(f32[2,3,1030]{2,1,0:T(4,128)S(1)} %get-tuple-element.49), channel_id=1, source_target_pairs={{0,2},{2,0},{1,3},{3,1},{4,6},{6,4},{5,7},{7,5},{8,10},{10,8},{9,1... | collective-permute-start | bytes 74168 | tf_op jit(solution)/shard_map/ppermute | solution.py:16
  43.4 13.7 %collective-permute-start.11 = (f32[2,3,1030]{2,1,0:T(4,128)S(1)}, f32[2,3,1030]{2,1,0:T(4,128)S(1)}, u32[]{:S(2)}, u32[]{:S(2)}) collective-permute-start(f32[2,3,1030]{2,1,0:T(4,128)S(1)} %get-tuple-element.50), channel_id=1, source_target_pairs={{2,0},{0,2},{3,1},{1,3},{6,4},{4,6},{7,5},{5,7},{10,8},{8,10},{11,... | collective-permute-start | bytes 74168 | tf_op jit(solution)/shard_map/ppermute | solution.py:17
  49.3 1.7 %copy-start.10 = (f32[32,1024]{1,0:T(8,128)S(1)}, f32[32,1024]{1,0:T(8,128)}, u32[]{:S(2)}) copy-start(f32[32,1024]{1,0:T(8,128)} %param.11) | copy-start | bytes 393220
  53.3 8.4 %collective-permute-start.4 = (f32[2,6,32,3]{3,1,2,0:T(8,128)S(1)}, f32[2,6,32,3]{3,1,2,0:T(8,128)S(1)}, u32[]{:S(2)}, u32[]{:S(2)}) collective-permute-start(f32[2,6,32,3]{3,1,2,0:T(8,128)S(1)} %get-tuple-element.42), channel_id=1, source_target_pairs={{0,4},{4,8},{8,12},{12,0},{1,5},{5,9},{9,13},{13,1},{2,6},{6,10},{... | collective-permute-start | bytes 13832 | tf_op jit(solution)/shard_map/ppermute | solution.py:16
  53.3 9.3 %collective-permute-start.5 = (f32[2,6,32,3]{3,1,2,0:T(8,128)S(1)}, f32[2,6,32,3]{3,1,2,0:T(8,128)}, u32[]{:S(2)}, u32[]{:S(2)}) collective-permute-start(f32[2,6,32,3]{3,1,2,0:T(8,128)S(1)} %get-tuple-element.41), channel_id=1, source_target_pairs={{4,0},{8,4},{12,8},{0,12},{5,1},{9,5},{13,9},{1,13},{6,2},{10,6},{... | collective-permute-start | bytes 13832 | tf_op jit(solution)/shard_map/ppermute | solution.py:17
  66.0 6.0 %collective-permute-start.6 = (f32[2,6,3,1030]{3,1,2,0:T(8,128)S(1)}, f32[2,6,3,1030]{3,1,2,0:T(8,128)S(1)}, u32[]{:S(2)}, u32[]{:S(2)}) collective-permute-start(f32[2,6,3,1030]{3,1,2,0:T(8,128)S(1)} %get-tuple-element.37), channel_id=1, source_target_pairs={{0,2},{2,0},{1,3},{3,1},{4,6},{6,4},{5,7},{7,5},{8,10},{10,8},{9,1... | collective-permute-start | bytes 444968 | tf_op jit(solution)/shard_map/ppermute | solution.py:16
  66.5 7.9 %collective-permute-start.7 = (f32[2,6,3,1030]{3,1,2,0:T(8,128)S(1)}, f32[2,6,3,1030]{3,1,2,0:T(8,128)S(1)}, u32[]{:S(2)}, u32[]{:S(2)}) collective-permute-start(f32[2,6,3,1030]{3,1,2,0:T(8,128)S(1)} %get-tuple-element.38), channel_id=1, source_target_pairs={{2,0},{0,2},{3,1},{1,3},{6,4},{4,6},{7,5},{5,7},{10,8},{8,10},{11,... | collective-permute-start | bytes 444968 | tf_op jit(solution)/shard_map/ppermute | solution.py:17
  68.6 14.1 %copy-start.2 = (f32[2,34,1025]{2,1,0:T(8,128)}, f32[2,34,1025]{2,1,0:T(8,128)S(1)}, u32[]{:S(2)}) copy-start(f32[2,34,1025]{2,1,0:T(8,128)S(1)} %slice.513) | copy-start | bytes 836404
  68.7 10.9 %copy-start.6 = (f32[2,35,1028]{2,1,0:T(8,128)}, f32[2,35,1028]{2,1,0:T(8,128)S(1)}, u32[]{:S(2)}) copy-start(f32[2,35,1028]{2,1,0:T(8,128)S(1)} %slice.507) | copy-start | bytes 863524
  68.9 14.6 %copy-start.4 = (f32[2,33,1026]{2,1,0:T(8,128)}, f32[2,33,1026]{2,1,0:T(8,128)S(1)}, u32[]{:S(2)}) copy-start(f32[2,33,1026]{2,1,0:T(8,128)S(1)} %slice.518) | copy-start | bytes 812596
  86.0 8.5 %copy-start = (f32[2,6,32,1024]{3,1,2,0:T(8,128)}, f32[2,6,32,1024]{3,1,2,0:T(8,128)S(1)}, u32[]{:S(2)}) copy-start(f32[2,6,32,1024]{3,1,2,0:T(8,128)S(1)} %slice_subtract_fusion.22) | copy-start | bytes 4718596
  86.2 8.4 %collective-permute-start.12 = (f32[2,6,32,3]{3,1,2,0:T(8,128)S(1)}, f32[2,6,32,3]{3,1,2,0:T(8,128)S(1)}, u32[]{:S(2)}, u32[]{:S(2)}) collective-permute-start(f32[2,6,32,3]{3,1,2,0:T(8,128)S(1)} %get-tuple-element.40), channel_id=1, source_target_pairs={{0,4},{4,8},{8,12},{12,0},{1,5},{5,9},{9,13},{13,1},{2,6},{6,10},{... | collective-permute-start | bytes 13832 | tf_op jit(solution)/shard_map/ppermute | solution.py:16
  87.4 9.3 %collective-permute-start.13 = (f32[2,6,32,3]{3,1,2,0:T(8,128)S(1)}, f32[2,6,32,3]{3,1,2,0:T(8,128)}, u32[]{:S(2)}, u32[]{:S(2)}) collective-permute-start(f32[2,6,32,3]{3,1,2,0:T(8,128)S(1)} %get-tuple-element.39), channel_id=1, source_target_pairs={{4,0},{8,4},{12,8},{0,12},{5,1},{9,5},{13,9},{1,13},{6,2},{10,6},{... | collective-permute-start | bytes 13832 | tf_op jit(solution)/shard_map/ppermute | solution.py:17
  94.6 0.7 copy-start.9
  100.0 6.0 %collective-permute-start.14 = (f32[2,6,3,1030]{3,1,2,0:T(8,128)S(1)}, f32[2,6,3,1030]{3,1,2,0:T(8,128)S(1)}, u32[]{:S(2)}, u32[]{:S(2)}) collective-permute-start(f32[2,6,3,1030]{3,1,2,0:T(8,128)S(1)} %get-tuple-element.35), channel_id=1, source_target_pairs={{0,2},{2,0},{1,3},{3,1},{4,6},{6,4},{5,7},{7,5},{8,10},{10,8},{9,1... | collective-permute-start | bytes 444968 | tf_op jit(solution)/shard_map/ppermute | solution.py:16
  100.5 7.9 %collective-permute-start.15 = (f32[2,6,3,1030]{3,1,2,0:T(8,128)S(1)}, f32[2,6,3,1030]{3,1,2,0:T(8,128)S(1)}, u32[]{:S(2)}, u32[]{:S(2)}) collective-permute-start(f32[2,6,3,1030]{3,1,2,0:T(8,128)S(1)} %get-tuple-element.36), channel_id=1, source_target_pairs={{2,0},{0,2},{3,1},{1,3},{6,4},{4,6},{7,5},{5,7},{10,8},{8,10},{11,... | collective-permute-start | bytes 444968 | tf_op jit(solution)/shard_map/ppermute | solution.py:17
  112.7 1.0 copy-start.7
  114.1 2.7 %copy-start.3 = (f32[2,34,1025]{2,1,0:T(8,128)S(1)}, f32[2,34,1025]{2,1,0:T(8,128)}, u32[]{:S(2)}) copy-start(f32[2,34,1025]{2,1,0:T(8,128)} %copy-done.2) | copy-start | bytes 836404
  116.8 1.0 copy-start.5
where the time goes:
time: 123 us; the launch traced here: 122 us
  other arithmetic  29.1 us (24%)
  starting transfers between devices  25.1 us (20%)
  waiting for transfers between devices  24.2 us (20%)
  local copies, waits for them, and re-layouts  21.9 us (18%)
  blocking collectives  13.9 us (11%)
  between operations  8.14 us (7%)
    ppermute x8, starting transfers between devices, padded_2(): after = lax.ppermute(leading, axis, down)  16.4 us
    ppermute x8, waiting for transfers between devices, padded_2(): before = lax.ppermute(last, axis, up)  15.8 us
    sub x6, other arithmetic, advance(): field_pad[:, :, 1:-1, 1:-1] + belt_flux[:, :, 1:-1, 1:]  15.4 us
    all_gather x1, blocking collectives, per_device(): gathered = lax.all_gather(rims, 'belt', axis=3, tiled=True)  13.9 us
    ppermute x8, starting transfers between devices, padded_2(): before = lax.ppermute(last, axis, up)  8.65 us
    concatenate x4, local copies, waits for them, and re-layouts, padded_2(): array = jnp.concatenate([before, array, after], axis=dim)  8.63 us
    ppermute x8, waiting for transfers between devices, padded_2(): after = lax.ppermute(leading, axis, down)  8.35 us
    mul x6, other arithmetic, advance(): belt_part[:, None] * (field_pad[:, :, :, 1:] - field_pad[:, :, :, :-1])  5.11 us
  transfers between devices with their start and end apart: 16, of which 9 were waited for; matrix products, arithmetic and copies ran while one was open for 13% of the time, Pallas kernels for 0%

commit v1 on v0

v1 whole, which is shorter than its diff:
```python
import functools

import jax
import jax.numpy as jnp
from jax import lax
from jax.experimental import pallas as pl
from jax.experimental.pallas import tpu as pltpu
from jax.sharding import PartitionSpec as P

STEPS = 6
LANES = 128
SUB = 8
SLOTS = 8
BF = jnp.bfloat16
F32 = jnp.float32


def split_hi_lo(value):
    hi = value.astype(BF).astype(F32)
    return hi, value - hi


def lane_iota():
    return lax.broadcasted_iota(jnp.int32, (SUB, LANES), 1)


def sub_iota(width):
    return lax.broadcasted_iota(jnp.int32, (SUB, width), 0)


def compact(tiles):
    slot = lane_iota() // 16
    packed = []
    for at in range(0, len(tiles), SLOTS):
        total = None
        for g, tile in enumerate(tiles[at : at + SLOTS]):
            moved = pltpu.roll(tile, (8 + 16 * g) % LANES, 1)
            total = moved if total is None else jnp.where(slot == g, moved, total)
        packed.append(total)
    return packed


def expand(packed, index):
    tile = packed[index // SLOTS]
    return pltpu.roll(tile, (-(8 + 16 * (index % SLOTS))) % LANES, 1)


def pack_kernel(ends, place_ref, wind_ref, metric_ref, kappa_ref, bulk_ref, corner_ref, side_ref, rim_ref):
    fields, levels, rows, cols = (2, wind_ref.shape[1], wind_ref.shape[2], wind_ref.shape[3])
    first = place_ref[1] == 0
    left = lane_iota() < LANES // 2
    top, bottom = slice(0, SUB), slice(rows - SUB, rows)

    def bands(whole):
        if ends == "pick":
            return [jnp.where(first, whole[bottom], whole[top])]
        return [whole[bottom], whole[top]]

    def edge(band):
        return jnp.where(left, band[:, :LANES], band[:, cols - LANES :])

    counts = 1 if ends == "pick" else 2
    band_rows = [[] for _ in range(counts)]
    side_tiles = []
    rim_rows = []
    for c in range(fields):
        for lev in range(levels):
            whole = wind_ref[c, lev].astype(F32)
            for at, band in enumerate(bands(whole)):
                band_rows[at].append(band)
            side_tiles += [edge(whole[r : r + SUB]) for r in range(0, rows, SUB)]
            rim_rows.append(jnp.where(first, whole[0:1], whole[rows - 1 : rows]))
    for q in range(fields + 1):
        whole = kappa_ref[q] if q < fields else metric_ref[...]
        for part in split_hi_lo(whole):
            for at, band in enumerate(bands(part)):
                band_rows[at].append(band)
            side_tiles += [edge(part[r : r + SUB]) for r in range(0, rows, SUB)]
    for at in range(counts):
        pieces = band_rows[at]
        for i in range(0, len(pieces), 2):
            both = jnp.concatenate([pieces[i], pieces[i + 1]], axis=0)
            bulk_ref[at, SUB * i : SUB * (i + 2)] = both.astype(BF)
        packed = compact([edge(p) for p in pieces])
        packed += [jnp.zeros((SUB, LANES), F32)] * (-len(packed) % 2)
        corner_ref[at] = jnp.concatenate(packed, axis=0).astype(BF)
    packed = compact(side_tiles)
    packed += [jnp.zeros((SUB, LANES), F32)] * (-len(packed) % 2)
    rim = jnp.concatenate(rim_rows + [jnp.zeros((16 - len(rim_rows), cols), F32)], axis=0).astype(BF)
    rim_ref[...] = rim
    side_ref[0:16] = rim
    for i in range(0, len(packed), 2):
        both = jnp.concatenate(packed[i : i + 2], axis=0).astype(BF)
        side_ref[16:32, LANES * (i // 2) : LANES * (i // 2 + 1)] = both
    done = LANES * (len(packed) // 2)
    side_ref[16:32, done:] = jnp.zeros((16, cols - done), BF)


def main_kernel(
    halves, slots, place_ref, wind_ref, metric_ref, kappa_ref, bulk_ref, side_a_ref, side_b_ref,
    corner_a_ref, corner_b_ref, rims_ref, out_ref, km_ref, coef_ref, ghost_ref,
):
    levels, rows, cols = wind_ref.shape[1], wind_ref.shape[2], wind_ref.shape[3]
    width = cols + LANES
    height = rows + SUB * halves
    tiles = rows // SUB
    at_belt, at_across, n_across = place_ref[0], place_ref[1], place_ref[2]
    first, last = at_across == 0, at_across == n_across - 1
    left = lane_iota() < LANES // 2
    even = lax.rem(at_belt, 2) == 0

    def side_tile(index):
        at, column = 16 + SUB * ((index // SLOTS) % 2), LANES * (index // SLOTS // 2)
        a = side_a_ref[16:32, column : column + LANES].astype(F32)[at - 16 : at - 8]
        b = side_b_ref[16:32, column : column + LANES].astype(F32)[at - 16 : at - 8]
        both = jnp.where(left == even, a, b)
        return pltpu.roll(both, (-(8 + 16 * (index % SLOTS))) % LANES, 1)

    def mix(index, a, b):
        shift = (-(8 + 16 * (index % SLOTS))) % LANES
        a = pltpu.roll(a, shift, 1)
        b = pltpu.roll(b, shift, 1)
        return jnp.where(left == even, a, b)

    def own_halo(index):
        group = index // SLOTS
        column = LANES * (group // 2)
        half = slice(SUB * (group % 2), SUB * (group % 2) + SUB)
        a = side_a_ref[16:32, column : column + LANES].astype(F32)[half]
        b = side_b_ref[16:32, column : column + LANES].astype(F32)[half]
        return mix(index, a, b)

    def band_halo(at, index):
        group = index // SLOTS
        base = 16 * (group // 2)
        half = slice(SUB * (group % 2), SUB * (group % 2) + SUB)
        a = corner_a_ref[at, base : base + 16].astype(F32)[half]
        b = corner_b_ref[at, base : base + 16].astype(F32)[half]
        return mix(index, a, b)

    def band(at, index):
        base = 16 * (index // 2)
        half = slice(SUB * (index % 2), SUB * (index % 2) + SUB)
        body = bulk_ref[at, base : base + 16].astype(F32)[half]
        return jnp.concatenate([body, band_halo(at, index)], axis=1)

    def slab(own, index, piece):
        halo = jnp.concatenate([own_halo(index * tiles + r) for r in range(tiles)], axis=0)
        rows_own = jnp.concatenate([own, halo], axis=1)
        return jnp.concatenate([rows_own] + [piece(at) for at in range(halves)], axis=0)

    @pl.when(pl.program_id(0) == 0)
    def _():
        fields = 2 * levels
        for q in range(3):
            own = kappa_ref[q] if q < 2 else metric_ref[...]
            hi, lo = split_hi_lo(own)
            i = fields + 2 * q
            km_ref[q] = slab(hi, i, lambda at, i=i: band(at, i)) + slab(
                lo, i + 1, lambda at, i=i: band(at, i + 1)
            )
        at_row = lax.broadcasted_iota(jnp.int32, (height, width), 0)
        closed = ((at_row == rows - 1) & last) | ((at_row == height - 1) & first)
        for q in range(2):
            kappa = km_ref[q]
            east = 0.5 * (kappa + pltpu.roll(kappa, width - 1, 1))
            west = pltpu.roll(east, 1, 1)
            south = jnp.where(closed, 0.0, 0.5 * (kappa + pltpu.roll(kappa, height - 1, 0)))
            north = pltpu.roll(south, 1, 0)
            coef_ref[q, 0] = 1.0 - ((east + west) + (south + north))
            coef_ref[q, 1] = east
            coef_ref[q, 2] = west
            coef_ref[q, 3] = south
            coef_ref[q, 4] = north
        km_ref[2] = 0.5 * km_ref[2]
        edge = jnp.where(first, 0, 1)
        n_belt = place_ref[3]
        lane_r = lax.broadcasted_iota(jnp.int32, (LANES, LANES), 0)
        lane_c = lax.broadcasted_iota(jnp.int32, (LANES, LANES), 1)
        forward = jnp.where(lane_r == lane_c, 1.0, 0.0)
        backward = jnp.where(lane_r + lane_c == LANES - 1, 1.0, 0.0)

        def ghost_tile(block, t):
            base = 4 + 3 * (edge * n_belt + block)
            peer, flip, turn = place_ref[base], place_ref[base + 1], place_ref[base + 2]
            flipped = flip == 1
            source = jnp.where(flipped, cols // LANES - 1 - t, t)
            found = None
            slot = place_ref[4 + 6 * n_belt + peer]
            raw = rims_ref[slot, :, pl.ds(pl.multiple_of(source * LANES, LANES), LANES)]
            turned = jnp.where(flipped, backward, forward).astype(BF)
            found = jnp.dot(raw, turned, preferred_element_type=F32)
            p, q = found[0:levels], found[levels : 2 * levels]
            cosine = jnp.where(turn == 0, 1.0, jnp.where(turn == 2, -1.0, 0.0))
            sine_neg = jnp.where(turn == 1, -1.0, jnp.where(turn == 3, 1.0, 0.0))
            return cosine * p + sine_neg * q, cosine * q - sine_neg * p

        for t in range(cols // LANES):
            for c, part in enumerate(ghost_tile(at_belt, t)):
                ghost_ref[c, 0:levels, LANES * t : LANES * (t + 1)] = part
        right = lax.rem(at_belt + 1, n_belt)
        before = lax.rem(at_belt + n_belt - 1, n_belt)
        after_tiles = ghost_tile(right, 0)
        before_tiles = ghost_tile(before, cols // LANES - 1)
        lane_row = lax.broadcasted_iota(jnp.int32, (levels, LANES), 1)
        for c in range(2):
            both = jnp.where(lane_row < LANES // 2, after_tiles[c], before_tiles[c])
            ghost_ref[c, 0:levels, cols:] = both

    level = pl.program_id(0)
    at_sub = sub_iota(width)
    winds = []
    for c in range(2):
        pass

    def field_index(c):
        return c * levels + level

    del field_index
    for lev in range(levels):

        @pl.when(level == lev)
        def _(lev=lev):
            winds = []
            for c in range(2):
                index = c * levels + lev
                ghost = ghost_ref[c, lev : lev + 1, :]

                def piece(at, index=index, ghost=ghost):
                    rows_at = band(at, index)
                    if halves == 1 or at == 1:
                        rows_at = jnp.where(first & (at_sub == SUB - 1), ghost, rows_at)
                    if at == 0:
                        rows_at = jnp.where(last & (at_sub == 0), ghost, rows_at)
                    return rows_at

                winds.append(slab(wind_ref[c, lev].astype(F32), index, piece))
            metric = km_ref[2]
            u, v = winds
            across_u = pltpu.roll(u, height - 1, 0) - pltpu.roll(u, 1, 0)
            across_v = pltpu.roll(v, height - 1, 0) - pltpu.roll(v, 1, 0)
            belt_u = pltpu.roll(u, width - 1, 1) - pltpu.roll(u, 1, 1)
            belt_v = pltpu.roll(v, width - 1, 1) - pltpu.roll(v, 1, 1)
            values = [metric * (across_u - belt_v), -metric * (belt_u + across_v)]
            for _ in range(STEPS):
                updated = []
                for c, f in enumerate(values):
                    updated.append(
                        coef_ref[c, 0] * f
                        + coef_ref[c, 1] * pltpu.roll(f, width - 1, 1)
                        + coef_ref[c, 2] * pltpu.roll(f, 1, 1)
                        + coef_ref[c, 3] * pltpu.roll(f, height - 1, 0)
                        + coef_ref[c, 4] * pltpu.roll(f, 1, 0)
                    )
                values = updated
            for c in range(2):
                out_ref[c, 0] = values[c][:rows, :cols]


def per_device(wind, metric, kappa, edge_peer, edge_flip, edge_turn):
    _, levels, rows, cols = wind.shape
    n_across, n_belt = lax.axis_size("across"), lax.axis_size("belt")
    at_across, at_belt = lax.axis_index("across"), lax.axis_index("belt")
    halves = 1 if n_across == 2 else 2
    bands = 2 * levels + 6
    corner_rows = 16 * (-(-bands // (2 * SLOTS)))

    blocks = jnp.arange(n_belt, dtype=jnp.int32)
    if n_belt == 4:
        offset = blocks ^ at_belt
        slot_of = jnp.where(offset == 2, 3, jnp.where(offset == 3, 2, offset))
    else:
        slot_of = blocks
    table = jnp.stack([edge_peer, edge_flip, edge_turn], axis=-1).reshape(-1)
    head = jnp.stack([at_belt, at_across, jnp.int32(n_across), jnp.int32(n_belt)])
    place = jnp.concatenate([head.astype(jnp.int32), table, slot_of.astype(jnp.int32)])

    vmem = pl.BlockSpec(memory_space=pltpu.VMEM)
    smem = pl.BlockSpec(memory_space=pltpu.SMEM)
    bulk, corner, side, rim = pl.pallas_call(
        functools.partial(pack_kernel, "pick" if halves == 1 else "both"),
        out_shape=[
            jax.ShapeDtypeStruct((halves, SUB * bands, cols), BF),
            jax.ShapeDtypeStruct((halves, corner_rows, LANES), BF),
            jax.ShapeDtypeStruct((32, cols), BF),
            jax.ShapeDtypeStruct((16, cols), BF),
        ],
        in_specs=[smem, vmem, vmem, vmem],
        out_specs=[vmem] * 4,
        compiler_params=pltpu.CompilerParams(vmem_limit_bytes=32 << 20),
        name="pack",
    )(place, wind, metric, kappa)

    pairs_a = [(i, i ^ 1) for i in range(n_belt)]
    pairs_b = [(i, ((i ^ 1) + 2 * (i % 2) - 2 * (1 - i % 2)) % n_belt) for i in range(n_belt)]
    pairs_b = [(i, (i + 1) % n_belt if i % 2 else (i - 1) % n_belt) for i in range(n_belt)]
    if halves == 1:
        swap = [(0, 1), (1, 0)]
        corner_in = lax.ppermute(corner, "across", swap)
        bulk_in = lax.ppermute(bulk, "across", swap)
    else:
        onward = [(i, i + 1) for i in range(n_across - 1)]
        back = [(i + 1, i) for i in range(n_across - 1)]

        def both_ways(message):
            return jnp.stack(
                [
                    lax.ppermute(message[1], "across", back),
                    lax.ppermute(message[0], "across", onward),
                ]
            )

        corner_in, bulk_in = both_ways(corner), both_ways(bulk)
    side_a = lax.ppermute(side, "belt", pairs_a)
    side_b = lax.ppermute(side, "belt", pairs_b)
    corner_a = lax.ppermute(corner_in, "belt", pairs_a)
    corner_b = lax.ppermute(corner_in, "belt", pairs_b)
    if n_belt == 4:
        rim_c = lax.ppermute(rim, "belt", [(i, i ^ 2) for i in range(n_belt)])
        rims = jnp.stack([rim, side_a[:16], side_b[:16], rim_c])
    else:
        rims = lax.all_gather(rim, "belt")

    height, width = rows + SUB * halves, cols + LANES
    whole = lambda shape: pl.BlockSpec(shape, lambda i: (0,) * len(shape))
    operands = [wind, metric, kappa, bulk_in, side_a, side_b, corner_a, corner_b, rims]
    return pl.pallas_call(
        functools.partial(main_kernel, halves, n_belt),
        grid=(levels,),
        out_shape=jax.ShapeDtypeStruct((2, levels, rows, cols), F32),
        in_specs=[smem] + [whole(x.shape) for x in operands],
        out_specs=pl.BlockSpec((2, 1, rows, cols), lambda i: (0, i, 0, 0)),
        scratch_shapes=[
            pltpu.VMEM((3, height, width), F32),
            pltpu.VMEM((2, 5, height, width), F32),
            pltpu.VMEM((2, SUB, width), F32),
        ],
        compiler_params=pltpu.CompilerParams(vmem_limit_bytes=48 << 20),
        name="diffuse",
    )(place, *operands)


def solution(mesh):
    return jax.shard_map(
        per_device,
        mesh=mesh,
        in_specs=(
            P(None, ("members", "lev"), "across", "belt"),
            P("across", "belt"),
            P(None, "across", "belt"),
            P(),
            P(),
            P(),
        ),
        out_specs=P(None, ("members", "lev"), "across", "belt"),
        check_vma=False,
    )
```

time: 123 us -> 32.1 us (0.26)
  other arithmetic: 29.1 us -> 0.74 us
  waiting for transfers between devices: 24.2 us -> 4.57 us
  local copies, waits for them, and re-layouts: 21.9 us -> 3.28 us
  starting transfers between devices: 25.1 us -> 10.6 us
  blocking collectives: 13.9 us -> 0 us
  Pallas kernels: 0 us -> 12.7 us
  between operations: 8.14 us -> 0.06 us
    ppermute x16 -> x7, waiting for transfers between devices: 24.2 us -> 4.57 us  [the longest x1 2.61 us: per_device(): corner_b = lax.ppermute(corner_in, 'belt', pairs_b)]
    sub x6 -> x0, other arithmetic: 15.4 us -> none  [advance(): field_pad[:, :, 1:-1, 1:-1] + belt_flux[:, :, 1:-1, 1:]]
    ppermute x16 -> x7, starting transfers between devices: 25.1 us -> 10.6 us  [the longest x1 5.11 us: per_device(): side_b = lax.ppermute(side, 'belt', pairs_b)]
    all_gather x1 -> x0, blocking collectives: 13.9 us -> none  [per_device(): gathered = lax.all_gather(rims, 'belt', axis=3, tiled=True)]
    pallas_call x0 -> x2, Pallas kernels: none -> 12.7 us  [the longest x1 11.9 us: per_device(): pl.pallas_call(functools.partial(main_kernel, halves, n_belt), grid=(leve...]
    mul x17 -> x0, other arithmetic: 9.63 us -> none  [the longest x6 5.11 us: advance(): belt_part[:, None] * (field_pad[:, :, :, 1:] - field_pad[:, :, :, :-1])]
    concatenate x4 -> x1, local copies, waits for them, and re-layouts: 8.63 us -> 0.09 us  [per_device(): jnp.concatenate([head.astype(jnp.int32), table, slot_of.astype(jnp.int32)])]
    slice x13 -> x0, local copies, waits for them, and re-layouts: 2.91 us -> none  [the longest x1 1.1 us: per_device(): rims = jnp.stack([wind[:, :, 0, :], wind[:, :, rows - 1, :]])]
  transfers between devices with their start and end apart: 16 -> 7, of which waited for: 9 -> 3; matrix products, arithmetic and copies ran while one was open for 13% -> 0% of each run, Pallas kernels for 0% -> 0%
where the time goes in v1:
time: 32.1 us; the launch traced here: 31.9 us
  Pallas kernels  12.7 us (40%)
  starting transfers between devices  10.6 us (33%)
  waiting for transfers between devices  4.57 us (14%)
  local copies, waits for them, and re-layouts  3.28 us (10%)
  other arithmetic  0.74 us (2%)
    pallas_call x1, Pallas kernels, per_device(): pl.pallas_call(functools.partial(main_kernel, halves, n_belt), grid=(leve...  11.9 us
    ppermute x1, starting transfers between devices, per_device(): side_b = lax.ppermute(side, 'belt', pairs_b)  5.11 us
    unnamed x12, local copies, waits for them, and re-layouts  3 us
    ppermute x1, starting transfers between devices, per_device(): corner_b = lax.ppermute(corner_in, 'belt', pairs_b)  2.77 us
    ppermute x1, waiting for transfers between devices, per_device(): corner_b = lax.ppermute(corner_in, 'belt', pairs_b)  2.61 us
    ppermute x1, starting transfers between devices, per_device(): corner_in = lax.ppermute(corner, 'across', swap)  1.49 us
    ppermute x1, waiting for transfers between devices, per_device(): corner_in = lax.ppermute(corner, 'across', swap)  0.98 us
    ppermute x1, waiting for transfers between devices, per_device(): corner_a = lax.ppermute(corner_in, 'belt', pairs_a)  0.97 us
  transfers between devices with their start and end apart: 7, of which 3 were waited for; matrix products, arithmetic and copies ran while one was open for 0% of the time, Pallas kernels for 0%

profile of v1, /device:TPU:0, one launch (start us, length us, event | category | flops | bytes accessed | tf_op | source)
XLA Modules:
  0.0 31.9 jit_solution(6502929446379783536)
XLA Ops:
  0.0 0.7 %pad_add_fusion = s32[2,4,3]{1,0,2:T(2,128)S(1)} fusion(s32[2,4,1]{1,0,2:T(2,128)} %bitcast.13, s32[2,4,1]{1,0,2:T(2,128)} %bitcast.14, s32[2,4,1]{1,0,2:T(2,128)} %bitcast.15), kind=kLoop, calls=%fused_computation.3 | loop fusion | flops 48 | bytes 192 | tf_op jit(solution)/shard_map/stack | solution.py:274
  0.7 0.1 copy.8
  0.8 0.1 reshape.3
  0.9 0.1 concatenate.3.place_ref
  1.0 0.0 copy-start
  1.0 1.1 %copy-done = bf16[2,6,32,1024]{3,2,1,0:T(8,128)(2,1)S(1)} copy-done((bf16[2,6,32,1024]{3,2,1,0:T(8,128)(2,1)S(1)}, bf16[2,6,32,1024]{3,2,1,0:T(8,128)(2,1)}, u32[]{:S(2)}) %copy-start) | copy-done | bytes 786456
  2.1 0.0 copy-start.2
  2.1 0.9 %copy-done.2 = f32[2,32,1024]{2,1,0:T(8,128)S(1)} copy-done((f32[2,32,1024]{2,1,0:T(8,128)S(1)}, f32[2,32,1024]{2,1,0:T(8,128)}, u32[]{:S(2)}) %copy-start.2) | copy-done | bytes 262168
  3.1 0.0 copy-start.4
  3.1 0.9 %copy-done.4 = f32[32,1024]{1,0:T(8,128)S(1)} copy-done((f32[32,1024]{1,0:T(8,128)S(1)}, f32[32,1024]{1,0:T(8,128)}, u32[]{:S(2)}) %copy-start.4) | copy-done | bytes 131096
  4.0 0.0 copy-start.1
  4.0 0.0 copy-start.3
  4.0 0.0 copy-start.5
  4.0 0.8 %pack.1 = (bf16[1,144,1024]{2,1,0:T(8,128)(2,1)S(1)}, bf16[1,32,128]{2,1,0:T(8,128)(2,1)S(1)}, bf16[32,1024]{1,0:T(8,128)(2,1)S(1)}, bf16[16,1024]{1,0:T(8,128)(2,1)S(1)}) custom-call(s32[32]{0:T(128)S(1)} %concatenate.3.place_ref, bf16[2,6,32,1024]{3,2,1,0:T(8,128)(2,1)S(1)} %copy-done, f32[32,1024]{1,0:T(8,128)S(1)} %copy-done.4, f32[2,32,1024]{2,1,0:T(8,128)S(1)} %copy-done.2), custom_call_target="tpu_custom_call" | custom-call | tf_op jit(solution)/shard_map/pack/pallas_call | solution.py:280
  4.8 5.1 %collective-permute-start.2 = (bf16[32,1024]{1,0:T(8,128)(2,1)S(1)}, bf16[32,1024]{1,0:T(8,128)(2,1)S(1)}, u32[]{:S(2)}, u32[]{:S(2)}) collective-permute-start(bf16[32,1024]{1,0:T(8,128)(2,1)S(1)} %get-tuple-element.10), channel_id=1, source_target_pairs={{0,12},{4,8},{8,4},{12,0},{1,13},{5,9},{9,5},{13,1},{2,14},{6,10},... | collective-permute-start | bytes 196616 | tf_op jit(solution)/shard_map/ppermute | solution.py:315
  9.9 1.5 %collective-permute-start.3 = (bf16[1,32,128]{2,1,0:T(8,128)(2,1)S(1)}, bf16[1,32,128]{2,1,0:T(8,128)(2,1)S(1)}, u32[]{:S(2)}, u32[]{:S(2)}) collective-permute-start(bf16[1,32,128]{2,1,0:T(8,128)(2,1)S(1)} %get-tuple-element.11), channel_id=1, source_target_pairs={{0,2},{2,0},{1,3},{3,1},{4,6},{6,4},{5,7},{7,5},{8,10},{10,8},{9,1... | collective-permute-start | bytes 24584 | tf_op jit(solution)/shard_map/ppermute | solution.py:299
  11.4 0.0 collective-permute-start.1
  11.4 0.8 %collective-permute-start.6 = (bf16[16,1024]{1,0:T(8,128)(2,1)S(1)}, bf16[16,1024]{1,0:T(8,128)(2,1)S(1)}, u32[]{:S(2)}, u32[]{:S(2)}) collective-permute-start(bf16[16,1024]{1,0:T(8,128)(2,1)S(1)} %get-tuple-element.12), channel_id=1, source_target_pairs={{0,8},{4,12},{8,0},{12,4},{1,9},{5,13},{9,1},{13,5},{2,10},{6,14},... | collective-permute-start | bytes 98312 | tf_op jit(solution)/shard_map/ppermute | solution.py:319
  12.2 0.4 %collective-permute-start = (bf16[1,144,1024]{2,1,0:T(8,128)(2,1)S(1)}, bf16[1,144,1024]{2,1,0:T(8,128)(2,1)S(1)}, u32[]{:S(2)}, u32[]{:S(2)}) collective-permute-start(bf16[1,144,1024]{2,1,0:T(8,128)(2,1)S(1)} %get-tuple-element.9), channel_id=1, source_target_pairs={{0,2},{2,0},{1,3},{3,1},{4,6},{6,4},{5,7},{7,5},{8,10},{10,8},{9,1... | collective-permute-start | bytes 884744 | tf_op jit(solution)/shard_map/ppermute | solution.py:300
  12.6 1.0 %collective-permute-done.3 = bf16[1,32,128]{2,1,0:T(8,128)(2,1)S(1)} collective-permute-done((bf16[1,32,128]{2,1,0:T(8,128)(2,1)S(1)}, bf16[1,32,128]{2,1,0:T(8,128)(2,1)S(1)}, u32[]{:S(2)}, u32[]{:S(2)}) %collective-permute-start.3) | collective-permute-done | bytes 8224 | tf_op jit(solution)/shard_map/ppermute | solution.py:299
  13.6 2.8 %collective-permute-start.5 = (bf16[1,32,128]{2,1,0:T(8,128)(2,1)S(1)}, bf16[1,32,128]{2,1,0:T(8,128)(2,1)S(1)}, u32[]{:S(2)}, u32[]{:S(2)}) collective-permute-start(bf16[1,32,128]{2,1,0:T(8,128)(2,1)S(1)} %collective-permute-done.3), channel_id=1, source_target_pairs={{0,12},{4,8},{8,4},{12,0},{1,13},{5,9},{9,5},{13,1},{2,14},{6,10},... | collective-permute-start | bytes 24584 | tf_op jit(solution)/shard_map/ppermute | solution.py:317
  16.3 0.0 collective-permute-done.2.side_b_ref
  16.3 0.0 collective-permute-start.4
  16.3 0.0 collective-permute-done.1.side_a_ref
  16.4 0.0 collective-permute-done.6
  16.4 2.6 %collective-permute-done.5.corner_b_ref = bf16[1,32,128]{2,1,0:T(8,128)(2,1)S(1)} collective-permute-done((bf16[1,32,128]{2,1,0:T(8,128)(2,1)S(1)}, bf16[1,32,128]{2,1,0:T(8,128)(2,1)S(1)}, u32[]{:S(2)}, u32[]{:S(2)}) %collective-permute-start.5) | collective-permute-done | bytes 8224 | tf_op jit(solution)/shard_map/ppermute | solution.py:317
  19.0 1.0 %collective-permute-done.4.corner_a_ref = bf16[1,32,128]{2,1,0:T(8,128)(2,1)S(1)} collective-permute-done((bf16[1,32,128]{2,1,0:T(8,128)(2,1)S(1)}, bf16[1,32,128]{2,1,0:T(8,128)(2,1)S(1)}, u32[]{:S(2)}, u32[]{:S(2)}) %collective-permute-start.4) | collective-permute-done | bytes 8224 | tf_op jit(solution)/shard_map/ppermute | solution.py:316
  20.0 0.0 collective-permute-done.bulk_ref
  20.0 0.0 copy-done.1
  20.0 0.0 copy-done.3
  20.0 0.0 copy-done.5
  20.0 11.9 %diffuse.1 = f32[2,6,32,1024]{3,2,1,0:T(8,128)} custom-call(s32[32]{0:T(128)S(1)} %concatenate.3.place_ref, bf16[2,6,32,1024]{3,2,1,0:T(8,128)(2,1)S(1)} %copy-done.1, f32[32,1024]{1,0:T(8,128)S(1)} %copy-done.5, f32[2,32,1024]{2,1,0:T(8,128)S(1)} %copy-done.3, bf16[1,144,1024]{2,1,0:T(8,128)(2,1)S(1)} %collective-permute-done.bulk_ref, ...), custom_call_target="tpu_custom_call" | custom-call | tf_op jit(solution)/shard_map/diffuse/pallas_call | solution.py:327
  (4 shorter events, 0.0 us)
Async XLA Ops:
  1.0 1.1 %copy-start = (bf16[2,6,32,1024]{3,2,1,0:T(8,128)(2,1)S(1)}, bf16[2,6,32,1024]{3,2,1,0:T(8,128)(2,1)}, u32[]{:S(2)}) copy-start(bf16[2,6,32,1024]{3,2,1,0:T(8,128)(2,1)} %wind_ref.3) | copy-start | bytes 2359300
  2.1 0.9 %copy-start.2 = (f32[2,32,1024]{2,1,0:T(8,128)S(1)}, f32[2,32,1024]{2,1,0:T(8,128)}, u32[]{:S(2)}) copy-start(f32[2,32,1024]{2,1,0:T(8,128)} %kappa_ref.3) | copy-start | bytes 786436
  3.1 0.9 %copy-start.4 = (f32[32,1024]{1,0:T(8,128)S(1)}, f32[32,1024]{1,0:T(8,128)}, u32[]{:S(2)}) copy-start(f32[32,1024]{1,0:T(8,128)} %metric_ref.3) | copy-start | bytes 393220
  4.0 16.0 %copy-start.1 = (bf16[2,6,32,1024]{3,2,1,0:T(8,128)(2,1)S(1)}, bf16[2,6,32,1024]{3,2,1,0:T(8,128)(2,1)}, u32[]{:S(2)}) copy-start(bf16[2,6,32,1024]{3,2,1,0:T(8,128)(2,1)} %wind_ref.3) | copy-start | bytes 2359300
  4.0 16.0 %copy-start.3 = (f32[2,32,1024]{2,1,0:T(8,128)S(1)}, f32[2,32,1024]{2,1,0:T(8,128)}, u32[]{:S(2)}) copy-start(f32[2,32,1024]{2,1,0:T(8,128)} %kappa_ref.3) | copy-start | bytes 786436
  4.0 16.0 %copy-start.5 = (f32[32,1024]{1,0:T(8,128)S(1)}, f32[32,1024]{1,0:T(8,128)}, u32[]{:S(2)}) copy-start(f32[32,1024]{1,0:T(8,128)} %metric_ref.3) | copy-start | bytes 393220
  4.8 11.5 %collective-permute-start.2 = (bf16[32,1024]{1,0:T(8,128)(2,1)S(1)}, bf16[32,1024]{1,0:T(8,128)(2,1)S(1)}, u32[]{:S(2)}, u32[]{:S(2)}) collective-permute-start(bf16[32,1024]{1,0:T(8,128)(2,1)S(1)} %get-tuple-element.10), channel_id=1, source_target_pairs={{0,12},{4,8},{8,4},{12,0},{1,13},{5,9},{9,5},{13,1},{2,14},{6,10},... | collective-permute-start | bytes 196616 | tf_op jit(solution)/shard_map/ppermute | solution.py:315
  9.9 3.7 %collective-permute-start.3 = (bf16[1,32,128]{2,1,0:T(8,128)(2,1)S(1)}, bf16[1,32,128]{2,1,0:T(8,128)(2,1)S(1)}, u32[]{:S(2)}, u32[]{:S(2)}) collective-permute-start(bf16[1,32,128]{2,1,0:T(8,128)(2,1)S(1)} %get-tuple-element.11), channel_id=1, source_target_pairs={{0,2},{2,0},{1,3},{3,1},{4,6},{6,4},{5,7},{7,5},{8,10},{10,8},{9,1... | collective-permute-start | bytes 24584 | tf_op jit(solution)/shard_map/ppermute | solution.py:299
  11.4 4.9 %collective-permute-start.1 = (bf16[32,1024]{1,0:T(8,128)(2,1)S(1)}, bf16[32,1024]{1,0:T(8,128)(2,1)S(1)}, u32[]{:S(2)}, u32[]{:S(2)}) collective-permute-start(bf16[32,1024]{1,0:T(8,128)(2,1)S(1)} %get-tuple-element.10), channel_id=1, source_target_pairs={{0,4},{4,0},{8,12},{12,8},{1,5},{5,1},{9,13},{13,9},{2,6},{6,2},{1... | collective-permute-start | bytes 196616 | tf_op jit(solution)/shard_map/ppermute | solution.py:314
  11.4 5.0 %collective-permute-start.6 = (bf16[16,1024]{1,0:T(8,128)(2,1)S(1)}, bf16[16,1024]{1,0:T(8,128)(2,1)S(1)}, u32[]{:S(2)}, u32[]{:S(2)}) collective-permute-start(bf16[16,1024]{1,0:T(8,128)(2,1)S(1)} %get-tuple-element.12), channel_id=1, source_target_pairs={{0,8},{4,12},{8,0},{12,4},{1,9},{5,13},{9,1},{13,5},{2,10},{6,14},... | collective-permute-start | bytes 98312 | tf_op jit(solution)/shard_map/ppermute | solution.py:319
  12.2 7.8 %collective-permute-start = (bf16[1,144,1024]{2,1,0:T(8,128)(2,1)S(1)}, bf16[1,144,1024]{2,1,0:T(8,128)(2,1)S(1)}, u32[]{:S(2)}, u32[]{:S(2)}) collective-permute-start(bf16[1,144,1024]{2,1,0:T(8,128)(2,1)S(1)} %get-tuple-element.9), channel_id=1, source_target_pairs={{0,2},{2,0},{1,3},{3,1},{4,6},{6,4},{5,7},{7,5},{8,10},{10,8},{9,1... | collective-permute-start | bytes 884744 | tf_op jit(solution)/shard_map/ppermute | solution.py:300
  13.6 5.4 %collective-permute-start.5 = (bf16[1,32,128]{2,1,0:T(8,128)(2,1)S(1)}, bf16[1,32,128]{2,1,0:T(8,128)(2,1)S(1)}, u32[]{:S(2)}, u32[]{:S(2)}) collective-permute-start(bf16[1,32,128]{2,1,0:T(8,128)(2,1)S(1)} %collective-permute-done.3), channel_id=1, source_target_pairs={{0,12},{4,8},{8,4},{12,0},{1,13},{5,9},{9,5},{13,1},{2,14},{6,10},... | collective-permute-start | bytes 24584 | tf_op jit(solution)/shard_map/ppermute | solution.py:317
  16.3 3.7 %collective-permute-start.4 = (bf16[1,32,128]{2,1,0:T(8,128)(2,1)S(1)}, bf16[1,32,128]{2,1,0:T(8,128)(2,1)S(1)}, u32[]{:S(2)}, u32[]{:S(2)}) collective-permute-start(bf16[1,32,128]{2,1,0:T(8,128)(2,1)S(1)} %collective-permute-done.3), channel_id=1, source_target_pairs={{0,4},{4,0},{8,12},{12,8},{1,5},{5,1},{9,13},{13,9},{2,6},{6,2},{1... | collective-permute-start | bytes 24584 | tf_op jit(solution)/shard_map/ppermute | solution.py:316

commit v2 on v0

v2 whole, which is shorter than its diff:
```python
import functools

import jax
import jax.numpy as jnp
import numpy as np
from jax import lax
from jax.experimental import pallas as pl
from jax.experimental.pallas import tpu as pltpu
from jax.sharding import PartitionSpec as P

STEPS = 6
LANES = 128
SUB = 8
SLOTS = 8
BF = jnp.bfloat16
F32 = jnp.float32
MARGIN = STEPS + 1
WINDOW = 3 * LANES
PACK_LIMIT = 8 << 20
MID_LIMIT = 20 << 20
EDGE_LIMIT = 20 << 20
MIDDLE_FROM, MIDDLE_TO = 4 * LANES - (WINDOW - 2 * MARGIN), 4 * LANES + (WINDOW - 2 * MARGIN)
MIDDLES = [(1, MIDDLE_FROM - MARGIN - LANES, 0), (3, LANES - MARGIN, 1)]


def split_hi_lo(value):
    hi = value.astype(BF).astype(F32)
    return hi, value - hi


def lane_iota():
    return lax.broadcasted_iota(jnp.int32, (SUB, LANES), 1)


def sub_iota(width):
    return lax.broadcasted_iota(jnp.int32, (SUB, width), 0)


def compact(tiles):
    slot = lane_iota() // 16
    packed = []
    for at in range(0, len(tiles), SLOTS):
        total = None
        for g, tile in enumerate(tiles[at : at + SLOTS]):
            moved = pltpu.roll(tile, (8 + 16 * g) % LANES, 1)
            total = moved if total is None else jnp.where(slot == g, moved, total)
        packed.append(total)
    return packed


def fetched(pairs, sems):
    copies = [pltpu.make_async_copy(src, dst, sems.at[i]) for i, (src, dst) in enumerate(pairs)]
    for copy in copies:
        copy.start()
    return copies


def edge_tile(band):
    left = lax.broadcasted_iota(jnp.int32, (band.shape[0], LANES), 1) < LANES // 2
    return jnp.where(left, band[:, :LANES], band[:, band.shape[1] - LANES :])


def compact_rows(tiles):
    packed = compact(tiles)
    packed += [jnp.zeros((SUB, LANES), F32)] * (-len(packed) % 2)
    return [jnp.concatenate(packed[i : i + 2], axis=0).astype(BF) for i in range(0, len(packed), 2)]


def pack_kernel(
    halves, ends_col, wind_hbm, metric_hbm, kappa_hbm, peer_hbm,
    bulk_ref, corner_ref, rim_ref, side_ref, own_ref, pick_ref, *scratch
):
    wind_ref, kappa_ref, metric_ref, peer_ref, sems = scratch
    levels, rows, cols = wind_hbm.shape[1:]
    first = lax.axis_index("across") == 0
    pairs = [(wind_hbm, wind_ref), (kappa_hbm, kappa_ref), (metric_hbm, metric_ref), (peer_hbm, peer_ref)]
    for copy in fetched(pairs, sems):
        copy.wait()
    at_belt = lax.axis_index("belt")
    wanted = peer_ref[jnp.where(first, 0, 1), at_belt ^ 1]
    pick_ref[...] = jnp.full(pick_ref.shape, jnp.where(wanted == at_belt, 1.0, 0.0), BF)
    top, bottom = slice(0, SUB), slice(rows - SUB, rows)

    def bands_of(whole):
        if halves == 1:
            return [jnp.where(first, whole[bottom], whole[top])]
        return [whole[bottom], whole[top]]

    pieces, tiles, rim_rows = [[] for _ in range(halves)], [], []
    for f in range(2 * levels):
        own_ref[rows * f : rows * (f + 1)] = wind_ref[f // levels, f % levels]
        whole = wind_ref[f // levels, f % levels].astype(F32)
        for k, band in enumerate(bands_of(whole)):
            pieces[k].append(band)
        tiles += [edge_tile(whole[r : r + SUB]) for r in range(0, rows, SUB)]
        rim_rows.append(jnp.where(first, whole[0:1], whole[rows - 1 : rows]))
    for q in range(3):
        for half, part in enumerate(split_hi_lo(kappa_ref[q] if q < 2 else metric_ref[...])):
            at = rows * (2 * levels + 2 * q + half)
            own_ref[at : at + rows] = part.astype(BF)
            for k, band in enumerate(bands_of(part)):
                pieces[k].append(band)
            tiles += [edge_tile(part[r : r + SUB]) for r in range(0, rows, SUB)]
    for k in range(halves):
        for i in range(0, len(pieces[k]), 2):
            both = jnp.concatenate([pieces[k][i], pieces[k][i + 1]], axis=0)
            bulk_ref[k, SUB * i : SUB * (i + 2)] = both.astype(BF)
        for i, tile in enumerate(compact_rows([edge_tile(p) for p in pieces[k]])):
            corner_ref[k, :, LANES * i : LANES * (i + 1)] = tile
    rim = jnp.concatenate(rim_rows + [jnp.zeros((16 - len(rim_rows), cols), F32)], axis=0)
    rim_ref[...] = rim.astype(BF)
    side_ref[...] = jnp.zeros(side_ref.shape, BF)
    for i, tile in enumerate(compact_rows(tiles)):
        side_ref[:, LANES * i : LANES * (i + 1)] = tile
    if ends_col is not None:
        side_ref[:, ends_col : ends_col + LANES] = edge_tile(rim).astype(BF)


def rim_slot(block, at_belt, n_belt):
    if n_belt != 4:
        return block
    return jnp.where(block == at_belt, 0, jnp.where((block ^ at_belt) == 2, 2, 1))


def end_slot(block, at_belt, n_belt):
    if n_belt != 4:
        return block
    offset = block ^ at_belt
    return jnp.where(offset == 2, 3, jnp.where(offset == 3, 2, offset))


class Rows:
    def __init__(self, levels, rows, halves):
        self.levels, self.rows, self.halves = levels, rows, halves
        self.fields, self.bands = 2 * levels, 2 * levels + 6
        self.tiles, self.span = rows // SUB, SUB * halves
        self.slab = self.tiles + halves
        self.height = SUB * self.slab

    def own_base(self, f):
        return 2 * self.height * (f // 2) + (self.height + self.span) * (f % 2)

    def band_base(self, f):
        return 2 * self.height * (f // 2) + self.rows

    def place_of(self, f, e):
        return e if f % 2 == 0 else (e + self.halves) % self.slab


def east_of(f):
    return [f[1], f[2], pltpu.roll(f[0], LANES - 1, 1)]


def west_of(f):
    return [pltpu.roll(f[2], 1, 1), f[0], f[1]]


def fill_order(order_ref, source_of):
    size = order_ref.shape[0]
    at = lax.broadcasted_iota(jnp.int32, (size, LANES), 0)
    lane = lax.broadcasted_iota(jnp.int32, (1, LANES), 1)
    for r in range(3):
        tile = jnp.where(at == source_of(3 * lane + r), 1.0, 0.0).astype(BF)
        order_ref[:, LANES * r : LANES * (r + 1)] = tile
        order_ref[:, LANES * (3 + r) : LANES * (4 + r)] = tile


def solve_window(lay, first, last, x_ref, order_ref, work):
    y_ref, coef_ref, met_ref, even_ref, odd_ref, fin_ref, z_ref = work
    levels, rows, fields, tiles = lay.levels, lay.rows, lay.fields, lay.tiles
    slab, height, span = lay.slab, lay.height, lay.span
    sub = lax.broadcasted_iota(jnp.int32, (SUB, LANES), 0)
    sub_slab = lax.broadcasted_iota(jnp.int32, (height, LANES), 0)
    closed = ((sub_slab == rows - 1) & last) | ((sub_slab == height - 1) & first)

    def put(ref, f, r, i, value):
        ref[f, r, SUB * (i + 1) : SUB * (i + 2)] = value
        if i == 0:
            ref[f, r, SUB * (slab + 1) : SUB * (slab + 2)] = value
        if i == slab - 1:
            ref[f, r, 0:SUB] = value
        if r == 0:
            return [(ref, f, 3, i, pltpu.roll(value, LANES - 1, 1))]
        if r == 2:
            return [(ref, f, 4, i, pltpu.roll(value, 1, 1))]
        return []

    def flush(rotated):
        for ref, f, plane, i, value in rotated:
            ref[f, plane, SUB * (i + 1) : SUB * (i + 2)] = value

    def advance(source, target, final):
        waiting = []
        for c in range(2):
            for e in range(tiles if final else slab):
                mid, east, west, south, north = (
                    [coef_ref[c, k, r, SUB * e : SUB * (e + 1)] for r in range(3)] for k in range(5)
                )
                results = []
                for lev in range(levels):
                    f = c * levels + lev
                    at = SUB * (lay.place_of(f, e) + 1)
                    here = [source[f, r, at : at + SUB] for r in range(5)]
                    right, left = [here[1], here[2], here[3]], [here[4], here[0], here[1]]
                    results.append(
                        [
                            (mid[r] * here[r] + south[r] * source[f, r, at + 1 : at + 1 + SUB])
                            + north[r] * source[f, r, at - 1 : at - 1 + SUB]
                            + (east[r] * right[r] + west[r] * left[r])
                            for r in range(3)
                        ]
                    )
                rotated = []
                for lev in range(levels):
                    f = c * levels + lev
                    for r in range(3):
                        if final:
                            fin_ref[rows * f + SUB * e : rows * f + SUB * (e + 1), LANES * r : LANES * (r + 1)] = results[lev][r]
                        else:
                            rotated += put(target, f, r, lay.place_of(f, e), results[lev][r])
                flush(waiting)
                waiting = rotated
        flush(waiting)

    whole = jnp.dot(x_ref[...], order_ref[:, 0:WINDOW], preferred_element_type=F32)
    for r in range(3):
        y_ref[r] = whole[:, LANES * r : LANES * (r + 1)]
    for q in range(3):
        base = height * (fields + 2 * q)
        low = base + height
        value = [
            y_ref[r, base : base + height]
            + jnp.concatenate([y_ref[r, low + span : low + height], y_ref[r, low : low + span]], axis=0)
            for r in range(3)
        ]
        if q == 2:
            for r in range(3):
                met_ref[r] = 0.5 * value[r]
            continue
        right = east_of(value)
        east = [0.5 * (value[r] + right[r]) for r in range(3)]
        west = west_of(east)
        for r in range(3):
            south = jnp.where(closed, 0.0, 0.5 * (value[r] + pltpu.roll(value[r], height - 1, 0)))
            north = pltpu.roll(south, 1, 0)
            coef_ref[q, 0, r] = 1.0 - ((east[r] + west[r]) + (south + north))
            coef_ref[q, 1, r] = east[r]
            coef_ref[q, 2, r] = west[r]
            coef_ref[q, 3, r] = south
            coef_ref[q, 4, r] = north
    waiting = []
    for e in range(slab):
        rotated = []
        metric = [met_ref[r, SUB * e : SUB * (e + 1)] for r in range(3)]
        for lev in range(levels):
            across, belt = [], []
            for c in range(2):
                f = c * levels + lev
                base, i = height * f, lay.place_of(f, e)
                at = base + SUB * i
                here = [y_ref[r, at : at + SUB] for r in range(3)]
                right, left = east_of(here), west_of(here)
                belt.append([right[r] - left[r] for r in range(3)])
                diffs = []
                for r in range(3):
                    if i < slab - 1:
                        below = y_ref[r, at + 1 : at + 1 + SUB]
                    else:
                        wrap = pltpu.roll(y_ref[r, base : base + SUB], SUB - 1, 0)
                        below = jnp.where(sub == SUB - 1, wrap, pltpu.roll(here[r], SUB - 1, 0))
                    if i > 0:
                        above = y_ref[r, at - 1 : at - 1 + SUB]
                    else:
                        end = base + height
                        wrap = pltpu.roll(y_ref[r, end - SUB : end], 1, 0)
                        above = jnp.where(sub == 0, wrap, pltpu.roll(here[r], 1, 0))
                    diffs.append(below - above)
                across.append(diffs)
            for r in range(3):
                curl = metric[r] * (across[0][r] - belt[1][r])
                divergence = metric[r] * (-belt[0][r] - across[1][r])
                rotated += put(even_ref, lev, r, lay.place_of(lev, e), curl)
                rotated += put(even_ref, levels + lev, r, lay.place_of(levels + lev, e), divergence)
        flush(waiting)
        waiting = rotated
    flush(waiting)

    def two(k, _):
        advance(even_ref, odd_ref, False)
        advance(odd_ref, even_ref, False)
        return 0

    lax.fori_loop(0, STEPS // 2 - 1, two, 0)
    advance(even_ref, odd_ref, False)
    advance(odd_ref, None, True)
    value = fin_ref[...]
    hi = value.astype(BF)
    z_ref[:, 0 : 3 * LANES] = hi
    z_ref[:, 3 * LANES :] = (value - hi.astype(F32)).astype(BF)


def work_shapes(lay):
    return [
        pltpu.VMEM((3, lay.height * lay.bands, LANES), F32),
        pltpu.VMEM((2, 5, 3, lay.height, LANES), F32),
        pltpu.VMEM((3, lay.height, LANES), F32),
        pltpu.VMEM((lay.fields, 5, lay.height + 2 * SUB, LANES), F32),
        pltpu.VMEM((lay.fields, 5, lay.height + 2 * SUB, LANES), F32),
        pltpu.VMEM((lay.rows * lay.fields, WINDOW), F32),
        pltpu.VMEM((lay.rows * lay.fields, 2 * WINDOW), BF),
    ]


def back_to_natural(z, order, cols):
    return lax.dot_general(z, order[cols], (((1,), (1,)), ((), ())), preferred_element_type=F32)


def ghost_tile_at(lay, first):
    return pl.multiple_of(jnp.where(first, 0, lay.rows - SUB), SUB)


def middle_kernel(
    lay, tile, offset, keep, own_ref, bulk_ref, after_ref,
    out_ref, order_ref, coef_out, met_out, x_ref, *work,
):
    del after_ref
    first, last = lax.axis_index("across") == 0, lax.axis_index("across") == lax.axis_size("across") - 1
    cols = slice(LANES * tile, LANES * (tile + 4))
    fill_order(order_ref, lambda place: place + offset)
    for f in range(lay.bands):
        base = lay.own_base(f)
        x_ref[base : base + lay.rows] = own_ref[lay.rows * f : lay.rows * (f + 1), cols]
    span = lay.span
    at_row = lax.broadcasted_iota(jnp.int32, (2 * span, 4 * LANES), 0)
    for f in range(0, lay.bands, 2):
        band = bulk_ref[span * f : span * (f + 2), cols]
        if f < lay.fields:
            band = band.astype(F32)
            for k in range(2):
                spot = jnp.where(first, span * (k + 1) - 1, jnp.where(last, span * k, -1))
                band = jnp.where(at_row == spot, 0.0, band)
            band = band.astype(BF)
        at = lay.band_base(f)
        x_ref[at : at + 2 * span] = band
    solve_window(lay, first, last, x_ref, order_ref, work)
    back = back_to_natural(work[-1][...], order_ref, slice(LANES * keep, LANES * (keep + 3)))
    for f in range(lay.fields):
        out_ref[f // lay.levels, f % lay.levels] = back[lay.rows * f : lay.rows * (f + 1)]
    at = ghost_tile_at(lay, first)
    coef_out[...] = work[1][:, :, :, pl.ds(at, SUB)]
    met_out[...] = work[2][:, pl.ds(at, SUB)]


def edge_kernel(lay, n_belt, relay, plan, peer_ref, flip_ref, turn_ref, own_ref, bulk_ref, *rest):
    if relay is None:
        side_a_ref, side_b_ref, corner_a_ref, corner_b_ref, rims_ref, ends_ref, *rest = rest
    else:
        rim_ref, side_ref, far_ref, near_ref, *rest = rest
        *rest, rims_ref, ends_ref = rest
        corner_at, ends_at = relay
        side_a_ref, side_b_ref = near_ref.at[16:32], near_ref.at[32:48]
        corner_a_ref, corner_b_ref = (
            near_ref.at[pl.ds(k, 16), corner_at:ends_at] for k in (16, 32)
        )
        for k, rim in enumerate((rim_ref[...], near_ref[0:16], far_ref[0:16])):
            rims_ref[k] = rim
        ends_cols = slice(ends_at, ends_at + LANES)
        for k, (ref, at) in enumerate(((side_ref, 0), (near_ref, 16), (near_ref, 32), (far_ref, 16))):
            ends_ref[k] = ref[at : at + 16, ends_cols]
    middles, rest = [rest[4 * k : 4 * k + 4] for k in range(2)], rest[8:]
    out_hbm, x_ref, order_ref, ghost_ref, grow_ref, ext_ref, strip_ref, sems, *work = rest
    levels, rows, cols = lay.levels, lay.rows, own_ref.shape[1]
    tiles, halves, fields, bands, span = lay.tiles, lay.halves, lay.fields, lay.bands, lay.span
    at_belt, at_across = lax.axis_index("belt"), lax.axis_index("across")
    first, last = at_across == 0, at_across == lax.axis_size("across") - 1
    ghost_at = ghost_tile_at(lay, first)
    rest_at = pl.multiple_of(jnp.where(first, SUB, 0), SUB)
    calm = pl.ds(rest_at, rows - SUB)
    left_end, split, right_start, right_end = plan
    early = [
        pltpu.make_async_copy(
            middles[0][0].at[:, :, calm, LANES:], out_hbm.at[:, :, calm, left_end:split], sems.at[0]
        ),
        pltpu.make_async_copy(
            middles[1][0].at[:, :, calm, : 2 * LANES], out_hbm.at[:, :, calm, split:right_start], sems.at[1]
        ),
    ]
    for copy in early:
        copy.start()
    even = lax.rem(at_belt, 2) == 0
    from_right = (lane_iota() // 8) % 2 == 1
    take_a = from_right == even

    def unpacked(a_ref, b_ref, groups):
        out = []
        for g in range(groups):
            column, half = LANES * (g // 2), slice(SUB * (g % 2), SUB * (g % 2) + SUB)
            a = a_ref(column).astype(F32)[half]
            b = b_ref(column).astype(F32)[half]
            out.append(jnp.where(take_a, a, b))
        return out

    def put_back(packed, index):
        return pltpu.roll(packed[index // SLOTS], (-(8 + 16 * (index % SLOTS))) % LANES, 1)

    ghost_ref[...] = jnp.zeros(ghost_ref.shape, F32)
    edge = jnp.where(first, 0, 1)
    lane_r = lax.broadcasted_iota(jnp.int32, (LANES, LANES), 0)
    lane_c = lax.broadcasted_iota(jnp.int32, (LANES, LANES), 1)
    backward = jnp.where(lane_r + lane_c == LANES - 1, 1.0, 0.0).astype(BF)
    blocks = [at_belt, lax.rem(at_belt + 1, n_belt), lax.rem(at_belt + n_belt - 1, n_belt)]
    peers = [peer_ref[edge, block] for block in blocks]
    own_rim = rims_ref[rim_slot(peers[0], at_belt, n_belt)]
    col_tiles = cols // LANES
    raw = [own_rim[:, LANES * t : LANES * (t + 1)] for t in range(col_tiles)]
    raw += [ends_ref[end_slot(peer, at_belt, n_belt)] for peer in peers[1:]]
    turned = jnp.dot(jnp.concatenate(raw, axis=0), backward, preferred_element_type=F32)

    def ghost_parts(block, plain, flipped):
        flip, turn = flip_ref[edge, block], turn_ref[edge, block]
        found = jnp.where(flip == 1, turned[16 * flipped : 16 * (flipped + 1)], raw[plain].astype(F32))
        p, q = found[0:levels], found[levels : 2 * levels]
        cosine = jnp.where(turn == 0, 1.0, jnp.where(turn == 2, -1.0, 0.0))
        sine_neg = jnp.where(turn == 1, -1.0, jnp.where(turn == 3, 1.0, 0.0))
        return cosine * p + sine_neg * q, cosine * q - sine_neg * p

    for t in range(col_tiles):
        for c, part in enumerate(ghost_parts(blocks[0], t, col_tiles - 1 - t)):
            ghost_ref[c, 0:levels, LANES * t : LANES * (t + 1)] = part
    after_tiles = ghost_parts(blocks[1], col_tiles, col_tiles)
    before_tiles = ghost_parts(blocks[2], col_tiles + 1, col_tiles + 1)
    lane_row = lax.broadcasted_iota(jnp.int32, (levels, LANES), 1)
    for c in range(2):
        both = jnp.where(lane_row < LANES // 2, after_tiles[c], before_tiles[c])
        ghost_ref[c, 0:levels, cols:] = both

    side_tiles = unpacked(
        lambda k: side_a_ref[:, k : k + LANES], lambda k: side_b_ref[:, k : k + LANES],
        -(-bands * tiles // SLOTS),
    )
    corners = [
        unpacked(
            lambda k, at=at: (corner_a_ref if relay else corner_a_ref.at[at])[:, k : k + LANES],
            lambda k, at=at: (corner_b_ref if relay else corner_b_ref.at[at])[:, k : k + LANES],
            -(-bands // SLOTS),
        )
        for at in range(halves)
    ]
    near_start, near_end = slice(0, 2 * LANES), slice(cols - 2 * LANES, cols)
    for part, place in ((near_start, slice(LANES, 3 * LANES)), (near_end, slice(3 * LANES, 5 * LANES))):
        for f in range(bands):
            base = lay.own_base(f)
            x_ref[base : base + rows, place] = own_ref[rows * f : rows * (f + 1), part]
    for f in range(bands):
        halo = jnp.concatenate([put_back(side_tiles, f * tiles + r) for r in range(tiles)], axis=0)
        x_ref[lay.own_base(f) : lay.own_base(f) + rows, 0:LANES] = halo.astype(BF)
    at_row = lax.broadcasted_iota(jnp.int32, (2 * span, 5 * LANES), 0)
    for f in range(0, bands, 2):
        body = bulk_ref[span * f : span * (f + 2)].astype(F32)
        halo = jnp.concatenate(
            [put_back(corners[at], f + k) for k in range(2) for at in range(halves)], axis=0
        )
        band = jnp.concatenate([halo, body[:, near_start], body[:, near_end]], axis=1)
        if f < fields:
            for k in range(2):
                c, lev = (f + k) // levels, (f + k) % levels
                row = ghost_ref[c, lev : lev + 1, :]
                row = jnp.concatenate([row[:, cols:], row[:, near_start], row[:, near_end]], axis=1)
                spot = jnp.where(first, span * (k + 1) - 1, jnp.where(last, span * k, -1))
                band = jnp.where(at_row == spot, row, band)
        x_ref[lay.band_base(f) : lay.band_base(f) + 2 * span] = band.astype(BF)

    half, size = WINDOW // 2, 5 * LANES

    def source_of(place):
        at_left = place + LANES - MARGIN
        at_right = place + size - (WINDOW - MARGIN)
        return jnp.where(place < half, at_left, jnp.where(at_right < size, at_right, at_right - size))

    fill_order(order_ref, source_of)

    sub = lax.broadcasted_iota(jnp.int32, (SUB, LANES), 0)
    spot = jnp.where(first, 0, SUB - 1)
    sign = jnp.where(first, -1.0, jnp.where(last, 1.0, 0.0))
    lift = jnp.where(sub == spot, sign, 0.0)
    values = []
    for k, (_, order, coef, met) in enumerate(middles):
        cols_k = slice(LANES * MIDDLES[k][0], LANES * (MIDDLES[k][0] + 4))
        rows_k = jnp.concatenate([ghost_ref[0, :, cols_k], ghost_ref[1, :, cols_k]], axis=0).astype(BF)
        found = jnp.dot(rows_k, order[:, 0:WINDOW], preferred_element_type=F32)
        for f in range(fields):
            c, lev = f // levels, f % levels
            row = found[SUB * c + lev : SUB * c + lev + 1]
            scale = [(1.0 - 2.0 * c) * lift * met[r] for r in range(3)]
            values.append([scale[r] * row[:, LANES * r : LANES * (r + 1)] for r in range(3)])
    inner_south, inner_north = sub < SUB - 1, sub > 0
    for _ in range(STEPS):
        updated = []
        for at, f in enumerate(values):
            coef, c = middles[at // fields][2], at % fields // levels
            right, left = east_of(f), west_of(f)
            updated.append(
                [
                    (coef[c, 0, r] * f[r] + coef[c, 1, r] * right[r] + coef[c, 2, r] * left[r])
                    + jnp.where(inner_south, coef[c, 3, r], 0.0) * pltpu.roll(f[r], SUB - 1, 0)
                    + jnp.where(inner_north, coef[c, 4, r], 0.0) * pltpu.roll(f[r], 1, 0)
                    for r in range(3)
                ]
            )
        values = updated
    for at, f in enumerate(values):
        for r in range(3):
            grow_ref[SUB * at : SUB * (at + 1), LANES * r : LANES * (r + 1)] = f[r]
    strips = []
    for k in range(2):
        grown = grow_ref[SUB * fields * k : SUB * fields * (k + 1)]
        hi = grown.astype(BF)
        parts = jnp.concatenate([hi, (grown - hi.astype(F32)).astype(BF)], axis=1)
        keep = MIDDLES[k][2]
        strips.append(back_to_natural(parts, middles[k][1], slice(LANES * keep, LANES * (keep + 3))))
    for f in range(fields):
        c, lev = f // levels, f % levels
        for k, part in ((0, slice(LANES, WINDOW)), (1, slice(0, 2 * LANES))):
            added = strips[k][SUB * f : SUB * (f + 1), part]
            strip_ref[c, lev, :, 2 * LANES * k : 2 * LANES * (k + 1)] = (
                middles[k][0][c, lev, pl.ds(ghost_at, SUB), part] + added
            )
    edge_rows = pl.ds(ghost_at, SUB)
    strip_copy = pltpu.make_async_copy(
        strip_ref, out_hbm.at[:, :, edge_rows, left_end:right_start], sems.at[2]
    )
    strip_copy.start()

    solve_window(lay, first, last, x_ref, order_ref, work)
    back = back_to_natural(work[-1][...], order_ref, slice(LANES, 5 * LANES))
    lane = lax.broadcasted_iota(jnp.int32, (rows, LANES), 1)
    lane_tile = lane[:SUB]
    low, high = MIDDLE_FROM - LANES, right_end - right_start
    for f in range(fields):
        c, lev = f // levels, f % levels
        mine = back[rows * f : rows * (f + 1)]
        ext_ref[c, lev, :, 0:LANES] = mine[:, 0:LANES]
        ext_ref[c, lev, :, 3 * LANES :] = mine[:, 3 * LANES :]
        one, two = slice(LANES, 2 * LANES), slice(2 * LANES, 3 * LANES)
        ext_ref[c, lev, :, one] = jnp.where(lane < low, mine[:, one], middles[0][0][c, lev, :, 0:LANES])
        ext_ref[c, lev, :, two] = jnp.where(lane >= high, mine[:, two], middles[1][0][c, lev, :, 2 * LANES :])
        for k, (place, mask, part) in enumerate(
            ((one, lane_tile >= low, slice(0, LANES)), (two, lane_tile < high, slice(2 * LANES, WINDOW)))
        ):
            added = strips[k][SUB * f : SUB * (f + 1), part]
            ext_ref[c, lev, edge_rows, place] = ext_ref[c, lev, edge_rows, place] + jnp.where(mask, added, 0.0)
    late = [
        pltpu.make_async_copy(ext_ref.at[:, :, :, : 2 * LANES], out_hbm.at[:, :, :, :left_end], sems.at[3]),
        pltpu.make_async_copy(ext_ref.at[:, :, :, 2 * LANES :], out_hbm.at[:, :, :, right_start:], sems.at[4]),
    ]
    for copy in late:
        copy.start()
    for copy in early + [strip_copy] + late:
        copy.wait()


def per_device(wind, metric, kappa, edge_peer, edge_flip, edge_turn):
    _, levels, rows, cols = wind.shape
    n_across, n_belt = lax.axis_size("across"), lax.axis_size("belt")
    halves = 1 if n_across == 2 else 2
    fields = 2 * levels
    bands = fields + 6
    corner_cols = LANES * (-(-bands // (2 * SLOTS)))
    side_cols = LANES * (-(-bands * (rows // SUB) // (2 * SLOTS)))
    ends_col = side_cols + corner_cols
    relay = halves == 1 and n_belt == 4 and ends_col + LANES <= cols

    vmem = pl.BlockSpec(memory_space=pltpu.VMEM)
    smem = pl.BlockSpec(memory_space=pltpu.SMEM)
    anywhere = pl.BlockSpec(memory_space=pl.ANY)
    lay = Rows(levels, rows, halves)
    height, span = lay.height, lay.span
    bulk, corner, rim, side, own, pick = pl.pallas_call(
        functools.partial(pack_kernel, halves, ends_col if relay else None),
        out_shape=[
            jax.ShapeDtypeStruct((halves, SUB * bands, cols), BF),
            jax.ShapeDtypeStruct((halves, 16, corner_cols), BF),
            jax.ShapeDtypeStruct((16, cols), BF),
            jax.ShapeDtypeStruct((16, cols), BF),
            jax.ShapeDtypeStruct((rows * bands, cols), BF),
            jax.ShapeDtypeStruct((16, cols), BF),
        ],
        in_specs=[anywhere] * 4,
        out_specs=[vmem] * 6,
        scratch_shapes=[
            pltpu.VMEM(wind.shape, BF),
            pltpu.VMEM(kappa.shape, F32),
            pltpu.VMEM(metric.shape, F32),
            pltpu.SMEM(edge_peer.shape, jnp.int32),
            pltpu.SemaphoreType.DMA((4,)),
        ],
        compiler_params=pltpu.CompilerParams(vmem_limit_bytes=PACK_LIMIT),
        name="pack",
    )(*(pltpu.with_memory_space_constraint(x, pltpu.HBM) for x in (wind, metric, kappa, edge_peer)))

    pairs_a = [(i, i ^ 1) for i in range(n_belt)]
    pairs_b = [(i, (i + 1) % n_belt if i % 2 else (i - 1) % n_belt) for i in range(n_belt)]
    if halves == 1:
        swap = [(0, 1), (1, 0)]
        bulk_in = lax.ppermute(bulk, "across", swap)
        corner_in = lax.ppermute(corner, "across", swap)
    else:
        onward = [(i, i + 1) for i in range(n_across - 1)]
        back = [(i + 1, i) for i in range(n_across - 1)]

        def both_ways(message):
            return jnp.stack(
                [
                    lax.ppermute(message[1], "across", back),
                    lax.ppermute(message[0], "across", onward),
                ]
            )

        corner_in, bulk_in = both_ways(corner), both_ways(bulk)
    bulk_in = bulk_in.reshape(halves, bands, SUB, cols).swapaxes(0, 1).reshape(bands * span, cols)

    def middle(k, after):
        tile, offset, keep = MIDDLES[k]
        shapes = [
            jax.ShapeDtypeStruct((2, levels, rows, WINDOW), F32),
            jax.ShapeDtypeStruct((4 * LANES, 2 * WINDOW), BF),
            jax.ShapeDtypeStruct((2, 5, 3, SUB, LANES), F32),
            jax.ShapeDtypeStruct((3, SUB, LANES), F32),
        ]
        return pl.pallas_call(
            functools.partial(middle_kernel, lay, tile, offset, keep),
            out_shape=shapes,
            in_specs=[vmem] * 2 + [anywhere],
            out_specs=[vmem] * len(shapes),
            scratch_shapes=[pltpu.VMEM((height * bands, 4 * LANES), BF)] + work_shapes(lay),
            compiler_params=pltpu.CompilerParams(vmem_limit_bytes=MID_LIMIT),
            cost_estimate=pl.CostEstimate(flops=2_000_000_000, bytes_accessed=2_000_000, transcendentals=0),
            name="middle",
        )(own, bulk_in, after)

    if relay:
        spot = slice(side_cols, ends_col)
        side = jnp.concatenate([side[:, :side_cols], corner_in[0], side[:, ends_col:]], axis=1)
        far = lax.ppermute(jnp.concatenate([rim, side]), "belt", [(i, i ^ 2) for i in range(n_belt)])
        rim_c, side_c = far[:16], far[16:]
        chosen = jnp.where(pick > 0, rim, rim_c)
        near = lax.ppermute(jnp.concatenate([chosen, side, side_c]), "belt", pairs_a)
        middle_0 = middle(0, corner_in)
        middle_1 = middle(1, corner_in)
        messages = [rim, side, far, near]
    else:
        side_a = lax.ppermute(side, "belt", pairs_a)
        side_b = lax.ppermute(side, "belt", pairs_b)
        corner_a = lax.ppermute(corner_in, "belt", pairs_a)
        corner_b = lax.ppermute(corner_in, "belt", pairs_b)
        rims = lax.all_gather(rim, "belt")
        if n_belt == 4:
            at_belt = lax.axis_index("belt")
            rims, ends = (rims[at_belt ^ jnp.array([0, 1, 2])], rims[at_belt ^ jnp.array([0, 1, 3, 2])])
        else:
            ends = rims
        ends = jnp.concatenate([ends[..., : LANES // 2], ends[..., cols - LANES // 2 :]], axis=-1)

        messages = [side_a, side_b, corner_a, corner_b, rims, ends]
        middle_0, middle_1 = middle(0, corner_in), middle(1, corner_in)
    operands = [own, bulk_in, *messages, *middle_0, *middle_1]
    own_rims = [pltpu.VMEM((3, 16, cols), BF), pltpu.VMEM((4, 16, LANES), BF)] if relay else []
    plan = (2 * LANES, cols // 2, cols - 2 * LANES, MIDDLE_TO)
    return pl.pallas_call(
        functools.partial(edge_kernel, lay, n_belt, (side_cols, ends_col) if relay else None, plan),
        out_shape=jax.ShapeDtypeStruct((2, levels, rows, cols), F32),
        in_specs=[smem] * 3 + [vmem] * len(operands),
        out_specs=anywhere,
        scratch_shapes=[
            pltpu.VMEM((height * bands, 5 * LANES), BF),
            pltpu.VMEM((5 * LANES, 2 * WINDOW), BF),
            pltpu.VMEM((2, SUB, cols + LANES), F32),
            pltpu.VMEM((2 * fields * SUB, WINDOW), F32),
            pltpu.VMEM((2, levels, rows, 4 * LANES), F32),
            pltpu.VMEM((2, levels, SUB, 4 * LANES), F32),
            pltpu.SemaphoreType.DMA((5,)),
        ]
        + work_shapes(lay)
        + own_rims,
        compiler_params=pltpu.CompilerParams(vmem_limit_bytes=EDGE_LIMIT),
        name="edges",
    )(edge_peer, edge_flip, edge_turn, *operands)


def solution(mesh):
    return jax.shard_map(
        per_device,
        mesh=mesh,
        in_specs=(
            P(None, ("members", "lev"), "across", "belt"),
            P("across", "belt"),
            P(None, "across", "belt"),
            P(),
            P(),
            P(),
        ),
        out_specs=P(None, ("members", "lev"), "across", "belt"),
        check_vma=False,
    )
```

time: 123 us -> 25.8 us (0.21)
  other arithmetic: 29.1 us -> 0.03 us
  local copies, waits for them, and re-layouts: 21.9 us -> 0.02 us
  waiting for transfers between devices: 24.2 us -> 3.79 us
  starting transfers between devices: 25.1 us -> 8.19 us
  blocking collectives: 13.9 us -> 0 us
  Pallas kernels: 0 us -> 13.6 us
  between operations: 8.14 us -> 0.08 us
    ppermute x16 -> x4, waiting for transfers between devices: 24.2 us -> 3.79 us  [the longest x1 2.24 us: per_device(): lax.ppermute(jnp.concatenate([rim, side]), 'belt', [(i, i ^ 2) for i in r...]
    ppermute x16 -> x4, starting transfers between devices: 25.1 us -> 8.19 us  [the longest x1 3.13 us: per_device(): lax.ppermute(jnp.concatenate([rim, side]), 'belt', [(i, i ^ 2) for i in r...]
    sub x6 -> x0, other arithmetic: 15.4 us -> none  [advance(): field_pad[:, :, 1:-1, 1:-1] + belt_flux[:, :, 1:-1, 1:]]
    all_gather x1 -> x0, blocking collectives: 13.9 us -> none  [per_device(): gathered = lax.all_gather(rims, 'belt', axis=3, tiled=True)]
    pallas_call x0 -> x4, Pallas kernels: none -> 13.6 us  [the longest x1 6.04 us: per_device(): pl.pallas_call(functools.partial(edge_kernel, lay, n_belt, (side_cols, en...]
    mul x17 -> x0, other arithmetic: 9.63 us -> none  [the longest x6 5.11 us: advance(): belt_part[:, None] * (field_pad[:, :, :, 1:] - field_pad[:, :, :, :-1])]
    concatenate x4 -> x0, local copies, waits for them, and re-layouts: 8.63 us -> none  [padded_2(): array = jnp.concatenate([before, array, after], axis=dim)]
    slice x13 -> x2, local copies, waits for them, and re-layouts: 2.91 us -> 0.01 us  [the longest x1 0.01 us: per_device(): side[:, ends_col:]]
  transfers between devices with their start and end apart: 16 -> 4, of which waited for: 9 -> 2; matrix products, arithmetic and copies ran while one was open for 13% -> 0% of each run, Pallas kernels for 0% -> 23%
where the time goes in v2:
time: 25.8 us; the launch traced here: 25.7 us
  Pallas kernels  13.6 us (53%)
  starting transfers between devices  8.19 us (32%)
  waiting for transfers between devices  3.79 us (15%)
    pallas_call x1, Pallas kernels, per_device(): pl.pallas_call(functools.partial(edge_kernel, lay, n_belt, (side_cols, en...  6.04 us
    pallas_call x2, Pallas kernels, middle(): pl.pallas_call(functools.partial(middle_kernel, lay, tile, offset, keep),...  6.03 us
    ppermute x1, starting transfers between devices, per_device(): lax.ppermute(jnp.concatenate([rim, side]), 'belt', [(i, i ^ 2) for i in r...  3.13 us
    ppermute x1, starting transfers between devices, per_device(): corner_in = lax.ppermute(corner, 'across', swap)  3 us
    ppermute x1, waiting for transfers between devices, per_device(): lax.ppermute(jnp.concatenate([rim, side]), 'belt', [(i, i ^ 2) for i in r...  2.24 us
    ppermute x1, starting transfers between devices, per_device(): lax.ppermute(jnp.concatenate([chosen, side, side_c]), 'belt', pairs_a)  1.97 us
    ppermute x1, waiting for transfers between devices, per_device(): corner_in = lax.ppermute(corner, 'across', swap)  1.54 us
    pallas_call x1, Pallas kernels, per_device(): pl.pallas_call(functools.partial(pack_kernel, halves, ends_col if relay e...  1.51 us
  transfers between devices with their start and end apart: 4, of which 2 were waited for; matrix products, arithmetic and copies ran while one was open for 0% of the time, Pallas kernels for 23%

profile of v2, /device:TPU:0, one launch (start us, length us, event | category | flops | bytes accessed | tf_op | source)
XLA Modules:
  0.0 25.7 jit_solution(16523478529476877683)
XLA Ops:
  0.0 1.5 %pack.1 = (bf16[1,144,1024]{2,1,0:T(8,128)(2,1)S(1)}, bf16[1,16,256]{2,1,0:T(8,128)(2,1)S(1)}, bf16[16,1024]{1,0:T(8,128)(2,1)S(1)}, bf16[16,1024]{1,0:T(8,128)(...) custom-call(bf16[2,6,32,1024]{3,2,1,0:T(8,128)(2,1)} %wind_hbm.1, f32[32,1024]{1,0:T(8,128)} %metric_hbm.1, ...), custom_call_target="tpu_custom_call" | custom-call | tf_op jit(solution)/shard_map/pack/pallas_call | solution.py:578
  1.5 3.0 %collective-permute-start.1 = (bf16[1,16,256]{2,1,0:T(8,128)(2,1)S(1)}, bf16[1,16,256]{2,1,0:T(8,128)(2,1)S(1)}, u32[]{:S(2)}, u32[]{:S(2)}) collective-permute-start(bf16[1,16,256]{2,1,0:T(8,128)(2,1)S(1)} %get-tuple-element.23), channel_id=1, source_target_pairs={{0,2},{2,0},{1,3},{3,1},{4,6},{6,4},{5,7},{7,5},{8,10},{10,8},{9,1... | collective-permute-start | bytes 24584 | tf_op jit(solution)/shard_map/ppermute | solution.py:606
  4.5 0.1 collective-permute-start
  4.6 1.5 %collective-permute-done.1.after_ref = bf16[1,16,256]{2,1,0:T(8,128)(2,1)S(1)} collective-permute-done((bf16[1,16,256]{2,1,0:T(8,128)(2,1)S(1)}, bf16[1,16,256]{2,1,0:T(8,128)(2,1)S(1)}, u32[]{:S(2)}, u32[]{:S(2)}) %collective-permute-start.1) | collective-permute-done | bytes 8224 | tf_op jit(solution)/shard_map/ppermute | solution.py:606
  6.2 3.1 %collective-permute-start.2 = (bf16[32,1024]{1,0:T(8,128)(2,1)S(1)}, bf16[32,1024]{1,0:T(8,128)(2,1)S(1)}, u32[]{:S(2)}, u32[]{:S(2)}) collective-permute-start(bf16[32,1024]{1,0:T(8,128)(2,1)S(1)} %maximum_maximum_fusion), channel_id=1, source_target_pairs={{0,8},{4,12},{8,0},{12,4},{1,9},{5,13},{9,1},{13,5},{2,10},{6,14},... | collective-permute-start | bytes 196616 | tf_op jit(solution)/shard_map/ppermute | solution.py:644
  9.3 2.2 %collective-permute-done.2.rest_2_ = bf16[32,1024]{1,0:T(8,128)(2,1)S(1)} collective-permute-done((bf16[32,1024]{1,0:T(8,128)(2,1)S(1)}, bf16[32,1024]{1,0:T(8,128)(2,1)S(1)}, u32[]{:S(2)}, u32[]{:S(2)}) %collective-permute-start.2) | collective-permute-done | bytes 65568 | tf_op jit(solution)/shard_map/ppermute | solution.py:644
  11.6 2.0 %collective-permute-start.3 = (bf16[48,1024]{1,0:T(8,128)(2,1)S(1)}, bf16[48,1024]{1,0:T(8,128)(2,1)S(1)}, u32[]{:S(2)}, u32[]{:S(2)}) collective-permute-start(bf16[48,1024]{1,0:T(8,128)(2,1)S(1)} %pad_maximum_fusion), channel_id=1, source_target_pairs={{0,4},{4,0},{8,12},{12,8},{1,5},{5,1},{9,13},{13,9},{2,6},{6,2},{1... | collective-permute-start | bytes 294920 | tf_op jit(solution)/shard_map/ppermute | solution.py:647
  13.5 0.0 collective-permute-done
  13.5 3.0 %middle.3 = (f32[2,6,32,384]{3,2,1,0:T(8,128)S(1)}, bf16[512,768]{1,0:T(8,128)(2,1)S(1)}, f32[2,5,3,8,128]{4,3,2,1,0:T(8,128)S(1)}, f32[3,8,128]{2,1,0:T(8,128)S(1)}) custom-call(bf16[576,1024]{1,0:T(8,128)(2,1)S(1)} %get-tuple-element.19.own_ref, bf16[144,1024]{1,0:T(8,128)(2,1)S(1)} %bitcast.2, bf16[1,16,256]{2,1,0:T(8,128)(2,1)S(1)} %collective-permute-done.1.after_ref), custom_call_target="tpu_custom_call" | custom-call | flops 2000000000 | bytes 2000000 | tf_op jit(solution)/shard_map/middle/pallas_call | solution.py:630
  16.6 0.0 copy-start
  16.6 0.0 copy-start.1
  16.6 0.0 copy-start.2
  16.6 3.0 %middle.2 = (f32[2,6,32,384]{3,2,1,0:T(8,128)S(1)}, bf16[512,768]{1,0:T(8,128)(2,1)S(1)}, f32[2,5,3,8,128]{4,3,2,1,0:T(8,128)S(1)}, f32[3,8,128]{2,1,0:T(8,128)S(1)}) custom-call(bf16[576,1024]{1,0:T(8,128)(2,1)S(1)} %get-tuple-element.19.own_ref, bf16[144,1024]{1,0:T(8,128)(2,1)S(1)} %bitcast.3, bf16[1,16,256]{2,1,0:T(8,128)(2,1)S(1)} %collective-permute-done.1.after_ref), custom_call_target="tpu_custom_call" | custom-call | flops 2000000000 | bytes 2000000 | tf_op jit(solution)/shard_map/middle/pallas_call | solution.py:630
  19.6 0.0 collective-permute-done.3.rest_3_
  19.6 0.0 copy-done
  19.6 0.0 copy-done.1
  19.6 0.0 copy-done.2
  19.6 6.0 %edges.1 = f32[2,6,32,1024]{3,2,1,0:T(8,128)} custom-call(s32[2,4]{1,0:T(2,128)S(1)} %copy-done, s32[2,4]{1,0:T(2,128)S(1)} %copy-done.1, s32[2,4]{1,0:T(2,128)S(1)} %copy-done.2, bf16[576,1024]{1,0:T(8,128)(2,1)S(1)} %get-tuple-element.19.own_ref, bf16[144,1024]{1,0:T(8,128)(2,1)S(1)} %bitcast.4, bf16[16,1024]{1,0:T(8,128)(2,1)S(1)} %get-tuple-element.21.rest_0_, ...), custom_call_target="tpu_custom_call" | custom-call | tf_op jit(solution)/shard_map/edges/pallas_call | solution.py:669
  (6 shorter events, 0.0 us)
Async XLA Ops:
  1.5 4.6 %collective-permute-start.1 = (bf16[1,16,256]{2,1,0:T(8,128)(2,1)S(1)}, bf16[1,16,256]{2,1,0:T(8,128)(2,1)S(1)}, u32[]{:S(2)}, u32[]{:S(2)}) collective-permute-start(bf16[1,16,256]{2,1,0:T(8,128)(2,1)S(1)} %get-tuple-element.23), channel_id=1, source_target_pairs={{0,2},{2,0},{1,3},{3,1},{4,6},{6,4},{5,7},{7,5},{8,10},{10,8},{9,1... | collective-permute-start | bytes 24584 | tf_op jit(solution)/shard_map/ppermute | solution.py:606
  4.5 9.0 %collective-permute-start = (bf16[1,144,1024]{2,1,0:T(8,128)(2,1)S(1)}, bf16[1,144,1024]{2,1,0:T(8,128)(2,1)S(1)}, u32[]{:S(2)}, u32[]{:S(2)}) collective-permute-start(bf16[1,144,1024]{2,1,0:T(8,128)(2,1)S(1)} %get-tuple-element.20), channel_id=1, source_target_pairs={{0,2},{2,0},{1,3},{3,1},{4,6},{6,4},{5,7},{7,5},{8,10},{10,8},{9,1... | collective-permute-start | bytes 884744 | tf_op jit(solution)/shard_map/ppermute | solution.py:605
  6.2 5.4 %collective-permute-start.2 = (bf16[32,1024]{1,0:T(8,128)(2,1)S(1)}, bf16[32,1024]{1,0:T(8,128)(2,1)S(1)}, u32[]{:S(2)}, u32[]{:S(2)}) collective-permute-start(bf16[32,1024]{1,0:T(8,128)(2,1)S(1)} %maximum_maximum_fusion), channel_id=1, source_target_pairs={{0,8},{4,12},{8,0},{12,4},{1,9},{5,13},{9,1},{13,5},{2,10},{6,14},... | collective-permute-start | bytes 196616 | tf_op jit(solution)/shard_map/ppermute | solution.py:644
  11.6 8.0 %collective-permute-start.3 = (bf16[48,1024]{1,0:T(8,128)(2,1)S(1)}, bf16[48,1024]{1,0:T(8,128)(2,1)S(1)}, u32[]{:S(2)}, u32[]{:S(2)}) collective-permute-start(bf16[48,1024]{1,0:T(8,128)(2,1)S(1)} %pad_maximum_fusion), channel_id=1, source_target_pairs={{0,4},{4,0},{8,12},{12,8},{1,5},{5,1},{9,13},{13,9},{2,6},{6,2},{1... | collective-permute-start | bytes 294920 | tf_op jit(solution)/shard_map/ppermute | solution.py:647
  16.6 3.1 %copy-start = (s32[2,4]{1,0:T(2,128)S(1)}, s32[2,4]{1,0:T(2,128)}, u32[]{:S(2)}) copy-start(s32[2,4]{1,0:T(2,128)} %peer_ref.1) | copy-start | bytes 100
  16.6 3.1 %copy-start.1 = (s32[2,4]{1,0:T(2,128)S(1)}, s32[2,4]{1,0:T(2,128)}, u32[]{:S(2)}) copy-start(s32[2,4]{1,0:T(2,128)} %flip_ref.1) | copy-start | bytes 100
  16.6 3.1 %copy-start.2 = (s32[2,4]{1,0:T(2,128)S(1)}, s32[2,4]{1,0:T(2,128)}, u32[]{:S(2)}) copy-start(s32[2,4]{1,0:T(2,128)} %turn_ref.1) | copy-start | bytes 100

commit v3 on v2

--- a/solution.py
+++ b/solution.py
@@ -66,9 +66,23 @@
     return [jnp.concatenate(packed[i : i + 2], axis=0).astype(BF) for i in range(0, len(packed), 2)]
 
 
+def bulk_place(t):
+    if 1 <= t <= 4:
+        return 0, LANES * (t - 1)
+    return 1, 0 if t == 0 else LANES * (t - 4)
+
+
+def bulk_tiles(refs, at, count, tiles):
+    parts = []
+    for t in tiles:
+        part, col = bulk_place(t)
+        parts.append(refs[part][at : at + count, col : col + LANES])
+    return jnp.concatenate(parts, axis=1)
+
+
 def pack_kernel(
     halves, ends_col, wind_hbm, metric_hbm, kappa_hbm, peer_hbm,
-    bulk_ref, corner_ref, rim_ref, side_ref, own_ref, pick_ref, *scratch
+    bulk_0_ref, bulk_1_ref, corner_ref, rim_ref, side_ref, own_ref, pick_ref, *scratch
 ):
     wind_ref, kappa_ref, metric_ref, peer_ref, sems = scratch
     levels, rows, cols = wind_hbm.shape[1:]
@@ -104,7 +118,11 @@
     for k in range(halves):
         for i in range(0, len(pieces[k]), 2):
             both = jnp.concatenate([pieces[k][i], pieces[k][i + 1]], axis=0)
-            bulk_ref[k, SUB * i : SUB * (i + 2)] = both.astype(BF)
+            both = both.astype(BF)
+            for t in range(cols // LANES):
+                part, at = bulk_place(t)
+                ref = (bulk_0_ref, bulk_1_ref)[part]
+                ref[k, SUB * i : SUB * (i + 2), at : at + LANES] = both[:, LANES * t : LANES * (t + 1)]
         for i, tile in enumerate(compact_rows([edge_tile(p) for p in pieces[k]])):
             corner_ref[k, :, LANES * i : LANES * (i + 1)] = tile
     rim = jnp.concatenate(rim_rows + [jnp.zeros((16 - len(rim_rows), cols), F32)], axis=0)
@@ -320,10 +338,10 @@
 
 
 def middle_kernel(
-    lay, tile, offset, keep, own_ref, bulk_ref, after_ref,
-    out_ref, order_ref, coef_out, met_out, x_ref, *work,
+    lay, tile, offset, keep, own_ref, bulk_0_ref, bulk_1_ref, pick_ref,
+    out_ref, order_ref, coef_out, met_out, pick_out, x_ref, *work,
 ):
-    del after_ref
+    pick_out[...] = pick_ref[...]
     first, last = lax.axis_index("across") == 0, lax.axis_index("across") == lax.axis_size("across") - 1
     cols = slice(LANES * tile, LANES * (tile + 4))
     fill_order(order_ref, lambda place: place + offset)
@@ -333,7 +351,7 @@
     span = lay.span
     at_row = lax.broadcasted_iota(jnp.int32, (2 * span, 4 * LANES), 0)
     for f in range(0, lay.bands, 2):
-        band = bulk_ref[span * f : span * (f + 2), cols]
+        band = bulk_tiles((bulk_0_ref, bulk_1_ref), span * f, 2 * span, range(tile, tile + 4))
         if f < lay.fields:
             band = band.astype(F32)
             for k in range(2):
@@ -351,7 +369,7 @@
     met_out[...] = work[2][:, pl.ds(at, SUB)]
 
 
-def edge_kernel(lay, n_belt, relay, plan, peer_ref, flip_ref, turn_ref, own_ref, bulk_ref, *rest):
+def edge_kernel(lay, n_belt, relay, plan, peer_ref, flip_ref, turn_ref, own_ref, bulk_0_ref, bulk_1_ref, *rest):
     if relay is None:
         side_a_ref, side_b_ref, corner_a_ref, corner_b_ref, rims_ref, ends_ref, *rest = rest
     else:
@@ -456,11 +474,14 @@
         x_ref[lay.own_base(f) : lay.own_base(f) + rows, 0:LANES] = halo.astype(BF)
     at_row = lax.broadcasted_iota(jnp.int32, (2 * span, 5 * LANES), 0)
     for f in range(0, bands, 2):
-        body = bulk_ref[span * f : span * (f + 2)].astype(F32)
+        col_tiles = cols // LANES
+        body = bulk_tiles(
+            (bulk_0_ref, bulk_1_ref), span * f, 2 * span, (0, 1, col_tiles - 2, col_tiles - 1)
+        ).astype(F32)
         halo = jnp.concatenate(
             [put_back(corners[at], f + k) for k in range(2) for at in range(halves)], axis=0
         )
-        band = jnp.concatenate([halo, body[:, near_start], body[:, near_end]], axis=1)
+        band = jnp.concatenate([halo, body], axis=1)
         if f < fields:
             for k in range(2):
                 c, lev = (f + k) // levels, (f + k) % levels
@@ -575,10 +596,11 @@
     anywhere = pl.BlockSpec(memory_space=pl.ANY)
     lay = Rows(levels, rows, halves)
     height, span = lay.height, lay.span
-    bulk, corner, rim, side, own, pick = pl.pallas_call(
+    bulk_0, bulk_1, corner, rim, side, own, pick = pl.pallas_call(
         functools.partial(pack_kernel, halves, ends_col if relay else None),
         out_shape=[
-            jax.ShapeDtypeStruct((halves, SUB * bands, cols), BF),
+            jax.ShapeDtypeStruct((halves, SUB * bands, 4 * LANES), BF),
+            jax.ShapeDtypeStruct((halves, SUB * bands, cols - 4 * LANES), BF),
             jax.ShapeDtypeStruct((halves, 16, corner_cols), BF),
             jax.ShapeDtypeStruct((16, cols), BF),
             jax.ShapeDtypeStruct((16, cols), BF),
@@ -586,7 +608,7 @@
             jax.ShapeDtypeStruct((16, cols), BF),
         ],
         in_specs=[anywhere] * 4,
-        out_specs=[vmem] * 6,
+        out_specs=[vmem] * 7,
         scratch_shapes=[
             pltpu.VMEM(wind.shape, BF),
             pltpu.VMEM(kappa.shape, F32),
@@ -602,8 +624,7 @@
     pairs_b = [(i, (i + 1) % n_belt if i % 2 else (i - 1) % n_belt) for i in range(n_belt)]
     if halves == 1:
         swap = [(0, 1), (1, 0)]
-        bulk_in = lax.ppermute(bulk, "across", swap)
-        corner_in = lax.ppermute(corner, "across", swap)
+        bulk_0, bulk_1, corner_in = (lax.ppermute(x, "across", swap) for x in (bulk_0, bulk_1, corner))
     else:
         onward = [(i, i + 1) for i in range(n_across - 1)]
         back = [(i + 1, i) for i in range(n_across - 1)]
@@ -616,37 +637,42 @@
                 ]
             )
 
-        corner_in, bulk_in = both_ways(corner), both_ways(bulk)
-    bulk_in = bulk_in.reshape(halves, bands, SUB, cols).swapaxes(0, 1).reshape(bands * span, cols)
-
-    def middle(k, after):
+        bulk_0, bulk_1, corner_in = both_ways(bulk_0), both_ways(bulk_1), both_ways(corner)
+    bulk_0, bulk_1 = (
+        x.reshape(halves, bands, SUB, x.shape[-1]).swapaxes(0, 1).reshape(bands * span, x.shape[-1])
+        for x in (bulk_0, bulk_1)
+    )
+
+    def middle(k, pick):
         tile, offset, keep = MIDDLES[k]
+        inputs = (own, bulk_0, bulk_0 if k == 0 else bulk_1, pick)
         shapes = [
             jax.ShapeDtypeStruct((2, levels, rows, WINDOW), F32),
             jax.ShapeDtypeStruct((4 * LANES, 2 * WINDOW), BF),
             jax.ShapeDtypeStruct((2, 5, 3, SUB, LANES), F32),
             jax.ShapeDtypeStruct((3, SUB, LANES), F32),
+            jax.ShapeDtypeStruct(pick.shape, BF),
         ]
         return pl.pallas_call(
             functools.partial(middle_kernel, lay, tile, offset, keep),
             out_shape=shapes,
-            in_specs=[vmem] * 2 + [anywhere],
+            in_specs=[vmem] * len(inputs),
             out_specs=[vmem] * len(shapes),
             scratch_shapes=[pltpu.VMEM((height * bands, 4 * LANES), BF)] + work_shapes(lay),
             compiler_params=pltpu.CompilerParams(vmem_limit_bytes=MID_LIMIT),
             cost_estimate=pl.CostEstimate(flops=2_000_000_000, bytes_accessed=2_000_000, transcendentals=0),
             name="middle",
-        )(own, bulk_in, after)
+        )(*inputs)
 
     if relay:
         spot = slice(side_cols, ends_col)
         side = jnp.concatenate([side[:, :side_cols], corner_in[0], side[:, ends_col:]], axis=1)
+        *middle_0, pick = middle(0, pick)
         far = lax.ppermute(jnp.concatenate([rim, side]), "belt", [(i, i ^ 2) for i in range(n_belt)])
         rim_c, side_c = far[:16], far[16:]
         chosen = jnp.where(pick > 0, rim, rim_c)
         near = lax.ppermute(jnp.concatenate([chosen, side, side_c]), "belt", pairs_a)
-        middle_0 = middle(0, corner_in)
-        middle_1 = middle(1, corner_in)
+        *middle_1, _ = middle(1, pick)
         messages = [rim, side, far, near]
     else:
         side_a = lax.ppermute(side, "belt", pairs_a)
@@ -662,8 +688,8 @@
         ends = jnp.concatenate([ends[..., : LANES // 2], ends[..., cols - LANES // 2 :]], axis=-1)
 
         messages = [side_a, side_b, corner_a, corner_b, rims, ends]
-        middle_0, middle_1 = middle(0, corner_in), middle(1, corner_in)
-    operands = [own, bulk_in, *messages, *middle_0, *middle_1]
+        (*middle_0, _), (*middle_1, _) = middle(0, pick), middle(1, pick)
+    operands = [own, bulk_0, bulk_1, *messages, *middle_0, *middle_1]
     own_rims = [pltpu.VMEM((3, 16, cols), BF), pltpu.VMEM((4, 16, LANES), BF)] if relay else []
     plan = (2 * LANES, cols // 2, cols - 2 * LANES, MIDDLE_TO)
     return pl.pallas_call(

time: 25.8 us -> 25.4 us (0.984)
  waiting for transfers between devices: 3.79 us -> 1.98 us
  starting transfers between devices: 8.19 us -> 9.41 us
    ppermute x1, waiting for transfers between devices: 2.24 us -> 0.01 us  [per_device(): lax.ppermute(jnp.concatenate([rim, side]), 'belt', [(i, i ^ 2) for i in r...]
    ppermute x2 -> x3, starting transfers between devices: 3.08 us -> 5.03 us  [per_device(): lax.ppermute(x, 'across', swap)]
    ppermute x2 -> x3, waiting for transfers between devices: 1.55 us -> 1.98 us  [per_device(): lax.ppermute(x, 'across', swap)]
    ppermute x1, starting transfers between devices: 3.13 us -> 2.74 us  [per_device(): lax.ppermute(jnp.concatenate([rim, side]), 'belt', [(i, i ^ 2) for i in r...]
    ppermute x1, starting transfers between devices: 1.97 us -> 1.64 us  [per_device(): lax.ppermute(jnp.concatenate([chosen, side, side_c]), 'belt', pairs_a)]
  transfers between devices with their start and end apart: 4 -> 5, of which waited for: 2 -> 1; matrix products, arithmetic and copies ran while one was open for 0% -> 0% of each run, Pallas kernels for 23% -> 25%
where the time goes in v3:
time: 25.4 us; the launch traced here: 25.3 us
  Pallas kernels  13.8 us (54%)
  starting transfers between devices  9.41 us (37%)
  waiting for transfers between devices  1.98 us (8%)
    pallas_call x2, Pallas kernels, middle(): pl.pallas_call(functools.partial(middle_kernel, lay, tile, offset, keep),...  6.24 us
    pallas_call x1, Pallas kernels, per_device(): pl.pallas_call(functools.partial(edge_kernel, lay, n_belt, (side_cols, en...  6.02 us
    ppermute x3, starting transfers between devices, per_device(): lax.ppermute(x, 'across', swap)  5.03 us
    ppermute x1, starting transfers between devices, per_device(): lax.ppermute(jnp.concatenate([rim, side]), 'belt', [(i, i ^ 2) for i in r...  2.74 us
    ppermute x3, waiting for transfers between devices, per_device(): lax.ppermute(x, 'across', swap)  1.98 us
    ppermute x1, starting transfers between devices, per_device(): lax.ppermute(jnp.concatenate([chosen, side, side_c]), 'belt', pairs_a)  1.64 us
    pallas_call x1, Pallas kernels, per_device(): pl.pallas_call(functools.partial(pack_kernel, halves, ends_col if relay e...  1.52 us
  transfers between devices with their start and end apart: 5, of which 1 were waited for; matrix products, arithmetic and copies ran while one was open for 0% of the time, Pallas kernels for 25%

profile of v3, /device:TPU:0, one launch (start us, length us, event | category | flops | bytes accessed | tf_op | source)
XLA Modules:
  0.0 25.3 jit_solution(5293381506179534836)
XLA Ops:
  0.0 1.5 %pack.1 = (bf16[1,144,512]{2,1,0:T(8,128)(2,1)S(1)}, bf16[1,144,512]{2,1,0:T(8,128)(2,1)S(1)}, bf16[1,16,256]{2,1,0:T(8,128)(2,1)S(1)}, bf16[16,1024]{1,0:T(8,12...) custom-call(bf16[2,6,32,1024]{3,2,1,0:T(8,128)(2,1)} %wind_hbm.1, ...), custom_call_target="tpu_custom_call" | custom-call | tf_op jit(solution)/shard_map/pack/pallas_call | solution.py:599
  1.5 3.0 %collective-permute-start.2 = (bf16[1,16,256]{2,1,0:T(8,128)(2,1)S(1)}, bf16[1,16,256]{2,1,0:T(8,128)(2,1)S(1)}, u32[]{:S(2)}, u32[]{:S(2)}) collective-permute-start(bf16[1,16,256]{2,1,0:T(8,128)(2,1)S(1)} %get-tuple-element.26), channel_id=1, source_target_pairs={{0,2},{2,0},{1,3},{3,1},{4,6},{6,4},{5,7},{7,5},{8,10},{10,8},{9,1... | collective-permute-start | bytes 24584 | tf_op jit(solution)/shard_map/ppermute | solution.py:627
  4.5 0.1 collective-permute-start
  4.6 1.9 %collective-permute-start.1 = (bf16[1,144,512]{2,1,0:T(8,128)(2,1)S(1)}, bf16[1,144,512]{2,1,0:T(8,128)(2,1)S(1)}, u32[]{:S(2)}, u32[]{:S(2)}) collective-permute-start(bf16[1,144,512]{2,1,0:T(8,128)(2,1)S(1)} %get-tuple-element.23), channel_id=1, source_target_pairs={{0,2},{2,0},{1,3},{3,1},{4,6},{6,4},{5,7},{7,5},{8,10},{10,8},{9,1... | collective-permute-start | bytes 442376 | tf_op jit(solution)/shard_map/ppermute | solution.py:627
  6.6 0.0 collective-permute-done.2
  6.6 2.7 %collective-permute-start.3 = (bf16[32,1024]{1,0:T(8,128)(2,1)S(1)}, bf16[32,1024]{1,0:T(8,128)(2,1)S(1)}, u32[]{:S(2)}, u32[]{:S(2)}) collective-permute-start(bf16[32,1024]{1,0:T(8,128)(2,1)S(1)} %maximum_maximum_fusion), channel_id=1, source_target_pairs={{0,8},{4,12},{8,0},{12,4},{1,9},{5,13},{9,1},{13,5},{2,10},{6,14},... | collective-permute-start | bytes 196616 | tf_op jit(solution)/shard_map/ppermute | solution.py:671
  9.3 2.0 %collective-permute-done = bf16[1,144,512]{2,1,0:T(8,128)(2,1)S(1)} collective-permute-done((bf16[1,144,512]{2,1,0:T(8,128)(2,1)S(1)}, bf16[1,144,512]{2,1,0:T(8,128)(2,1)S(1)}, u32[]{:S(2)}, u32[]{:S(2)}) %collective-permute-start) | collective-permute-done | bytes 147488 | tf_op jit(solution)/shard_map/ppermute | solution.py:627
  11.3 3.0 %middle.2 = (f32[2,6,32,384]{3,2,1,0:T(8,128)S(1)}, bf16[512,768]{1,0:T(8,128)(2,1)S(1)}, f32[2,5,3,8,128]{4,3,2,1,0:T(8,128)S(1)}, f32[3,8,128]{2,1,0:T(8,128)S(1)}, bf16[16,1024]{1,0:T(8,128)(2,1)S(1)}) custom-call(bf16[576,1024]{1,0:T(8,128)(2,1)S(1)} %get-tuple-element.21.own_ref, bf16[144,512]{1,0:T(8,128)(2,1)S(1)} %bitcast.3, ...), custom_call_target="tpu_custom_call" | custom-call | flops 2000000000 | bytes 2000000 | tf_op jit(solution)/shard_map/middle/pallas_call | solution.py:656
  14.3 0.0 collective-permute-done.3.rest_2_
  14.4 1.6 %collective-permute-start.4 = (bf16[48,1024]{1,0:T(8,128)(2,1)S(1)}, bf16[48,1024]{1,0:T(8,128)(2,1)S(1)}, u32[]{:S(2)}, u32[]{:S(2)}) collective-permute-start(bf16[48,1024]{1,0:T(8,128)(2,1)S(1)} %pad_maximum_fusion), channel_id=1, source_target_pairs={{0,4},{4,0},{8,12},{12,8},{1,5},{5,1},{9,13},{13,9},{2,6},{6,2},{1... | collective-permute-start | bytes 294920 | tf_op jit(solution)/shard_map/ppermute | solution.py:674
  16.0 0.0 collective-permute-done.1
  16.0 0.0 copy-start
  16.0 0.0 copy-start.1
  16.0 0.0 copy-start.2
  16.0 3.2 %middle.3 = (f32[2,6,32,384]{3,2,1,0:T(8,128)S(1)}, bf16[512,768]{1,0:T(8,128)(2,1)S(1)}, f32[2,5,3,8,128]{4,3,2,1,0:T(8,128)S(1)}, f32[3,8,128]{2,1,0:T(8,128)S(1)}, bf16[16,1024]{1,0:T(8,128)(2,1)}) custom-call(bf16[576,1024]{1,0:T(8,128)(2,1)S(1)} %get-tuple-element.21.own_ref, bf16[144,512]{1,0:T(8,128)(2,1)S(1)} %bitcast.5, ...), custom_call_target="tpu_custom_call" | custom-call | flops 2000000000 | bytes 2000000 | tf_op jit(solution)/shard_map/middle/pallas_call | solution.py:656
  19.3 0.0 collective-permute-done.4.rest_3_
  19.3 0.0 copy-done
  19.3 0.0 copy-done.1
  19.3 0.0 copy-done.2
  19.3 6.0 %edges.1 = f32[2,6,32,1024]{3,2,1,0:T(8,128)} custom-call(s32[2,4]{1,0:T(2,128)S(1)} %copy-done, s32[2,4]{1,0:T(2,128)S(1)} %copy-done.1, s32[2,4]{1,0:T(2,128)S(1)} %copy-done.2, bf16[576,1024]{1,0:T(8,128)(2,1)S(1)} %get-tuple-element.21.own_ref, bf16[144,512]{1,0:T(8,128)(2,1)S(1)} %bitcast.6, bf16[144,512]{1,0:T(8,128)(2,1)S(1)} %bitcast.8, ...), custom_call_target="tpu_custom_call" | custom-call | tf_op jit(solution)/shard_map/edges/pallas_call | solution.py:695
  (6 shorter events, 0.0 us)
Async XLA Ops:
  1.5 5.0 %collective-permute-start.2 = (bf16[1,16,256]{2,1,0:T(8,128)(2,1)S(1)}, bf16[1,16,256]{2,1,0:T(8,128)(2,1)S(1)}, u32[]{:S(2)}, u32[]{:S(2)}) collective-permute-start(bf16[1,16,256]{2,1,0:T(8,128)(2,1)S(1)} %get-tuple-element.26), channel_id=1, source_target_pairs={{0,2},{2,0},{1,3},{3,1},{4,6},{6,4},{5,7},{7,5},{8,10},{10,8},{9,1... | collective-permute-start | bytes 24584 | tf_op jit(solution)/shard_map/ppermute | solution.py:627
  4.5 6.8 %collective-permute-start = (bf16[1,144,512]{2,1,0:T(8,128)(2,1)S(1)}, bf16[1,144,512]{2,1,0:T(8,128)(2,1)S(1)}, u32[]{:S(2)}, u32[]{:S(2)}) collective-permute-start(bf16[1,144,512]{2,1,0:T(8,128)(2,1)S(1)} %get-tuple-element.22), channel_id=1, source_target_pairs={{0,2},{2,0},{1,3},{3,1},{4,6},{6,4},{5,7},{7,5},{8,10},{10,8},{9,1... | collective-permute-start | bytes 442376 | tf_op jit(solution)/shard_map/ppermute | solution.py:627
  4.6 11.4 %collective-permute-start.1 = (bf16[1,144,512]{2,1,0:T(8,128)(2,1)S(1)}, bf16[1,144,512]{2,1,0:T(8,128)(2,1)S(1)}, u32[]{:S(2)}, u32[]{:S(2)}) collective-permute-start(bf16[1,144,512]{2,1,0:T(8,128)(2,1)S(1)} %get-tuple-element.23), channel_id=1, source_target_pairs={{0,2},{2,0},{1,3},{3,1},{4,6},{6,4},{5,7},{7,5},{8,10},{10,8},{9,1... | collective-permute-start | bytes 442376 | tf_op jit(solution)/shard_map/ppermute | solution.py:627
  6.6 7.7 %collective-permute-start.3 = (bf16[32,1024]{1,0:T(8,128)(2,1)S(1)}, bf16[32,1024]{1,0:T(8,128)(2,1)S(1)}, u32[]{:S(2)}, u32[]{:S(2)}) collective-permute-start(bf16[32,1024]{1,0:T(8,128)(2,1)S(1)} %maximum_maximum_fusion), channel_id=1, source_target_pairs={{0,8},{4,12},{8,0},{12,4},{1,9},{5,13},{9,1},{13,5},{2,10},{6,14},... | collective-permute-start | bytes 196616 | tf_op jit(solution)/shard_map/ppermute | solution.py:671
  14.4 4.9 %collective-permute-start.4 = (bf16[48,1024]{1,0:T(8,128)(2,1)S(1)}, bf16[48,1024]{1,0:T(8,128)(2,1)S(1)}, u32[]{:S(2)}, u32[]{:S(2)}) collective-permute-start(bf16[48,1024]{1,0:T(8,128)(2,1)S(1)} %pad_maximum_fusion), channel_id=1, source_target_pairs={{0,4},{4,0},{8,12},{12,8},{1,5},{5,1},{9,13},{13,9},{2,6},{6,2},{1... | collective-permute-start | bytes 294920 | tf_op jit(solution)/shard_map/ppermute | solution.py:674
  16.0 3.2 %copy-start = (s32[2,4]{1,0:T(2,128)S(1)}, s32[2,4]{1,0:T(2,128)}, u32[]{:S(2)}) copy-start(s32[2,4]{1,0:T(2,128)} %peer_ref.1) | copy-start | bytes 100
  16.0 3.2 %copy-start.1 = (s32[2,4]{1,0:T(2,128)S(1)}, s32[2,4]{1,0:T(2,128)}, u32[]{:S(2)}) copy-start(s32[2,4]{1,0:T(2,128)} %flip_ref.1) | copy-start | bytes 100
  16.0 3.2 %copy-start.2 = (s32[2,4]{1,0:T(2,128)S(1)}, s32[2,4]{1,0:T(2,128)}, u32[]{:S(2)}) copy-start(s32[2,4]{1,0:T(2,128)} %turn_ref.1) | copy-start | bytes 100

commit v4 on v2

v4 whole, which is shorter than its diff:
```python
import functools

import jax
import jax.numpy as jnp
import numpy as np
from jax import lax
from jax.experimental import pallas as pl
from jax.experimental.pallas import tpu as pltpu
from jax.sharding import PartitionSpec as P

STEPS = 6
LANES = 128
SUB = 8
SLOTS = 8
BF = jnp.bfloat16
F32 = jnp.float32
MARGIN = STEPS + 1
PARTS = 4
WINDOW = PARTS * LANES
PACK_LIMIT = 8 << 20
MID_LIMIT = 20 << 20
EDGE_LIMIT = 20 << 20


def split_hi_lo(value):
    hi = value.astype(BF).astype(F32)
    return hi, value - hi


def lane_iota():
    return lax.broadcasted_iota(jnp.int32, (SUB, LANES), 1)


def sub_iota(width):
    return lax.broadcasted_iota(jnp.int32, (SUB, width), 0)


def compact(tiles):
    slot = lane_iota() // 16
    packed = []
    for at in range(0, len(tiles), SLOTS):
        total = None
        for g, tile in enumerate(tiles[at : at + SLOTS]):
            moved = pltpu.roll(tile, (8 + 16 * g) % LANES, 1)
            total = moved if total is None else jnp.where(slot == g, moved, total)
        packed.append(total)
    return packed


def fetched(pairs, sems):
    copies = [pltpu.make_async_copy(src, dst, sems.at[i]) for i, (src, dst) in enumerate(pairs)]
    for copy in copies:
        copy.start()
    return copies


def edge_tile(band):
    left = lax.broadcasted_iota(jnp.int32, (band.shape[0], LANES), 1) < LANES // 2
    return jnp.where(left, band[:, :LANES], band[:, band.shape[1] - LANES :])


def compact_rows(tiles):
    packed = compact(tiles)
    packed += [jnp.zeros((SUB, LANES), F32)] * (-len(packed) % 2)
    return [jnp.concatenate(packed[i : i + 2], axis=0).astype(BF) for i in range(0, len(packed), 2)]


def pack_kernel(
    halves, ends_col, n_belt, wind_hbm, metric_hbm, kappa_hbm, peer_hbm, flip_hbm, turn_hbm,
    bulk_ref, corner_ref, rim_ref, side_ref, own_ref, pick_ref, facts_ref, *scratch
):
    wind_ref, kappa_ref, metric_ref, peer_ref, flip_ref, turn_ref, sems = scratch
    levels, rows, cols = wind_hbm.shape[1:]
    first = lax.axis_index("across") == 0
    pairs = [(wind_hbm, wind_ref), (kappa_hbm, kappa_ref), (metric_hbm, metric_ref)]
    pairs += [(peer_hbm, peer_ref), (flip_hbm, flip_ref), (turn_hbm, turn_ref)]
    for copy in fetched(pairs, sems):
        copy.wait()
    at_belt = lax.axis_index("belt")
    edge = jnp.where(first, 0, 1)
    for i, block in enumerate((at_belt, lax.rem(at_belt + 1, n_belt), lax.rem(at_belt + n_belt - 1, n_belt))):
        slot = (end_slot if i else rim_slot)(peer_ref[edge, block], at_belt, n_belt)
        turn = turn_ref[edge, block]
        cosine = jnp.where(turn == 0, 1.0, jnp.where(turn == 2, -1.0, 0.0))
        sine_neg = jnp.where(turn == 1, -1.0, jnp.where(turn == 3, 1.0, 0.0))
        found = (slot.astype(F32), flip_ref[edge, block].astype(F32), cosine, sine_neg)
        for k, value in enumerate(found):
            facts_ref[4 * i + k] = jnp.full((16, LANES), value, F32)
    wanted = peer_ref[edge, at_belt ^ 1]
    pick_ref[...] = jnp.full(pick_ref.shape, jnp.where(wanted == at_belt, 1.0, 0.0), BF)
    top, bottom = slice(0, SUB), slice(rows - SUB, rows)

    def bands_of(whole):
        if halves == 1:
            return [jnp.where(first, whole[bottom], whole[top])]
        return [whole[bottom], whole[top]]

    pieces, tiles, rim_rows = [[] for _ in range(halves)], [], []
    for f in range(2 * levels):
        own_ref[rows * f : rows * (f + 1)] = wind_ref[f // levels, f % levels]
        whole = wind_ref[f // levels, f % levels].astype(F32)
        for k, band in enumerate(bands_of(whole)):
            pieces[k].append(band)
        tiles += [edge_tile(whole[r : r + SUB]) for r in range(0, rows, SUB)]
        rim_rows.append(jnp.where(first, whole[0:1], whole[rows - 1 : rows]))
    for q in range(3):
        for half, part in enumerate(split_hi_lo(kappa_ref[q] if q < 2 else metric_ref[...])):
            at = rows * (2 * levels + 2 * q + half)
            own_ref[at : at + rows] = part.astype(BF)
            for k, band in enumerate(bands_of(part)):
                pieces[k].append(band)
            tiles += [edge_tile(part[r : r + SUB]) for r in range(0, rows, SUB)]
    for k in range(halves):
        for i in range(0, len(pieces[k]), 2):
            both = jnp.concatenate([pieces[k][i], pieces[k][i + 1]], axis=0)
            bulk_ref[k, SUB * i : SUB * (i + 2)] = both.astype(BF)
        for i, tile in enumerate(compact_rows([edge_tile(p) for p in pieces[k]])):
            corner_ref[k, :, LANES * i : LANES * (i + 1)] = tile
    rim = jnp.concatenate(rim_rows + [jnp.zeros((16 - len(rim_rows), cols), F32)], axis=0)
    rim_ref[...] = rim.astype(BF)
    side_ref[...] = jnp.zeros(side_ref.shape, BF)
    for i, tile in enumerate(compact_rows(tiles)):
        side_ref[:, LANES * i : LANES * (i + 1)] = tile
    if ends_col is not None:
        side_ref[:, ends_col : ends_col + LANES] = edge_tile(rim).astype(BF)


def rim_slot(block, at_belt, n_belt):
    if n_belt != 4:
        return block
    return jnp.where(block == at_belt, 0, jnp.where((block ^ at_belt) == 2, 2, 1))


def end_slot(block, at_belt, n_belt):
    if n_belt != 4:
        return block
    offset = block ^ at_belt
    return jnp.where(offset == 2, 3, jnp.where(offset == 3, 2, offset))


class Rows:
    def __init__(self, levels, rows, halves):
        self.levels, self.rows, self.halves = levels, rows, halves
        self.fields, self.bands = 2 * levels, 2 * levels + 6
        self.tiles, self.span = rows // SUB, SUB * halves
        self.slab = self.tiles + halves
        self.height = SUB * self.slab

    def own_base(self, f):
        return 2 * self.height * (f // 2) + (self.height + self.span) * (f % 2)

    def band_base(self, f):
        return 2 * self.height * (f // 2) + self.rows

    def place_of(self, f, e):
        return e if f % 2 == 0 else (e + self.halves) % self.slab


def east_of(f):
    return [*f[1:], pltpu.roll(f[0], LANES - 1, 1)]


def west_of(f):
    return [pltpu.roll(f[-1], 1, 1), *f[:-1]]


def fill_order(order_ref, offset):
    size = order_ref.shape[0]
    at = lax.broadcasted_iota(jnp.int32, (size, LANES), 0)
    lane = lax.broadcasted_iota(jnp.int32, (1, LANES), 1)
    for r in range(PARTS):
        tile = jnp.where(at == PARTS * lane + (r + offset), 1.0, 0.0).astype(BF)
        order_ref[:, LANES * r : LANES * (r + 1)] = tile
        order_ref[:, LANES * (PARTS + r) : LANES * (PARTS + r + 1)] = tile


def solve_window(lay, first, last, x_ref, order_ref, work, extra=None):
    y_ref, coef_ref, met_ref, even_ref, odd_ref, fin_ref, z_ref = work
    levels, rows, fields, tiles = lay.levels, lay.rows, lay.fields, lay.tiles
    slab, height, span = lay.slab, lay.height, lay.span
    sub = lax.broadcasted_iota(jnp.int32, (SUB, LANES), 0)
    sub_slab = lax.broadcasted_iota(jnp.int32, (height, LANES), 0)
    closed = ((sub_slab == rows - 1) & last) | ((sub_slab == height - 1) & first)

    def put(ref, f, r, i, value):
        ref[f, r, SUB * (i + 1) : SUB * (i + 2)] = value
        if i == 0:
            ref[f, r, SUB * (slab + 1) : SUB * (slab + 2)] = value
        if i == slab - 1:
            ref[f, r, 0:SUB] = value
        if r == 0:
            return [(ref, f, PARTS, i, pltpu.roll(value, LANES - 1, 1))]
        if r == PARTS - 1:
            return [(ref, f, PARTS + 1, i, pltpu.roll(value, 1, 1))]
        return []

    def flush(rotated):
        for ref, f, plane, i, value in rotated:
            ref[f, plane, SUB * (i + 1) : SUB * (i + 2)] = value

    extra_place = slab + 2

    def advance(source, target, final):
        waiting = []
        for c in range(2):
            for e in [*range(tiles if final else slab)] + [None] * (extra is not None):
                mid, east, west, south, north = (
                    [
                        extra[0][c, k, r] if e is None else coef_ref[c, k, r, SUB * e : SUB * (e + 1)]
                        for r in range(PARTS)
                    ]
                    for k in range(5)
                )

                def place(f, e=e):
                    return extra_place if e is None else lay.place_of(f, e)

                results = []
                for lev in range(levels):
                    f = c * levels + lev
                    at = SUB * (place(f) + 1)
                    here = [source[f, r, at : at + SUB] for r in range(PARTS + 2)]
                    right = here[1 : PARTS + 1]
                    left = [here[PARTS + 1], *here[: PARTS - 1]]
                    results.append(
                        [
                            (mid[r] * here[r] + south[r] * source[f, r, at + 1 : at + 1 + SUB])
                            + north[r] * source[f, r, at - 1 : at - 1 + SUB]
                            + (east[r] * right[r] + west[r] * left[r])
                            for r in range(PARTS)
                        ]
                    )
                rotated = []
                for lev in range(levels):
                    f = c * levels + lev
                    for r in range(PARTS):
                        if final:
                            at = rows * fields + SUB * f if e is None else rows * f + SUB * e
                            fin_ref[at : at + SUB, LANES * r : LANES * (r + 1)] = results[lev][r]
                        else:
                            rotated += put(target, f, r, place(f), results[lev][r])
                flush(waiting)
                waiting = rotated
        flush(waiting)

    whole = jnp.dot(x_ref[...], order_ref[:, 0:WINDOW], preferred_element_type=F32)
    for r in range(PARTS):
        y_ref[r] = whole[:, LANES * r : LANES * (r + 1)]
    for q in range(3):
        base = height * (fields + 2 * q)
        low = base + height
        value = [
            y_ref[r, base : base + height]
            + jnp.concatenate([y_ref[r, low + span : low + height], y_ref[r, low : low + span]], axis=0)
            for r in range(PARTS)
        ]
        if q == 2:
            for r in range(PARTS):
                met_ref[r] = 0.5 * value[r]
            continue
        right = east_of(value)
        east = [0.5 * (value[r] + right[r]) for r in range(PARTS)]
        west = west_of(east)
        for r in range(PARTS):
            south = jnp.where(closed, 0.0, 0.5 * (value[r] + pltpu.roll(value[r], height - 1, 0)))
            north = pltpu.roll(south, 1, 0)
            coef_ref[q, 0, r] = 1.0 - ((east[r] + west[r]) + (south + north))
            coef_ref[q, 1, r] = east[r]
            coef_ref[q, 2, r] = west[r]
            coef_ref[q, 3, r] = south
            coef_ref[q, 4, r] = north
    waiting = []
    for e in range(slab):
        rotated = []
        metric = [met_ref[r, SUB * e : SUB * (e + 1)] for r in range(PARTS)]
        for lev in range(levels):
            across, belt = [], []
            for c in range(2):
                f = c * levels + lev
                base, i = height * f, lay.place_of(f, e)
                at = base + SUB * i
                here = [y_ref[r, at : at + SUB] for r in range(PARTS)]
                right, left = east_of(here), west_of(here)
                belt.append([right[r] - left[r] for r in range(PARTS)])
                diffs = []
                for r in range(PARTS):
                    if i < slab - 1:
                        below = y_ref[r, at + 1 : at + 1 + SUB]
                    else:
                        wrap = pltpu.roll(y_ref[r, base : base + SUB], SUB - 1, 0)
                        below = jnp.where(sub == SUB - 1, wrap, pltpu.roll(here[r], SUB - 1, 0))
                    if i > 0:
                        above = y_ref[r, at - 1 : at - 1 + SUB]
                    else:
                        end = base + height
                        wrap = pltpu.roll(y_ref[r, end - SUB : end], 1, 0)
                        above = jnp.where(sub == 0, wrap, pltpu.roll(here[r], 1, 0))
                    diffs.append(below - above)
                across.append(diffs)
            for r in range(PARTS):
                curl = metric[r] * (across[0][r] - belt[1][r])
                divergence = metric[r] * (-belt[0][r] - across[1][r])
                rotated += put(even_ref, lev, r, lay.place_of(lev, e), curl)
                rotated += put(even_ref, levels + lev, r, lay.place_of(levels + lev, e), divergence)
        flush(waiting)
        waiting = rotated
    flush(waiting)

    if extra is not None:
        for ref in (even_ref, odd_ref):
            for at in (extra_place, extra_place + 2):
                ref[:, 0:PARTS, SUB * at : SUB * (at + 1)] = jnp.zeros((fields, PARTS, SUB, LANES), F32)
        rotated = []
        for f in range(fields):
            c, lev = f // levels, f % levels
            at = height * lay.bands + SUB * c + lev
            for r in range(PARTS):
                value = (1.0 - 2.0 * c) * extra[1][r] * y_ref[r, at : at + 1]
                rotated += put(even_ref, f, r, extra_place, value)
        flush(rotated)

    def two(k, _):
        advance(even_ref, odd_ref, False)
        advance(odd_ref, even_ref, False)
        return 0

    lax.fori_loop(0, STEPS // 2 - 1, two, 0)
    advance(even_ref, odd_ref, False)
    advance(odd_ref, None, True)
    value = fin_ref[...]
    hi = value.astype(BF)
    z_ref[:, 0:WINDOW] = hi
    z_ref[:, WINDOW:] = (value - hi.astype(F32)).astype(BF)


def work_shapes(lay, extra):
    out_rows = (lay.rows + SUB * extra) * lay.fields
    plane = (lay.fields, PARTS + 2, lay.height + 2 * SUB + 3 * SUB * extra, LANES)
    return [
        pltpu.VMEM((PARTS, lay.height * lay.bands + 2 * SUB * extra, LANES), F32),
        pltpu.VMEM((2, 5, PARTS, lay.height, LANES), F32),
        pltpu.VMEM((PARTS, lay.height, LANES), F32),
        pltpu.VMEM(plane, F32),
        pltpu.VMEM(plane, F32),
        pltpu.VMEM((out_rows, WINDOW), F32),
        pltpu.VMEM((out_rows, 2 * WINDOW), BF),
    ]


def back_to_natural(z, order):
    return lax.dot_general(z, order, (((1,), (1,)), ((), ())), preferred_element_type=F32)


def ghost_tile_at(lay, first):
    return pl.multiple_of(jnp.where(first, 0, lay.rows - SUB), SUB)


def collect_rims(relay, refs, rims_ref, ends_ref):
    rim_ref, side_ref, far_ref, near_ref = refs
    for k, rim in enumerate((rim_ref[...], near_ref[0:16], far_ref[0:16])):
        rims_ref[k] = rim
    ends_cols = slice(relay[1], relay[1] + LANES)
    for k, (ref, at) in enumerate(((side_ref, 0), (near_ref, 16), (near_ref, 32), (far_ref, 16))):
        ends_ref[k] = ref[at : at + 16, ends_cols]


def ghost_rows(lay, facts_ref, rims_ref, ends_ref, ghost_ref):
    levels, cols = lay.levels, rims_ref.shape[-1]
    col_tiles = cols // LANES
    ghost_ref[...] = jnp.zeros(ghost_ref.shape, F32)

    def selected(i, ref, place):
        found = ref[0, :, place].astype(F32)
        for q in range(1, ref.shape[0]):
            found = jnp.where(facts_ref[4 * i] == q, ref[q, :, place].astype(F32), found)
        return found

    raw = [selected(0, rims_ref, slice(LANES * t, LANES * (t + 1))) for t in range(col_tiles)]
    raw += [selected(i, ends_ref, slice(0, LANES)) for i in (1, 2)]
    lane_r = lax.broadcasted_iota(jnp.int32, (LANES, LANES), 0)
    lane_c = lax.broadcasted_iota(jnp.int32, (LANES, LANES), 1)
    backward = jnp.where(lane_r + lane_c == LANES - 1, 1.0, 0.0).astype(BF)
    turned = reorder(jnp.concatenate(raw, axis=0).astype(BF), backward)

    def ghost_parts(i, plain, flipped):
        found = jnp.where(facts_ref[4 * i + 1] == 1, turned[16 * flipped : 16 * (flipped + 1)], raw[plain])
        p, q = found[0:levels], found[levels : 2 * levels]
        cosine, sine_neg = facts_ref[4 * i + 2, 0:levels], facts_ref[4 * i + 3, 0:levels]
        return cosine * p + sine_neg * q, cosine * q - sine_neg * p

    for t in range(col_tiles):
        for c, part in enumerate(ghost_parts(0, t, col_tiles - 1 - t)):
            ghost_ref[c, 0:levels, LANES * t : LANES * (t + 1)] = part
    after_tiles = ghost_parts(1, col_tiles, col_tiles)
    before_tiles = ghost_parts(2, col_tiles + 1, col_tiles + 1)
    lane_row = lax.broadcasted_iota(jnp.int32, (levels, LANES), 1)
    for c in range(2):
        both = jnp.where(lane_row < LANES // 2, after_tiles[c], before_tiles[c])
        ghost_ref[c, 0:levels, cols:] = both


def reorder(rows, order):
    return jnp.dot(rows, order, preferred_element_type=F32)


def middle_kernel(lay, k, relay, own_ref, bulk_ref, *rest):
    first, last = lax.axis_index("across") == 0, lax.axis_index("across") == lax.axis_size("across") - 1
    ghost_ref = None
    if k == 1:
        order_ref, weights_ref, touched_ref, facts_ref, *rest = rest
        if relay is None:
            rims_ref, ends_ref, out_ref, ghost_ref, grown_ref, x_ref, *work = rest
        else:
            *rest, rims_ref, ends_ref = rest
            collect_rims(relay, rest[:4], rims_ref, ends_ref)
            out_ref, ghost_ref, grown_ref, x_ref, *work = rest[4:]
        ghost_rows(lay, facts_ref, rims_ref, ends_ref, ghost_ref)
    else:
        out_ref, order_ref, weights_ref, touched_ref, x_ref, *work = rest
        fill_order(order_ref, 0)
    cols = slice(WINDOW * k, WINDOW * (k + 1))
    for f in range(lay.bands):
        base = lay.own_base(f)
        x_ref[base : base + lay.rows] = own_ref[lay.rows * f : lay.rows * (f + 1), cols]
    span = lay.span
    at_row = lax.broadcasted_iota(jnp.int32, (2 * span, WINDOW), 0)
    for f in range(0, lay.bands, 2):
        band = bulk_ref[span * f : span * (f + 2), cols]
        if f < lay.fields:
            band = band.astype(F32)
            for g in range(2):
                c, lev = (f + g) // lay.levels, (f + g) % lay.levels
                row = 0.0 if ghost_ref is None else ghost_ref[c, lev : lev + 1, cols]
                spot = jnp.where(first, span * (g + 1) - 1, jnp.where(last, span * g, -1))
                band = jnp.where(at_row == spot, row, band)
            band = band.astype(BF)
        at = lay.band_base(f)
        x_ref[at : at + 2 * span] = band
    extra = None
    if k == 1:
        beside = jnp.concatenate([ghost_ref[c, :, :WINDOW] for c in range(2)], axis=0)
        x_ref[lay.height * lay.bands :] = beside.astype(BF)
        sub = lax.broadcasted_iota(jnp.int32, (SUB, LANES), 0)
        sign = jnp.where(first, -1.0, jnp.where(last, 1.0, 0.0))
        lift = jnp.where(sub == jnp.where(first, 0, SUB - 1), sign, 0.0)
        extra = weights_ref, [lift * touched_ref[r] for r in range(PARTS)]
    solve_window(lay, first, last, x_ref, order_ref, work, extra)
    back = back_to_natural(work[-1][...], order_ref[...])
    for f in range(lay.fields):
        c, lev = f // lay.levels, f % lay.levels
        out_ref[c, lev] = back[lay.rows * f : lay.rows * (f + 1)]
        if k == 1:
            at = lay.rows * lay.fields + SUB * f
            grown_ref[c, lev] = back[at : at + SUB]
    if k == 0:
        at = ghost_tile_at(lay, first)
        weights_ref[...] = work[1][:, :, :, pl.ds(at, SUB)]
        touched_ref[...] = work[2][:, pl.ds(at, SUB)]


def weights(kappa, closed_rows):
    height, width = kappa.shape
    east = 0.5 * (kappa + pltpu.roll(kappa, width - 1, 1))
    west = pltpu.roll(east, 1, 1)
    south = jnp.where(closed_rows, 0.0, 0.5 * (kappa + pltpu.roll(kappa, height - 1, 0)))
    north = pltpu.roll(south, 1, 0)
    return 1.0 - ((east + west) + (south + north)), east, west, south, north


def diffused(values, coefs):
    def step(f, mid, east, west, south, north):
        height, width = f.shape
        return (mid * f + east * pltpu.roll(f, width - 1, 1) + west * pltpu.roll(f, 1, 1)) + (
            south * pltpu.roll(f, height - 1, 0) + north * pltpu.roll(f, 1, 0)
        )

    for _ in range(STEPS):
        values = [[step(f, *coef) for f in component] for component, coef in zip(values, coefs)]
    return values


def edge_kernel(lay, relay, own_ref, bulk_ref, ghost_ref, grown_ref, m0_ref, m1_ref, *rest):
    if relay is None:
        side_a_ref, side_b_ref, corner_a_ref, corner_b_ref, *rest = rest
    else:
        near_ref, *rest = rest
        side_a_ref, side_b_ref = near_ref.at[16:32], near_ref.at[32:48]
        corner_a_ref, corner_b_ref = (near_ref.at[pl.ds(k, 16), relay[0] : relay[1]] for k in (16, 32))
    out_hbm, head_ref, seam_ref, tail_ref, strip_ref, sems = rest
    levels, rows, cols = lay.levels, lay.rows, own_ref.shape[1]
    tiles, halves, fields, bands, span = lay.tiles, lay.halves, lay.fields, lay.bands, lay.span
    at_belt, at_across = lax.axis_index("belt"), lax.axis_index("across")
    first, last = at_across == 0, at_across == lax.axis_size("across") - 1
    ghost_at = ghost_tile_at(lay, first)
    edge_rows = pl.ds(ghost_at, SUB)
    calm = pl.ds(pl.multiple_of(jnp.where(first, SUB, 0), SUB), rows - SUB)
    inner, after = slice(LANES, WINDOW - LANES), slice(WINDOW + LANES, cols - LANES)
    early = [
        pltpu.make_async_copy(m0_ref.at[:, :, calm, inner], out_hbm.at[:, :, calm, inner], sems.at[0]),
        pltpu.make_async_copy(m1_ref.at[:, :, :, inner], out_hbm.at[:, :, :, after], sems.at[1]),
    ]
    for copy in early:
        copy.start()
    even = lax.rem(at_belt, 2) == 0
    from_right = (lane_iota() // 8) % 2 == 1
    take_a = from_right == even

    def unpacked(a_ref, b_ref, groups):
        out = []
        for g in range(groups):
            column, half = LANES * (g // 2), slice(SUB * (g % 2), SUB * (g % 2) + SUB)
            a = a_ref(column).astype(F32)[half]
            b = b_ref(column).astype(F32)[half]
            out.append(jnp.where(take_a, a, b))
        return out

    def put_back(packed, index):
        return pltpu.roll(packed[index // SLOTS], (-(8 + 16 * (index % SLOTS))) % LANES, 1)

    side_tiles = unpacked(
        lambda k: side_a_ref[:, k : k + LANES], lambda k: side_b_ref[:, k : k + LANES],
        -(-bands * tiles // SLOTS),
    )
    corners = [
        unpacked(
            lambda k, at=at: (corner_a_ref if relay else corner_a_ref.at[at])[:, k : k + LANES],
            lambda k, at=at: (corner_b_ref if relay else corner_b_ref.at[at])[:, k : k + LANES],
            -(-bands // SLOTS),
        )
        for at in range(halves)
    ]

    places = [slice(at, at + LANES) for at in (0, WINDOW - LANES, WINDOW, cols - LANES)]

    def fold(rows_of, halo):
        lane = lax.broadcasted_iota(jnp.int32, halo.shape, 1)
        start, before_seam, after_seam, end = (rows_of(place) for place in places)
        left = pltpu.roll(jnp.where(lane >= LANES - SUB, halo, start), SUB, 1)
        seam = pltpu.roll(jnp.where(lane >= LANES // 2, before_seam, after_seam), LANES // 2, 1)
        right = pltpu.roll(jnp.where(lane < SUB, halo, end), LANES - SUB, 1)
        return jnp.where(lane < 40, left, jnp.where(lane < 88, seam, right))

    ghosts = [fold(lambda place, c=c: ghost_ref[c, :, place], ghost_ref[c, :, cols:]) for c in range(2)]
    at_band = lax.broadcasted_iota(jnp.int32, (span, LANES), 0)
    spot = jnp.where(first, span - 1, jnp.where(last, 0, -1))
    slabs = []
    for f in range(bands):
        own = slice(rows * f, rows * (f + 1))
        halo = jnp.concatenate([put_back(side_tiles, f * tiles + r) for r in range(tiles)], axis=0)
        own_rows = fold(lambda place, own=own: own_ref[own, place].astype(F32), halo)
        pair, half = slice(span * (f - f % 2), span * (f - f % 2 + 2)), slice(span * (f % 2), span * (f % 2 + 1))
        band = fold(
            lambda place, pair=pair, half=half: bulk_ref[pair, place].astype(F32)[half],
            jnp.concatenate([put_back(corners[at], f) for at in range(halves)], axis=0),
        )
        if f < fields:
            c, lev = f // levels, f % levels
            band = jnp.where(at_band == spot, ghosts[c][lev : lev + 1], band)
        slabs.append(jnp.concatenate([own_rows, band], axis=0))
    at_row = lax.broadcasted_iota(jnp.int32, (lay.height, LANES), 0)
    closed = ((at_row == rows - 1) & last) | ((at_row == lay.height - 1) & first)
    kappas = [slabs[fields + 2 * q] + slabs[fields + 2 * q + 1] for q in range(3)]
    metric = 0.5 * kappas[2]

    def across_diff(f):
        return pltpu.roll(f, lay.height - 1, 0) - pltpu.roll(f, 1, 0)

    def belt_diff(f):
        return pltpu.roll(f, LANES - 1, 1) - pltpu.roll(f, 1, 1)

    pairs = [(slabs[lev], slabs[levels + lev]) for lev in range(levels)]
    values = [
        [metric * (across_diff(u) - belt_diff(v)) for u, v in pairs],
        [metric * (-belt_diff(u) - across_diff(v)) for u, v in pairs],
    ]
    values = diffused(values, [weights(kappas[c], closed) for c in range(2)])

    lane = lax.broadcasted_iota(jnp.int32, (rows, LANES), 1)
    lane_tile = lane[:SUB]
    low, high = MARGIN, LANES - MARGIN
    first_tile, last_tile = slice(0, LANES), slice(WINDOW - LANES, WINDOW)
    for c in range(2):
        for lev in range(levels):
            result, added = values[c][lev][:rows], grown_ref[c, lev]
            turned = pltpu.roll(result, LANES // 2, 1)
            head_ref[c, lev] = jnp.where(lane < low, pltpu.roll(result, LANES - SUB, 1), m0_ref[c, lev, :, first_tile])
            seam_ref[c, lev, :, :LANES] = jnp.where(lane >= high, turned, m0_ref[c, lev, :, last_tile])
            seam_ref[c, lev, :, LANES:] = jnp.where(lane < low, turned, m1_ref[c, lev, :, first_tile])
            tail_ref[c, lev] = jnp.where(lane >= high, pltpu.roll(result, SUB, 1), m1_ref[c, lev, :, last_tile])
            head_ref[c, lev, edge_rows] = head_ref[c, lev, edge_rows] + jnp.where(
                lane_tile >= low, added[:, first_tile], 0.0
            )
            seam_ref[c, lev, edge_rows, :LANES] = seam_ref[c, lev, edge_rows, :LANES] + jnp.where(
                lane_tile < high, added[:, last_tile], 0.0
            )
            strip_ref[c, lev] = m0_ref[c, lev, edge_rows, inner] + added[:, inner]
    late = [
        pltpu.make_async_copy(strip_ref, out_hbm.at[:, :, edge_rows, inner], sems.at[2]),
        pltpu.make_async_copy(head_ref, out_hbm.at[:, :, :, :LANES], sems.at[3]),
        pltpu.make_async_copy(seam_ref, out_hbm.at[:, :, :, WINDOW - LANES : WINDOW + LANES], sems.at[4]),
        pltpu.make_async_copy(tail_ref, out_hbm.at[:, :, :, cols - LANES :], sems.at[5]),
    ]
    for copy in late:
        copy.start()
    for copy in early + late:
        copy.wait()


def per_device(wind, metric, kappa, edge_peer, edge_flip, edge_turn):
    _, levels, rows, cols = wind.shape
    n_across, n_belt = lax.axis_size("across"), lax.axis_size("belt")
    halves = 1 if n_across == 2 else 2
    fields = 2 * levels
    bands = fields + 6
    corner_cols = LANES * (-(-bands // (2 * SLOTS)))
    side_cols = LANES * (-(-bands * (rows // SUB) // (2 * SLOTS)))
    ends_col = side_cols + corner_cols
    relay = halves == 1 and n_belt == 4 and ends_col + LANES <= cols

    vmem = pl.BlockSpec(memory_space=pltpu.VMEM)
    anywhere = pl.BlockSpec(memory_space=pl.ANY)
    lay = Rows(levels, rows, halves)
    height, span = lay.height, lay.span
    bulk, corner, rim, side, own, pick, facts = pl.pallas_call(
        functools.partial(pack_kernel, halves, ends_col if relay else None, n_belt),
        out_shape=[
            jax.ShapeDtypeStruct((halves, SUB * bands, cols), BF),
            jax.ShapeDtypeStruct((halves, 16, corner_cols), BF),
            jax.ShapeDtypeStruct((16, cols), BF),
            jax.ShapeDtypeStruct((16, cols), BF),
            jax.ShapeDtypeStruct((rows * bands, cols), BF),
            jax.ShapeDtypeStruct((16, cols), BF),
            jax.ShapeDtypeStruct((12, 16, LANES), F32),
        ],
        in_specs=[anywhere] * 6,
        out_specs=[vmem] * 7,
        scratch_shapes=[
            pltpu.VMEM(wind.shape, BF),
            pltpu.VMEM(kappa.shape, F32),
            pltpu.VMEM(metric.shape, F32),
            pltpu.SMEM(edge_peer.shape, jnp.int32),
            pltpu.SMEM(edge_flip.shape, jnp.int32),
            pltpu.SMEM(edge_turn.shape, jnp.int32),
            pltpu.SemaphoreType.DMA((6,)),
        ],
        compiler_params=pltpu.CompilerParams(vmem_limit_bytes=PACK_LIMIT),
        name="pack",
    )(
        *(
            pltpu.with_memory_space_constraint(x, pltpu.HBM)
            for x in (wind, metric, kappa, edge_peer, edge_flip, edge_turn)
        )
    )

    pairs_a = [(i, i ^ 1) for i in range(n_belt)]
    pairs_b = [(i, (i + 1) % n_belt if i % 2 else (i - 1) % n_belt) for i in range(n_belt)]
    if halves == 1:
        swap = [(0, 1), (1, 0)]
        bulk_in = lax.ppermute(bulk, "across", swap)
        corner_in = lax.ppermute(corner, "across", swap)
    else:
        onward = [(i, i + 1) for i in range(n_across - 1)]
        back = [(i + 1, i) for i in range(n_across - 1)]

        def both_ways(message):
            return jnp.stack(
                [
                    lax.ppermute(message[1], "across", back),
                    lax.ppermute(message[0], "across", onward),
                ]
            )

        corner_in, bulk_in = both_ways(corner), both_ways(bulk)
    bulk_in = bulk_in.reshape(halves, bands, SUB, cols).swapaxes(0, 1).reshape(bands * span, cols)

    def middle(k, messages):
        shapes = [jax.ShapeDtypeStruct((2, levels, rows, WINDOW), F32)]
        more = []
        operands = [own, bulk_in, *messages]
        spaces = [vmem] * len(operands)
        if k == 0:
            shapes += [
                jax.ShapeDtypeStruct((WINDOW, 2 * WINDOW), BF),
                jax.ShapeDtypeStruct((2, 5, PARTS, SUB, LANES), F32),
                jax.ShapeDtypeStruct((PARTS, SUB, LANES), F32),
            ]
        else:
            shapes += [
                jax.ShapeDtypeStruct((2, SUB, cols + LANES), F32),
                jax.ShapeDtypeStruct((2, levels, SUB, WINDOW), F32),
            ]
            if relay:
                more = [pltpu.VMEM((3, 16, cols), BF), pltpu.VMEM((4, 16, LANES), BF)]
        return pl.pallas_call(
            functools.partial(middle_kernel, lay, k, (side_cols, ends_col) if relay else None),
            out_shape=shapes,
            in_specs=spaces,
            out_specs=[vmem] * len(shapes),
            scratch_shapes=[pltpu.VMEM((height * bands + 2 * SUB * k, WINDOW), BF)]
            + work_shapes(lay, k)
            + more,
            compiler_params=pltpu.CompilerParams(vmem_limit_bytes=MID_LIMIT),
            cost_estimate=pl.CostEstimate(flops=2_000_000_000, bytes_accessed=2_000_000, transcendentals=0),
            name="middle",
        )(*operands)

    window_0, *shared = middle(0, [])
    if relay:
        spot = slice(side_cols, ends_col)
        side = jnp.concatenate([side[:, :side_cols], corner_in[0], side[:, ends_col:]], axis=1)
        far = lax.ppermute(jnp.concatenate([rim, side]), "belt", [(i, i ^ 2) for i in range(n_belt)])
        rim_c, side_c = far[:16], far[16:]
        chosen = jnp.where(pick > 0, rim, rim_c)
        near = lax.ppermute(jnp.concatenate([chosen, side, side_c]), "belt", pairs_a)
        rim_parts, messages = [rim, side, far, near], [near]
    else:
        side_a = lax.ppermute(side, "belt", pairs_a)
        side_b = lax.ppermute(side, "belt", pairs_b)
        corner_a = lax.ppermute(corner_in, "belt", pairs_a)
        corner_b = lax.ppermute(corner_in, "belt", pairs_b)
        rims = lax.all_gather(rim, "belt")
        if n_belt == 4:
            at_belt = lax.axis_index("belt")
            rims, ends = (rims[at_belt ^ jnp.array([0, 1, 2])], rims[at_belt ^ jnp.array([0, 1, 3, 2])])
        else:
            ends = rims
        ends = jnp.concatenate([ends[..., : LANES // 2], ends[..., cols - LANES // 2 :]], axis=-1)

        rim_parts, messages = [rims, ends], [side_a, side_b, corner_a, corner_b]
    window_1, ghost, grown = middle(1, [*shared, facts, *rim_parts])
    operands = [own, bulk_in, ghost, grown, window_0, window_1, *messages]
    return pl.pallas_call(
        functools.partial(edge_kernel, lay, (side_cols, ends_col) if relay else None),
        out_shape=jax.ShapeDtypeStruct((2, levels, rows, cols), F32),
        in_specs=[vmem] * len(operands),
        out_specs=anywhere,
        scratch_shapes=[
            pltpu.VMEM((2, levels, rows, LANES), F32),
            pltpu.VMEM((2, levels, rows, 2 * LANES), F32),
            pltpu.VMEM((2, levels, rows, LANES), F32),
            pltpu.VMEM((2, levels, SUB, WINDOW - 2 * LANES), F32),
            pltpu.SemaphoreType.DMA((6,)),
        ],
        compiler_params=pltpu.CompilerParams(vmem_limit_bytes=EDGE_LIMIT),
        name="edges",
    )(*operands)


def solution(mesh):
    return jax.shard_map(
        per_device,
        mesh=mesh,
        in_specs=(
            P(None, ("members", "lev"), "across", "belt"),
            P("across", "belt"),
            P(None, "across", "belt"),
            P(),
            P(),
            P(),
        ),
        out_specs=P(None, ("members", "lev"), "across", "belt"),
        check_vma=False,
    )
```

time: 25.8 us -> 25.1 us (0.973)
  Pallas kernels: 13.6 us -> 12.9 us
    pallas_call x3, Pallas kernels: 12.1 us -> 11.3 us  [the longest x2 7.62 us: middle(): pl.pallas_call(functools.partial(middle_kernel, lay, k, (side_cols, ends_...]
  transfers between devices with their start and end apart: 4 -> 4, of which waited for: 2 -> 2; matrix products, arithmetic and copies ran while one was open for 0% -> 0% of each run, Pallas kernels for 23% -> 14%
where the time goes in v4:
time: 25.1 us; the launch traced here: 24.9 us
  Pallas kernels  12.9 us (51%)
  starting transfers between devices  8.19 us (33%)
  waiting for transfers between devices  3.79 us (15%)
    pallas_call x2, Pallas kernels, middle(): pl.pallas_call(functools.partial(middle_kernel, lay, k, (side_cols, ends_...  7.62 us
    pallas_call x1, Pallas kernels, per_device(): pl.pallas_call(functools.partial(edge_kernel, lay, (side_cols, ends_col)...  3.73 us
    ppermute x1, starting transfers between devices, per_device(): lax.ppermute(jnp.concatenate([rim, side]), 'belt', [(i, i ^ 2) for i in r...  3.13 us
    ppermute x1, starting transfers between devices, per_device(): corner_in = lax.ppermute(corner, 'across', swap)  3 us
    ppermute x1, waiting for transfers between devices, per_device(): lax.ppermute(jnp.concatenate([rim, side]), 'belt', [(i, i ^ 2) for i in r...  2.24 us
    ppermute x1, starting transfers between devices, per_device(): lax.ppermute(jnp.concatenate([chosen, side, side_c]), 'belt', pairs_a)  1.97 us
    pallas_call x1, Pallas kernels, per_device(): pl.pallas_call(functools.partial(pack_kernel, halves, ends_col if relay e...  1.55 us
    ppermute x1, waiting for transfers between devices, per_device(): corner_in = lax.ppermute(corner, 'across', swap)  1.54 us
  transfers between devices with their start and end apart: 4, of which 2 were waited for; matrix products, arithmetic and copies ran while one was open for 0% of the time, Pallas kernels for 14%

profile of v4, /device:TPU:0, one launch (start us, length us, event | category | flops | bytes accessed | tf_op | source)
XLA Modules:
  0.0 24.9 jit_solution(11832528331137449253)
XLA Ops:
  0.0 1.6 %pack.1 = (bf16[1,144,1024]{2,1,0:T(8,128)(2,1)S(1)}, bf16[1,16,256]{2,1,0:T(8,128)(2,1)S(1)}, bf16[16,1024]{1,0:T(8,128)(2,1)S(1)}, bf16[16,1024]{1,0:T(8,128)(...) custom-call(bf16[2,6,32,1024]{3,2,1,0:T(8,128)(2,1)} %wind_hbm.1, ...), custom_call_target="tpu_custom_call" | custom-call | tf_op jit(solution)/shard_map/pack/pallas_call | solution.py:624
  1.6 3.0 %collective-permute-start.1 = (bf16[1,16,256]{2,1,0:T(8,128)(2,1)S(1)}, bf16[1,16,256]{2,1,0:T(8,128)(2,1)S(1)}, u32[]{:S(2)}, u32[]{:S(2)}) collective-permute-start(bf16[1,16,256]{2,1,0:T(8,128)(2,1)S(1)} %get-tuple-element.27), channel_id=1, source_target_pairs={{0,2},{2,0},{1,3},{3,1},{4,6},{6,4},{5,7},{7,5},{8,10},{10,8},{9,1... | collective-permute-start | bytes 24584 | tf_op jit(solution)/shard_map/ppermute | solution.py:660
  4.6 0.1 collective-permute-start
  4.7 1.5 %collective-permute-done.1 = bf16[1,16,256]{2,1,0:T(8,128)(2,1)S(1)} collective-permute-done((bf16[1,16,256]{2,1,0:T(8,128)(2,1)S(1)}, bf16[1,16,256]{2,1,0:T(8,128)(2,1)S(1)}, u32[]{:S(2)}, u32[]{:S(2)}) %collective-permute-start.1) | collective-permute-done | bytes 8224 | tf_op jit(solution)/shard_map/ppermute | solution.py:660
  6.2 3.1 %collective-permute-start.2 = (bf16[32,1024]{1,0:T(8,128)(2,1)S(1)}, bf16[32,1024]{1,0:T(8,128)(2,1)S(1)}, u32[]{:S(2)}, u32[]{:S(2)}) collective-permute-start(bf16[32,1024]{1,0:T(8,128)(2,1)S(1)} %maximum_maximum_fusion), channel_id=1, source_target_pairs={{0,8},{4,12},{8,0},{12,4},{1,9},{5,13},{9,1},{13,5},{2,10},{6,14},... | collective-permute-start | bytes 196616 | tf_op jit(solution)/shard_map/ppermute | solution.py:711
  9.3 2.2 %collective-permute-done.2.rest_6_ = bf16[32,1024]{1,0:T(8,128)(2,1)S(1)} collective-permute-done((bf16[32,1024]{1,0:T(8,128)(2,1)S(1)}, bf16[32,1024]{1,0:T(8,128)(2,1)S(1)}, u32[]{:S(2)}, u32[]{:S(2)}) %collective-permute-start.2) | collective-permute-done | bytes 65568 | tf_op jit(solution)/shard_map/ppermute | solution.py:711
  11.6 2.0 %collective-permute-start.3 = (bf16[48,1024]{1,0:T(8,128)(2,1)S(1)}, bf16[48,1024]{1,0:T(8,128)(2,1)S(1)}, u32[]{:S(2)}, u32[]{:S(2)}) collective-permute-start(bf16[48,1024]{1,0:T(8,128)(2,1)S(1)} %pad_maximum_fusion), channel_id=1, source_target_pairs={{0,4},{4,0},{8,12},{12,8},{1,5},{5,1},{9,13},{13,9},{2,6},{6,2},{1... | collective-permute-start | bytes 294920 | tf_op jit(solution)/shard_map/ppermute | solution.py:714
  13.6 0.0 collective-permute-done
  13.6 3.5 %middle.2 = (f32[2,6,32,512]{3,2,1,0:T(8,128)S(1)}, bf16[512,1024]{1,0:T(8,128)(2,1)S(1)}, f32[2,5,4,8,128]{4,3,2,1,0:T(8,128)S(1)}, f32[4,8,128]{2,1,0:T(8,128)S(1)}) custom-call(bf16[576,1024]{1,0:T(8,128)(2,1)S(1)} %get-tuple-element.19.own_ref, bf16[144,1024]{1,0:T(8,128)(2,1)S(1)} %bitcast.2), custom_call_target="tpu_custom_call" | custom-call | flops 2000000000 | bytes 2000000 | tf_op jit(solution)/shard_map/middle/pallas_call | solution.py:694
  17.1 0.0 collective-permute-done.3.rest_7_.rest_0_
  17.1 4.1 %middle.3 = (f32[2,6,32,512]{3,2,1,0:T(8,128)S(1)}, f32[2,8,1152]{2,1,0:T(8,128)S(1)}, f32[2,6,8,512]{3,2,1,0:T(8,128)S(1)}) custom-call(bf16[576,1024]{1,0:T(8,128)(2,1)S(1)} %get-tuple-element.19.own_ref, bf16[144,1024]{1,0:T(8,128)(2,1)S(1)} %bitcast.3, bf16[512,1024]{1,0:T(8,128)(2,1)S(1)} %get-tuple-element.21.rest_0_, ...), custom_call_target="tpu_custom_call" | custom-call | flops 2000000000 | bytes 2000000 | tf_op jit(solution)/shard_map/middle/pallas_call | solution.py:694
  21.2 3.7 %edges.1 = f32[2,6,32,1024]{3,2,1,0:T(8,128)} custom-call(bf16[576,1024]{1,0:T(8,128)(2,1)S(1)} %get-tuple-element.19.own_ref, bf16[144,1024]{1,0:T(8,128)(2,1)S(1)} %bitcast.4, f32[2,8,1152]{2,1,0:T(8,128)S(1)} %get-tuple-element.29.ghost_ref, f32[2,6,8,512]{3,2,1,0:T(8,128)S(1)} %get-tuple-element.30.grown_ref, ...), custom_call_target="tpu_custom_call" | custom-call | tf_op jit(solution)/shard_map/edges/pallas_call | solution.py:732
  (6 shorter events, 0.0 us)
Async XLA Ops:
  1.6 4.6 %collective-permute-start.1 = (bf16[1,16,256]{2,1,0:T(8,128)(2,1)S(1)}, bf16[1,16,256]{2,1,0:T(8,128)(2,1)S(1)}, u32[]{:S(2)}, u32[]{:S(2)}) collective-permute-start(bf16[1,16,256]{2,1,0:T(8,128)(2,1)S(1)} %get-tuple-element.27), channel_id=1, source_target_pairs={{0,2},{2,0},{1,3},{3,1},{4,6},{6,4},{5,7},{7,5},{8,10},{10,8},{9,1... | collective-permute-start | bytes 24584 | tf_op jit(solution)/shard_map/ppermute | solution.py:660
  4.6 9.0 %collective-permute-start = (bf16[1,144,1024]{2,1,0:T(8,128)(2,1)S(1)}, bf16[1,144,1024]{2,1,0:T(8,128)(2,1)S(1)}, u32[]{:S(2)}, u32[]{:S(2)}) collective-permute-start(bf16[1,144,1024]{2,1,0:T(8,128)(2,1)S(1)} %get-tuple-element.20), channel_id=1, source_target_pairs={{0,2},{2,0},{1,3},{3,1},{4,6},{6,4},{5,7},{7,5},{8,10},{10,8},{9,1... | collective-permute-start | bytes 884744 | tf_op jit(solution)/shard_map/ppermute | solution.py:659
  6.2 5.4 %collective-permute-start.2 = (bf16[32,1024]{1,0:T(8,128)(2,1)S(1)}, bf16[32,1024]{1,0:T(8,128)(2,1)S(1)}, u32[]{:S(2)}, u32[]{:S(2)}) collective-permute-start(bf16[32,1024]{1,0:T(8,128)(2,1)S(1)} %maximum_maximum_fusion), channel_id=1, source_target_pairs={{0,8},{4,12},{8,0},{12,4},{1,9},{5,13},{9,1},{13,5},{2,10},{6,14},... | collective-permute-start | bytes 196616 | tf_op jit(solution)/shard_map/ppermute | solution.py:711
  11.6 5.5 %collective-permute-start.3 = (bf16[48,1024]{1,0:T(8,128)(2,1)S(1)}, bf16[48,1024]{1,0:T(8,128)(2,1)S(1)}, u32[]{:S(2)}, u32[]{:S(2)}) collective-permute-start(bf16[48,1024]{1,0:T(8,128)(2,1)S(1)} %pad_maximum_fusion), channel_id=1, source_target_pairs={{0,4},{4,0},{8,12},{12,8},{1,5},{5,1},{9,13},{13,9},{2,6},{6,2},{1... | collective-permute-start | bytes 294920 | tf_op jit(solution)/shard_map/ppermute | solution.py:714

commit v5 on v4

--- a/solution.py
+++ b/solution.py
@@ -65,9 +65,46 @@
     return [jnp.concatenate(packed[i : i + 2], axis=0).astype(BF) for i in range(0, len(packed), 2)]
 
 
+def pack_rows_kernel(halves, wind_hbm, metric_hbm, kappa_hbm, bulk_ref, corner_ref, *scratch):
+    wind_ref, kappa_ref, metric_ref, sems = scratch
+    levels, rows = wind_hbm.shape[1], wind_hbm.shape[2]
+    first = lax.axis_index("across") == 0
+
+    def load(slot, at):
+        band = pl.multiple_of(jnp.where(at == 0, 0, rows - SUB), SUB)
+        return [
+            (wind_hbm.at[:, :, pl.ds(at, 16)], wind_ref.at[slot]),
+            (kappa_hbm.at[:, pl.ds(band, SUB)], kappa_ref.at[slot]),
+            (metric_hbm.at[pl.ds(band, SUB)], metric_ref.at[slot]),
+        ]
+
+    if halves == 1:
+        spots = [pl.multiple_of(jnp.where(first, rows - 16, 0), 16)]
+        low = [first]
+    else:
+        spots = [jnp.int32(rows - 16), jnp.int32(0)]
+        low = [True, False]
+    copies = fetched(sum([load(k, at) for k, at in enumerate(spots)], []), sems)
+    for copy in copies:
+        copy.wait()
+    for k in range(halves):
+        pieces = []
+        for c in range(2):
+            for lev in range(levels):
+                both = wind_ref[k, c, lev].astype(F32)
+                pieces.append(jnp.where(low[k], both[SUB:], both[:SUB]))
+        for q in range(3):
+            pieces += split_hi_lo(kappa_ref[k, q] if q < 2 else metric_ref[k])
+        for i in range(0, len(pieces), 2):
+            both = jnp.concatenate([pieces[i], pieces[i + 1]], axis=0)
+            bulk_ref[k, SUB * i : SUB * (i + 2)] = both.astype(BF)
+        for i, tile in enumerate(compact_rows([edge_tile(p) for p in pieces])):
+            corner_ref[k, :, LANES * i : LANES * (i + 1)] = tile
+
+
 def pack_kernel(
-    halves, ends_col, n_belt, wind_hbm, metric_hbm, kappa_hbm, peer_hbm, flip_hbm, turn_hbm,
-    bulk_ref, corner_ref, rim_ref, side_ref, own_ref, pick_ref, facts_ref, *scratch
+    ends_col, n_belt, wind_hbm, metric_hbm, kappa_hbm, peer_hbm, flip_hbm, turn_hbm,
+    rim_ref, side_ref, own_ref, pick_ref, facts_ref, *scratch
 ):
     wind_ref, kappa_ref, metric_ref, peer_ref, flip_ref, turn_ref, sems = scratch
     levels, rows, cols = wind_hbm.shape[1:]
@@ -88,34 +125,17 @@
             facts_ref[4 * i + k] = jnp.full((16, LANES), value, F32)
     wanted = peer_ref[edge, at_belt ^ 1]
     pick_ref[...] = jnp.full(pick_ref.shape, jnp.where(wanted == at_belt, 1.0, 0.0), BF)
-    top, bottom = slice(0, SUB), slice(rows - SUB, rows)
-
-    def bands_of(whole):
-        if halves == 1:
-            return [jnp.where(first, whole[bottom], whole[top])]
-        return [whole[bottom], whole[top]]
-
-    pieces, tiles, rim_rows = [[] for _ in range(halves)], [], []
+    tiles, rim_rows = [], []
     for f in range(2 * levels):
         own_ref[rows * f : rows * (f + 1)] = wind_ref[f // levels, f % levels]
         whole = wind_ref[f // levels, f % levels].astype(F32)
-        for k, band in enumerate(bands_of(whole)):
-            pieces[k].append(band)
         tiles += [edge_tile(whole[r : r + SUB]) for r in range(0, rows, SUB)]
         rim_rows.append(jnp.where(first, whole[0:1], whole[rows - 1 : rows]))
     for q in range(3):
         for half, part in enumerate(split_hi_lo(kappa_ref[q] if q < 2 else metric_ref[...])):
             at = rows * (2 * levels + 2 * q + half)
             own_ref[at : at + rows] = part.astype(BF)
-            for k, band in enumerate(bands_of(part)):
-                pieces[k].append(band)
             tiles += [edge_tile(part[r : r + SUB]) for r in range(0, rows, SUB)]
-    for k in range(halves):
-        for i in range(0, len(pieces[k]), 2):
-            both = jnp.concatenate([pieces[k][i], pieces[k][i + 1]], axis=0)
-            bulk_ref[k, SUB * i : SUB * (i + 2)] = both.astype(BF)
-        for i, tile in enumerate(compact_rows([edge_tile(p) for p in pieces[k]])):
-            corner_ref[k, :, LANES * i : LANES * (i + 1)] = tile
     rim = jnp.concatenate(rim_rows + [jnp.zeros((16 - len(rim_rows), cols), F32)], axis=0)
     rim_ref[...] = rim.astype(BF)
     side_ref[...] = jnp.zeros(side_ref.shape, BF)
@@ -162,6 +182,11 @@
 
 def west_of(f):
     return [pltpu.roll(f[-1], 1, 1), *f[:-1]]
+
+
+def order_kernel(after_ref, order_ref):
+    del after_ref
+    fill_order(order_ref, 0)
 
 
 def fill_order(order_ref, offset):
@@ -416,8 +441,7 @@
             out_ref, ghost_ref, grown_ref, x_ref, *work = rest[4:]
         ghost_rows(lay, facts_ref, rims_ref, ends_ref, ghost_ref)
     else:
-        out_ref, order_ref, weights_ref, touched_ref, x_ref, *work = rest
-        fill_order(order_ref, 0)
+        order_ref, out_ref, weights_ref, touched_ref, x_ref, *work = rest
     cols = slice(WINDOW * k, WINDOW * (k + 1))
     for f in range(lay.bands):
         base = lay.own_base(f)
@@ -498,7 +522,9 @@
     early = [
         pltpu.make_async_copy(m0_ref.at[:, :, calm, inner], out_hbm.at[:, :, calm, inner], sems.at[0]),
         pltpu.make_async_copy(m1_ref.at[:, :, :, inner], out_hbm.at[:, :, :, after], sems.at[1]),
+        pltpu.make_async_copy(strip_ref, out_hbm.at[:, :, edge_rows, inner], sems.at[2]),
     ]
+    strip_ref[...] = m0_ref[:, :, edge_rows, inner] + grown_ref[:, :, :, inner]
     for copy in early:
         copy.start()
     even = lax.rem(at_belt, 2) == 0
@@ -579,6 +605,7 @@
     lane_tile = lane[:SUB]
     low, high = MARGIN, LANES - MARGIN
     first_tile, last_tile = slice(0, LANES), slice(WINDOW - LANES, WINDOW)
+    late = []
     for c in range(2):
         for lev in range(levels):
             result, added = values[c][lev][:rows], grown_ref[c, lev]
@@ -593,15 +620,18 @@
             seam_ref[c, lev, edge_rows, :LANES] = seam_ref[c, lev, edge_rows, :LANES] + jnp.where(
                 lane_tile < high, added[:, last_tile], 0.0
             )
-            strip_ref[c, lev] = m0_ref[c, lev, edge_rows, inner] + added[:, inner]
-    late = [
-        pltpu.make_async_copy(strip_ref, out_hbm.at[:, :, edge_rows, inner], sems.at[2]),
-        pltpu.make_async_copy(head_ref, out_hbm.at[:, :, :, :LANES], sems.at[3]),
-        pltpu.make_async_copy(seam_ref, out_hbm.at[:, :, :, WINDOW - LANES : WINDOW + LANES], sems.at[4]),
-        pltpu.make_async_copy(tail_ref, out_hbm.at[:, :, :, cols - LANES :], sems.at[5]),
-    ]
-    for copy in late:
-        copy.start()
+        late += [
+            pltpu.make_async_copy(ref.at[c], out_hbm.at[c, :, :, place], sems.at[3 + 3 * c + k])
+            for k, (ref, place) in enumerate(
+                (
+                    (head_ref, slice(0, LANES)),
+                    (seam_ref, slice(WINDOW - LANES, WINDOW + LANES)),
+                    (tail_ref, slice(cols - LANES, cols)),
+                )
+            )
+        ]
+        for copy in late[3 * c :]:
+            copy.start()
     for copy in early + late:
         copy.wait()
 
@@ -621,11 +651,30 @@
     anywhere = pl.BlockSpec(memory_space=pl.ANY)
     lay = Rows(levels, rows, halves)
     height, span = lay.height, lay.span
-    bulk, corner, rim, side, own, pick, facts = pl.pallas_call(
-        functools.partial(pack_kernel, halves, ends_col if relay else None, n_belt),
+    pinned = [
+        pltpu.with_memory_space_constraint(x, pltpu.HBM)
+        for x in (wind, metric, kappa, edge_peer, edge_flip, edge_turn)
+    ]
+    bulk, corner = pl.pallas_call(
+        functools.partial(pack_rows_kernel, halves),
         out_shape=[
             jax.ShapeDtypeStruct((halves, SUB * bands, cols), BF),
             jax.ShapeDtypeStruct((halves, 16, corner_cols), BF),
+        ],
+        in_specs=[anywhere] * 3,
+        out_specs=[vmem] * 2,
+        scratch_shapes=[
+            pltpu.VMEM((halves, 2, levels, 16, cols), BF),
+            pltpu.VMEM((halves, 2, SUB, cols), F32),
+            pltpu.VMEM((halves, SUB, cols), F32),
+            pltpu.SemaphoreType.DMA((3 * halves,)),
+        ],
+        compiler_params=pltpu.CompilerParams(vmem_limit_bytes=PACK_LIMIT),
+        name="pack_rows",
+    )(*pinned[:3])
+    rim, side, own, pick, facts = pl.pallas_call(
+        functools.partial(pack_kernel, ends_col if relay else None, n_belt),
+        out_shape=[
             jax.ShapeDtypeStruct((16, cols), BF),
             jax.ShapeDtypeStruct((16, cols), BF),
             jax.ShapeDtypeStruct((rows * bands, cols), BF),
@@ -633,7 +682,7 @@
             jax.ShapeDtypeStruct((12, 16, LANES), F32),
         ],
         in_specs=[anywhere] * 6,
-        out_specs=[vmem] * 7,
+        out_specs=[vmem] * 5,
         scratch_shapes=[
             pltpu.VMEM(wind.shape, BF),
             pltpu.VMEM(kappa.shape, F32),
@@ -645,12 +694,7 @@
         ],
         compiler_params=pltpu.CompilerParams(vmem_limit_bytes=PACK_LIMIT),
         name="pack",
-    )(
-        *(
-            pltpu.with_memory_space_constraint(x, pltpu.HBM)
-            for x in (wind, metric, kappa, edge_peer, edge_flip, edge_turn)
-        )
-    )
+    )(*pinned)
 
     pairs_a = [(i, i ^ 1) for i in range(n_belt)]
     pairs_b = [(i, (i + 1) % n_belt if i % 2 else (i - 1) % n_belt) for i in range(n_belt)]
@@ -680,7 +724,6 @@
         spaces = [vmem] * len(operands)
         if k == 0:
             shapes += [
-                jax.ShapeDtypeStruct((WINDOW, 2 * WINDOW), BF),
                 jax.ShapeDtypeStruct((2, 5, PARTS, SUB, LANES), F32),
                 jax.ShapeDtypeStruct((PARTS, SUB, LANES), F32),
             ]
@@ -704,7 +747,19 @@
             name="middle",
         )(*operands)
 
-    window_0, *shared = middle(0, [])
+    def order_after(message):
+        return pl.pallas_call(
+            order_kernel,
+            out_shape=jax.ShapeDtypeStruct((WINDOW, 2 * WINDOW), BF),
+            in_specs=[anywhere],
+            out_specs=vmem,
+            compiler_params=pltpu.CompilerParams(vmem_limit_bytes=PACK_LIMIT),
+            cost_estimate=pl.CostEstimate(flops=100_000_000, bytes_accessed=1_000_000, transcendentals=0),
+            name="order",
+        )(message)
+
+    order = order_after(corner_in)
+    window_0, *shared = middle(0, [order])
     if relay:
         spot = slice(side_cols, ends_col)
         side = jnp.concatenate([side[:, :side_cols], corner_in[0], side[:, ends_col:]], axis=1)
@@ -727,7 +782,7 @@
         ends = jnp.concatenate([ends[..., : LANES // 2], ends[..., cols - LANES // 2 :]], axis=-1)
 
         rim_parts, messages = [rims, ends], [side_a, side_b, corner_a, corner_b]
-    window_1, ghost, grown = middle(1, [*shared, facts, *rim_parts])
+    window_1, ghost, grown = middle(1, [order, *shared, facts, *rim_parts])
     operands = [own, bulk_in, ghost, grown, window_0, window_1, *messages]
     return pl.pallas_call(
         functools.partial(edge_kernel, lay, (side_cols, ends_col) if relay else None),
@@ -739,7 +794,7 @@
             pltpu.VMEM((2, levels, rows, 2 * LANES), F32),
             pltpu.VMEM((2, levels, rows, LANES), F32),
             pltpu.VMEM((2, levels, SUB, WINDOW - 2 * LANES), F32),
-            pltpu.SemaphoreType.DMA((6,)),
+            pltpu.SemaphoreType.DMA((9,)),
         ],
         compiler_params=pltpu.CompilerParams(vmem_limit_bytes=EDGE_LIMIT),
         name="edges",

time: 25.1 us -> 24.5 us (0.976)
  waiting for transfers between devices: 3.79 us -> 2.4 us
  Pallas kernels: 12.9 us -> 13.9 us
  starting transfers between devices: 8.19 us -> 7.93 us
    ppermute x1, waiting for transfers between devices: 1.54 us -> 0.02 us  [per_device(): corner_in = lax.ppermute(corner, 'across', swap)]
    pallas_call x1 -> x3, Pallas kernels: 1.55 us -> 2.81 us  [the longest x1 1.5 us: per_device(): pl.pallas_call(functools.partial(pack_kernel, ends_col if relay else None...]
    ppermute x1, starting transfers between devices: 1.97 us -> 1.68 us  [per_device(): lax.ppermute(jnp.concatenate([chosen, side, side_c]), 'belt', pairs_a)]
  transfers between devices with their start and end apart: 4 -> 4, of which waited for: 2 -> 1; matrix products, arithmetic and copies ran while one was open for 0% -> 0% of each run, Pallas kernels for 14% -> 21%
where the time goes in v5:
time: 24.5 us; the launch traced here: 24.4 us
  Pallas kernels  13.9 us (57%)
  starting transfers between devices  7.93 us (32%)
  waiting for transfers between devices  2.4 us (10%)
    pallas_call x2, Pallas kernels, middle(): pl.pallas_call(functools.partial(middle_kernel, lay, k, (side_cols, ends_...  7.52 us
    pallas_call x1, Pallas kernels, per_device(): pl.pallas_call(functools.partial(edge_kernel, lay, (side_cols, ends_col)...  3.59 us
    ppermute x1, starting transfers between devices, per_device(): lax.ppermute(jnp.concatenate([rim, side]), 'belt', [(i, i ^ 2) for i in r...  3.17 us
    ppermute x1, starting transfers between devices, per_device(): corner_in = lax.ppermute(corner, 'across', swap)  3 us
    ppermute x1, waiting for transfers between devices, per_device(): lax.ppermute(jnp.concatenate([rim, side]), 'belt', [(i, i ^ 2) for i in r...  2.38 us
    ppermute x1, starting transfers between devices, per_device(): lax.ppermute(jnp.concatenate([chosen, side, side_c]), 'belt', pairs_a)  1.68 us
    pallas_call x1, Pallas kernels, per_device(): pl.pallas_call(functools.partial(pack_kernel, ends_col if relay else None...  1.5 us
    pallas_call x1, Pallas kernels, per_device(): pl.pallas_call(functools.partial(pack_rows_kernel, halves), out_shape=[ja...  1.16 us
  transfers between devices with their start and end apart: 4, of which 1 were waited for; matrix products, arithmetic and copies ran while one was open for 0% of the time, Pallas kernels for 21%

profile of v5, /device:TPU:0, one launch (start us, length us, event | category | flops | bytes accessed | tf_op | source)
XLA Modules:
  0.0 24.4 jit_solution(1797203582032017404)
XLA Ops:
  0.0 1.2 %pack_rows.1 = (bf16[1,144,1024]{2,1,0:T(8,128)(2,1)S(1)}, bf16[1,16,256]{2,1,0:T(8,128)(2,1)S(1)}) custom-call(bf16[2,6,32,1024]{3,2,1,0:T(8,128)(2,1)} %wind_hbm.3, f32[32,1024]{1,0:T(8,128)} %metric_hbm.3, f32[2,32,1024]{2,1,0:T(8,128)} %kappa_hbm.3), custom_call_target="tpu_custom_call" | custom-call | tf_op jit(solution)/shard_map/pack_rows/pallas_call | solution.py:658
  1.2 3.0 %collective-permute-start.1 = (bf16[1,16,256]{2,1,0:T(8,128)(2,1)S(1)}, bf16[1,16,256]{2,1,0:T(8,128)(2,1)S(1)}, u32[]{:S(2)}, u32[]{:S(2)}) collective-permute-start(bf16[1,16,256]{2,1,0:T(8,128)(2,1)S(1)} %get-tuple-element.20), channel_id=1, source_target_pairs={{0,2},{2,0},{1,3},{3,1},{4,6},{6,4},{5,7},{7,5},{8,10},{10,8},{9,1... | collective-permute-start | bytes 24584 | tf_op jit(solution)/shard_map/ppermute | solution.py:704
  4.2 0.1 collective-permute-start
  4.3 1.5 %pack.1 = (bf16[16,1024]{1,0:T(8,128)(2,1)S(1)}, bf16[16,1024]{1,0:T(8,128)(2,1)S(1)}, bf16[576,1024]{1,0:T(8,128)(2,1)S(1)}, bf16[16,1024]{1,0:T(8,128)(2,1)S(1)}, f32[12,16,128]{2,1,0:T(8,128)S(1)}) custom-call(bf16[2,6,32,1024]{3,2,1,0:T(8,128)(2,1)} %wind_hbm.3, f32[32,1024]{1,0:T(8,128)} %metric_hbm.3, f32[2,32,1024]{2,1,0:T(8,128)} %kappa_hbm.3, ...), custom_call_target="tpu_custom_call" | custom-call | tf_op jit(solution)/shard_map/pack/pallas_call | solution.py:675
  5.8 0.0 collective-permute-done.1.after_ref
  5.8 3.2 %collective-permute-start.2 = (bf16[32,1024]{1,0:T(8,128)(2,1)S(1)}, bf16[32,1024]{1,0:T(8,128)(2,1)S(1)}, u32[]{:S(2)}, u32[]{:S(2)}) collective-permute-start(bf16[32,1024]{1,0:T(8,128)(2,1)S(1)} %maximum_maximum_fusion), channel_id=1, source_target_pairs={{0,8},{4,12},{8,0},{12,4},{1,9},{5,13},{9,1},{13,5},{2,10},{6,14},... | collective-permute-start | bytes 196616 | tf_op jit(solution)/shard_map/ppermute | solution.py:766
  9.0 0.1 order.1.rest_0_
  9.1 2.4 %collective-permute-done.2.rest_6_ = bf16[32,1024]{1,0:T(8,128)(2,1)S(1)} collective-permute-done((bf16[32,1024]{1,0:T(8,128)(2,1)S(1)}, bf16[32,1024]{1,0:T(8,128)(2,1)S(1)}, u32[]{:S(2)}, u32[]{:S(2)}) %collective-permute-start.2) | collective-permute-done | bytes 65568 | tf_op jit(solution)/shard_map/ppermute | solution.py:766
  11.6 1.7 %collective-permute-start.3 = (bf16[48,1024]{1,0:T(8,128)(2,1)S(1)}, bf16[48,1024]{1,0:T(8,128)(2,1)S(1)}, u32[]{:S(2)}, u32[]{:S(2)}) collective-permute-start(bf16[48,1024]{1,0:T(8,128)(2,1)S(1)} %pad_maximum_fusion), channel_id=1, source_target_pairs={{0,4},{4,0},{8,12},{12,8},{1,5},{5,1},{9,13},{13,9},{2,6},{6,2},{1... | collective-permute-start | bytes 294920 | tf_op jit(solution)/shard_map/ppermute | solution.py:769
  13.2 0.0 collective-permute-done
  13.2 3.4 %middle.2 = (f32[2,6,32,512]{3,2,1,0:T(8,128)S(1)}, f32[2,5,4,8,128]{4,3,2,1,0:T(8,128)S(1)}, f32[4,8,128]{2,1,0:T(8,128)S(1)}) custom-call(bf16[576,1024]{1,0:T(8,128)(2,1)S(1)} %get-tuple-element.18.own_ref, bf16[144,1024]{1,0:T(8,128)(2,1)S(1)} %bitcast.2, bf16[512,1024]{1,0:T(8,128)(2,1)S(1)} %order.1.rest_0_), custom_call_target="tpu_custom_call" | custom-call | flops 2000000000 | bytes 2000000 | tf_op jit(solution)/shard_map/middle/pallas_call | solution.py:737
  16.7 0.0 collective-permute-done.3.rest_7_.rest_0_
  16.7 4.1 %middle.3 = (f32[2,6,32,512]{3,2,1,0:T(8,128)S(1)}, f32[2,8,1152]{2,1,0:T(8,128)S(1)}, f32[2,6,8,512]{3,2,1,0:T(8,128)S(1)}) custom-call(bf16[576,1024]{1,0:T(8,128)(2,1)S(1)} %get-tuple-element.18.own_ref, bf16[144,1024]{1,0:T(8,128)(2,1)S(1)} %bitcast.3, bf16[512,1024]{1,0:T(8,128)(2,1)S(1)} %order.1.rest_0_, ...), custom_call_target="tpu_custom_call" | custom-call | flops 2000000000 | bytes 2000000 | tf_op jit(solution)/shard_map/middle/pallas_call | solution.py:737
  20.8 3.6 %edges.1 = f32[2,6,32,1024]{3,2,1,0:T(8,128)} custom-call(bf16[576,1024]{1,0:T(8,128)(2,1)S(1)} %get-tuple-element.18.own_ref, bf16[144,1024]{1,0:T(8,128)(2,1)S(1)} %bitcast.4, f32[2,8,1152]{2,1,0:T(8,128)S(1)} %get-tuple-element.27.ghost_ref, f32[2,6,8,512]{3,2,1,0:T(8,128)S(1)} %get-tuple-element.28.grown_ref, ...), custom_call_target="tpu_custom_call" | custom-call | tf_op jit(solution)/shard_map/edges/pallas_call | solution.py:787
  (6 shorter events, 0.0 us)
Async XLA Ops:
  1.2 4.6 %collective-permute-start.1 = (bf16[1,16,256]{2,1,0:T(8,128)(2,1)S(1)}, bf16[1,16,256]{2,1,0:T(8,128)(2,1)S(1)}, u32[]{:S(2)}, u32[]{:S(2)}) collective-permute-start(bf16[1,16,256]{2,1,0:T(8,128)(2,1)S(1)} %get-tuple-element.20), channel_id=1, source_target_pairs={{0,2},{2,0},{1,3},{3,1},{4,6},{6,4},{5,7},{7,5},{8,10},{10,8},{9,1... | collective-permute-start | bytes 24584 | tf_op jit(solution)/shard_map/ppermute | solution.py:704
  4.2 9.1 %collective-permute-start = (bf16[1,144,1024]{2,1,0:T(8,128)(2,1)S(1)}, bf16[1,144,1024]{2,1,0:T(8,128)(2,1)S(1)}, u32[]{:S(2)}, u32[]{:S(2)}) collective-permute-start(bf16[1,144,1024]{2,1,0:T(8,128)(2,1)S(1)} %get-tuple-element.19), channel_id=1, source_target_pairs={{0,2},{2,0},{1,3},{3,1},{4,6},{6,4},{5,7},{7,5},{8,10},{10,8},{9,1... | collective-permute-start | bytes 884744 | tf_op jit(solution)/shard_map/ppermute | solution.py:703
  5.8 5.7 %collective-permute-start.2 = (bf16[32,1024]{1,0:T(8,128)(2,1)S(1)}, bf16[32,1024]{1,0:T(8,128)(2,1)S(1)}, u32[]{:S(2)}, u32[]{:S(2)}) collective-permute-start(bf16[32,1024]{1,0:T(8,128)(2,1)S(1)} %maximum_maximum_fusion), channel_id=1, source_target_pairs={{0,8},{4,12},{8,0},{12,4},{1,9},{5,13},{9,1},{13,5},{2,10},{6,14},... | collective-permute-start | bytes 196616 | tf_op jit(solution)/shard_map/ppermute | solution.py:766
  11.6 5.1 %collective-permute-start.3 = (bf16[48,1024]{1,0:T(8,128)(2,1)S(1)}, bf16[48,1024]{1,0:T(8,128)(2,1)S(1)}, u32[]{:S(2)}, u32[]{:S(2)}) collective-permute-start(bf16[48,1024]{1,0:T(8,128)(2,1)S(1)} %pad_maximum_fusion), channel_id=1, source_target_pairs={{0,4},{4,0},{8,12},{12,8},{1,5},{5,1},{9,13},{13,9},{2,6},{6,2},{1... | collective-permute-start | bytes 294920 | tf_op jit(solution)/shard_map/ppermute | solution.py:769
